TPU v7x, 128 devices: a whole 4x4x4 slice. The times are simulated.
128 devices in a mesh: node: 8 (over y_lo, x), feat: 16 (over z, y_hi, core).
Axes of the slice: x: 4, y: 4 (y_hi: 2, y_lo: 2; y = y_hi * 2 + y_lo), z: 4, core: 2. Of those that a mesh axis runs over, the one named last changes fastest.
Arguments:
- features: bfloat16 [128, 65536], P('feat', 'node'), may hold values from -6 to 6
- weight: bfloat16 [128, 256], P(None, 'feat'), may hold values from -0.5 to 0.5
- bias: float32 [256], P('feat'), may hold values from -3 to 3
- tile_values: bfloat16 [8, 8, 48, 128, 128], P('node'), may hold values from -0.25 to 0.25
- tile_rows: int32 [8, 8, 48], P('node'), may hold values from 0 to 63
- tile_cols: int32 [8, 8, 48], P('node'), may hold values from 0 to 63
- tile_count: int32 [8, 8], P('node'), may hold values from 0 to 48, as said below
- cotangent: bfloat16 [256, 65536], P('feat', 'node'), may hold values from -6 to 6
Outputs:
- out_field: bfloat16 [256, 65536], P('feat', 'node')
- grad_features: bfloat16 [128, 65536], P('feat', 'node')
- grad_weight: float32 [128, 256], P(None, 'feat')
- grad_bias: float32 [256], P('feat')
Inputs may be any that keep to these rules, and one draw needn't show every extreme that they name: tile_count[i, i] = 48 for every shard i; slots at or beyond tile_count are unused.
All inputs are finite; a program needn't handle non-finite values.
Results may differ from a plain program's by a relative error of at most 0.0075.
Values may be sent and summed in bfloat16 or wider, within the bound.
A program may use at most 64 MiB of HBM per device.

v0:
```python
import math

import jax
import jax.numpy as jnp
from jax import lax
from jax.sharding import PartitionSpec as P


def passed_along(x, axis, by):
    count = lax.axis_size(axis)
    return lax.ppermute(x, axis, [(i, (i + by) % count) for i in range(count)])


def forward_part(source, tile_block, row_list, col_list, amount):
    tile_size = tile_block.shape[-1]
    row_tiles = source.shape[1] // tile_size
    adjacency_blocks = source.reshape(source.shape[0], row_tiles, tile_size)
    picked = jnp.take(adjacency_blocks, col_list, axis=1)
    block_products = jnp.einsum(
        "ftc,trc->ftr", picked, tile_block, preferred_element_type=jnp.float32
    )
    usable = jnp.arange(col_list.shape[0]) < amount
    spread_lookup = (
        (row_list[None, :] == jnp.arange(row_tiles)[:, None]) & usable[None, :]
    ).astype(jnp.float32)
    summed_rows = jnp.einsum(
        "nd,idq->inq", spread_lookup, block_products, precision=lax.Precision.HIGHEST
    )
    return summed_rows.reshape(source.shape[0], row_tiles * tile_size)


def backward_part(source, tile_block, row_list, col_list, amount):
    tile_size = tile_block.shape[-1]
    row_tiles = source.shape[1] // tile_size
    adjacency_blocks = source.reshape(source.shape[0], row_tiles, tile_size)
    picked = jnp.take(adjacency_blocks, row_list, axis=1)
    block_products = jnp.einsum(
        "ftr,trc->ftc", picked, tile_block, preferred_element_type=jnp.float32
    )
    usable = jnp.arange(row_list.shape[0]) < amount
    spread_lookup = (
        (col_list[None, :] == jnp.arange(row_tiles)[:, None]) & usable[None, :]
    ).astype(jnp.float32)
    summed_rows = jnp.einsum(
        "st,ftc->fsc", spread_lookup, block_products, precision=lax.Precision.HIGHEST
    )
    return summed_rows.reshape(source.shape[0], row_tiles * tile_size)


def select(table, shard_id):
    return lax.dynamic_index_in_dim(table, shard_id, 0, keepdims=False)


def local(features, weight, bias, tile_values, tile_rows, tile_cols, tile_count, cotangent):
    groups = tile_values[0]
    row_lists = tile_rows[0]
    col_lists = tile_cols[0]
    counts = tile_count[0]
    nshard = lax.axis_size("node")
    own_shard = lax.axis_index("node")

    def collected_piece(source, shard_id):
        return forward_part(
            source,
            select(groups, shard_id),
            select(row_lists, shard_id),
            select(col_lists, shard_id),
            select(counts, shard_id),
        )

    full_in = lax.all_gather(features, "feat", axis=0, tiled=True)
    projected = jnp.einsum("ih,in->hn", weight, full_in, preferred_element_type=jnp.float32).astype(
        jnp.bfloat16
    )
    running_totals = projected.astype(jnp.float32) + collected_piece(projected, own_shard)

    def one_step(cycle_step, carry):
        summed_rows, held = carry
        held = passed_along(held, "node", 1)
        summed_rows = summed_rows + collected_piece(held, (own_shard - cycle_step) % nshard)
        return (summed_rows, held)

    running_totals, held = lax.fori_loop(1, nshard, one_step, (running_totals, projected))
    preact = running_totals + bias[:, None]
    out_field = jax.nn.silu(preact).astype(jnp.bfloat16)
    sigmoid_pre = jax.nn.sigmoid(preact)
    grad_pre = (
        cotangent.astype(jnp.float32) * sigmoid_pre * (1.0 + preact * (1.0 - sigmoid_pre))
    ).astype(jnp.bfloat16)

    def spread_part(shard_id):
        return backward_part(
            grad_pre,
            select(groups, shard_id),
            select(row_lists, shard_id),
            select(col_lists, shard_id),
            select(counts, shard_id),
        )

    carried = spread_part((own_shard + 1) % nshard)

    def back_step(cycle_step, partial_sum):
        partial_sum = passed_along(partial_sum, "node", -1)
        return partial_sum + spread_part((own_shard + cycle_step + 1) % nshard)

    carried = lax.fori_loop(1, nshard, back_step, carried)
    grad_proj = (grad_pre.astype(jnp.float32) + carried).astype(jnp.bfloat16)
    grad_features = lax.psum_scatter(
        jnp.einsum("ih,hn->in", weight, grad_proj, preferred_element_type=jnp.float32),
        "feat",
        scatter_dimension=0,
        tiled=True,
    )
    weight_term = jnp.einsum("in,hn->ih", full_in, grad_proj, preferred_element_type=jnp.float32)
    bias_term = jnp.sum(grad_pre.astype(jnp.float32), axis=1)
    weight_term, bias_term = lax.psum((weight_term, bias_term), "node")
    normalizer = 1.0 / math.sqrt(features.shape[1] * nshard)
    return (
        out_field,
        grad_features.astype(jnp.bfloat16),
        weight_term * normalizer,
        bias_term * normalizer,
    )


def solution(mesh):
    return jax.shard_map(
        local,
        mesh=mesh,
        in_specs=(
            P("feat", "node"),
            P(None, "feat"),
            P("feat"),
            P("node", None, None, None, None),
            P("node", None, None),
            P("node", None, None),
            P("node", None),
            P("feat", "node"),
        ),
        out_specs=(P("feat", "node"), P("feat", "node"), P(None, "feat"), P("feat")),
        check_vma=False,
    )
```

profile of v0, /device:TPU:0, one launch (start us, length us, event | category | flops | bytes accessed | tf_op | source)
XLA Modules:
  0.0 364.9 jit_solution(1262652066402219663)
XLA Ops:
  12.7 47.9 %all-gather.2.cloned.1.call-done = bf16[128,8192]{1,0:T(8,128)(2,1)} async-done(((bf16[8,8192]{1,0:T(8,128)(2,1)}), bf16[128,8192]{1,0:T(8,128)(2,1)}) %all-gather.2.cloned.1.call-update) | async-done | bytes 2097168 | tf_op jit(solution)/shard_map/all_gather | solution.py:71
  63.3 2.4 fusion.48
  66.5 91.8 %while.32 = (s32[]{:T(128)}, f32[16,8192]{1,0:T(8,128)S(1)}, bf16[16,8192]{1,0:T(8,128)(2,1)S(1)}, s32[]{:T(128)}, bf16[8,48,128,128]{3,2,1,0:T(8,128)(2,1)}, /*...) while((s32[]{:T(128)}, f32[16,8192]{1,0:T(8,128)S(1)}, ...), condition=%wide.region_1.3_spmd, body=%wide.region_0.2_spmd.sunk | while | flops 100900192 | bytes 7149396 | solution.py:83
  70.7 6.5 %collective-permute-done = bf16[16,8192]{1,0:T(8,128)(2,1)S(1)} collective-permute-done((bf16[16,8192]{1,0:T(8,128)(2,1)S(1)}, bf16[16,8192]{1,0:T(8,128)(2,1)S(1)}, u32[]{:S(2)}, u32[]{:S(2)}) %collective-permute-start) | collective-permute-done | bytes 262176 | tf_op jit(solution)/shard_map/while/body/eval_jaxpr/ppermute | solution.py:11
  77.9 2.4 fusion.116
  84.0 7.1 %collective-permute-done = bf16[16,8192]{1,0:T(8,128)(2,1)S(1)} collective-permute-done((bf16[16,8192]{1,0:T(8,128)(2,1)S(1)}, bf16[16,8192]{1,0:T(8,128)(2,1)S(1)}, u32[]{:S(2)}, u32[]{:S(2)}) %collective-permute-start) | collective-permute-done | bytes 262176 | tf_op jit(solution)/shard_map/while/body/eval_jaxpr/ppermute | solution.py:11
  91.7 2.4 fusion.116
  97.8 6.2 %collective-permute-done = bf16[16,8192]{1,0:T(8,128)(2,1)S(1)} collective-permute-done((bf16[16,8192]{1,0:T(8,128)(2,1)S(1)}, bf16[16,8192]{1,0:T(8,128)(2,1)S(1)}, u32[]{:S(2)}, u32[]{:S(2)}) %collective-permute-start) | collective-permute-done | bytes 262176 | tf_op jit(solution)/shard_map/while/body/eval_jaxpr/ppermute | solution.py:11
  104.6 2.4 fusion.116
  110.8 5.8 %collective-permute-done = bf16[16,8192]{1,0:T(8,128)(2,1)S(1)} collective-permute-done((bf16[16,8192]{1,0:T(8,128)(2,1)S(1)}, bf16[16,8192]{1,0:T(8,128)(2,1)S(1)}, u32[]{:S(2)}, u32[]{:S(2)}) %collective-permute-start) | collective-permute-done | bytes 262176 | tf_op jit(solution)/shard_map/while/body/eval_jaxpr/ppermute | solution.py:11
  117.2 2.4 fusion.116
  123.4 5.8 %collective-permute-done = bf16[16,8192]{1,0:T(8,128)(2,1)S(1)} collective-permute-done((bf16[16,8192]{1,0:T(8,128)(2,1)S(1)}, bf16[16,8192]{1,0:T(8,128)(2,1)S(1)}, u32[]{:S(2)}, u32[]{:S(2)}) %collective-permute-start) | collective-permute-done | bytes 262176 | tf_op jit(solution)/shard_map/while/body/eval_jaxpr/ppermute | solution.py:11
  129.8 2.4 fusion.116
  135.9 5.8 %collective-permute-done = bf16[16,8192]{1,0:T(8,128)(2,1)S(1)} collective-permute-done((bf16[16,8192]{1,0:T(8,128)(2,1)S(1)}, bf16[16,8192]{1,0:T(8,128)(2,1)S(1)}, u32[]{:S(2)}, u32[]{:S(2)}) %collective-permute-start) | collective-permute-done | bytes 262176 | tf_op jit(solution)/shard_map/while/body/eval_jaxpr/ppermute | solution.py:11
  142.4 2.4 fusion.116
  148.5 5.8 %collective-permute-done = bf16[16,8192]{1,0:T(8,128)(2,1)S(1)} collective-permute-done((bf16[16,8192]{1,0:T(8,128)(2,1)S(1)}, bf16[16,8192]{1,0:T(8,128)(2,1)S(1)}, u32[]{:S(2)}, u32[]{:S(2)}) %collective-permute-start) | collective-permute-done | bytes 262176 | tf_op jit(solution)/shard_map/while/body/eval_jaxpr/ppermute | solution.py:11
  155.0 2.4 fusion.116
  163.0 102.2 %while.33 = (s32[]{:T(128)}, f32[16,8192]{1,0:T(8,128)S(1)}, s32[]{:T(128)}, bf16[8,48,128,128]{3,2,1,0:T(8,128)(2,1)}, bf16[16,8192]{1,0:T(8,128)(2,1)S(1)}, /*...) while((s32[]{:T(128)}, f32[16,8192]{1,0:T(8,128)S(1)}, ...), condition=%wide.region_3.5_spmd, body=%wide.region_2.4_spmd.sunk | while | flops 100900192 | bytes 7673696 | solution.py:106
  169.0 8.4 %collective-permute-done.1 = f32[16,8192]{1,0:T(8,128)S(1)} collective-permute-done((f32[16,8192]{1,0:T(8,128)S(1)}, f32[16,8192]{1,0:T(8,128)S(1)}, u32[]{:S(2)}, u32[]{:S(2)}) %collective-permute-start.1) | collective-permute-done | bytes 524320 | tf_op jit(solution)/shard_map/while/body/eval_jaxpr/ppermute | solution.py:11
  183.8 8.3 %collective-permute-done.1 = f32[16,8192]{1,0:T(8,128)S(1)} collective-permute-done((f32[16,8192]{1,0:T(8,128)S(1)}, f32[16,8192]{1,0:T(8,128)S(1)}, u32[]{:S(2)}, u32[]{:S(2)}) %collective-permute-start.1) | collective-permute-done | bytes 524320 | tf_op jit(solution)/shard_map/while/body/eval_jaxpr/ppermute | solution.py:11
  199.7 6.2 %collective-permute-done.1 = f32[16,8192]{1,0:T(8,128)S(1)} collective-permute-done((f32[16,8192]{1,0:T(8,128)S(1)}, f32[16,8192]{1,0:T(8,128)S(1)}, u32[]{:S(2)}, u32[]{:S(2)}) %collective-permute-start.1) | collective-permute-done | bytes 524320 | tf_op jit(solution)/shard_map/while/body/eval_jaxpr/ppermute | solution.py:11
  206.3 4.6 %collective-permute-start.1 = (f32[16,8192]{1,0:T(8,128)S(1)}, f32[16,8192]{1,0:T(8,128)S(1)}, u32[]{:S(2)}, u32[]{:S(2)}) collective-permute-start(f32[16,8192]{1,0:T(8,128)S(1)} %get-tuple-element.625), channel_id=1, source_target_pairs={{0,112},{16,0},{32,16},{48,32},{64,48},{80,64},{96,80},{112,96},{1... | collective-permute-start | bytes 1572872 | tf_op jit(solution)/shard_map/while/body/eval_jaxpr/ppermute | solution.py:11
  216.8 5.6 %collective-permute-done.1 = f32[16,8192]{1,0:T(8,128)S(1)} collective-permute-done((f32[16,8192]{1,0:T(8,128)S(1)}, f32[16,8192]{1,0:T(8,128)S(1)}, u32[]{:S(2)}, u32[]{:S(2)}) %collective-permute-start.1) | collective-permute-done | bytes 524320 | tf_op jit(solution)/shard_map/while/body/eval_jaxpr/ppermute | solution.py:11
  222.9 4.7 %collective-permute-start.1 = (f32[16,8192]{1,0:T(8,128)S(1)}, f32[16,8192]{1,0:T(8,128)S(1)}, u32[]{:S(2)}, u32[]{:S(2)}) collective-permute-start(f32[16,8192]{1,0:T(8,128)S(1)} %get-tuple-element.625), channel_id=1, source_target_pairs={{0,112},{16,0},{32,16},{48,32},{64,48},{80,64},{96,80},{112,96},{1... | collective-permute-start | bytes 1572872 | tf_op jit(solution)/shard_map/while/body/eval_jaxpr/ppermute | solution.py:11
  233.4 4.8 %collective-permute-done.1 = f32[16,8192]{1,0:T(8,128)S(1)} collective-permute-done((f32[16,8192]{1,0:T(8,128)S(1)}, f32[16,8192]{1,0:T(8,128)S(1)}, u32[]{:S(2)}, u32[]{:S(2)}) %collective-permute-start.1) | collective-permute-done | bytes 524320 | tf_op jit(solution)/shard_map/while/body/eval_jaxpr/ppermute | solution.py:11
  238.6 4.7 %collective-permute-start.1 = (f32[16,8192]{1,0:T(8,128)S(1)}, f32[16,8192]{1,0:T(8,128)S(1)}, u32[]{:S(2)}, u32[]{:S(2)}) collective-permute-start(f32[16,8192]{1,0:T(8,128)S(1)} %get-tuple-element.625), channel_id=1, source_target_pairs={{0,112},{16,0},{32,16},{48,32},{64,48},{80,64},{96,80},{112,96},{1... | collective-permute-start | bytes 1572872 | tf_op jit(solution)/shard_map/while/body/eval_jaxpr/ppermute | solution.py:11
  249.1 3.9 %collective-permute-done.1 = f32[16,8192]{1,0:T(8,128)S(1)} collective-permute-done((f32[16,8192]{1,0:T(8,128)S(1)}, f32[16,8192]{1,0:T(8,128)S(1)}, u32[]{:S(2)}, u32[]{:S(2)}) %collective-permute-start.1) | collective-permute-done | bytes 524320 | tf_op jit(solution)/shard_map/while/body/eval_jaxpr/ppermute | solution.py:11
  253.4 4.7 %collective-permute-start.1 = (f32[16,8192]{1,0:T(8,128)S(1)}, f32[16,8192]{1,0:T(8,128)S(1)}, u32[]{:S(2)}, u32[]{:S(2)}) collective-permute-start(f32[16,8192]{1,0:T(8,128)S(1)} %get-tuple-element.625), channel_id=1, source_target_pairs={{0,112},{16,0},{32,16},{48,32},{64,48},{80,64},{96,80},{112,96},{1... | collective-permute-start | bytes 1572872 | tf_op jit(solution)/shard_map/while/body/eval_jaxpr/ppermute | solution.py:11
  265.2 2.7 convolution_bitcast_fusion
  267.9 5.6 %copy.33 = f32[128,8192]{1,0:T(8,128)} copy(f32[128,8192]{0,1:T(8,128)} %convolution_bitcast_fusion) | data formatting | bytes 8388608
  275.8 21.0 %all-reduce = (f32[128,16]{0,1:T(8,128)S(1)}, f32[16]{0:T(128)S(1)}) all-reduce(f32[128,16]{0,1:T(8,128)S(1)} %convolution_bitcast_fusion.1, f32[16]{0:T(128)S(1)} %get-tuple-element.459), channel_id=1, replica_groups=mesh['node'=8,'feat'=16] {'node'}, use_global_device_ids=true, to_apply=%region_5.7 | all-reduce | flops 2064 | bytes 16512 | tf_op jit(solution)/shard_map/psum | solution.py:116
  297.9 56.9 %reduce-scatter.4.cloned.1.call-done = f32[8,8192]{1,0:T(8,128)} async-done(((f32[128,8192]{1,0:T(8,128)}), f32[8,8192]{1,0:T(8,128)}) %reduce-scatter.4.cloned.1.call-update) | async-done | bytes 262160
  (189 shorter events, 98.1 us)
Async XLA Ops:
  7.2 53.5 %copy-start = (bf16[128,16]{0,1:T(8,128)(2,1)S(1)}, bf16[128,16]{0,1:T(8,128)(2,1)}, u32[]{:S(2)}) copy-start(bf16[128,16]{0,1:T(8,128)(2,1)} %param.15) | copy-start | bytes 12292
  7.2 53.4 %all-gather.2.cloned.1.call-start = ((), (), s32[]{:S(2)}) async-start(), calls=%async_computation.1 | async-start | bytes 2228224 | tf_op jit(solution)/shard_map/all_gather | solution.py:71
  7.9 346.9 %reduce-scatter.4.cloned.1.call-start = ((), (), s32[]{:S(2)}) async-start(), calls=%async_computation.2 | async-start | bytes 4456448
  63.3 3.2 copy-start.3
  66.5 91.8 %copy-start.2 = (bf16[16,8192]{1,0:T(8,128)(2,1)S(1)}, bf16[16,8192]{1,0:T(8,128)(2,1)}, u32[]{:S(2)}) copy-start(bf16[16,8192]{1,0:T(8,128)(2,1)} %param.21) | copy-start | bytes 786436
  66.5 91.8 %copy-start.4 = (f32[16]{0:T(128)S(1)}, f32[16]{0:T(128)}, u32[]{:S(2)}) copy-start(f32[16]{0:T(128)} %param.16) | copy-start | bytes 196
  66.6 10.6 %collective-permute-start = (bf16[16,8192]{1,0:T(8,128)(2,1)S(1)}, bf16[16,8192]{1,0:T(8,128)(2,1)S(1)}, u32[]{:S(2)}, u32[]{:S(2)}) collective-permute-start(bf16[16,8192]{1,0:T(8,128)(2,1)S(1)} %get-tuple-element.590), channel_id=1, source_target_pairs={{0,16},{16,32},{32,48},{48,64},{64,80},{80,96},{96,112},{112,0},{1... | collective-permute-start | bytes 786440 | tf_op jit(solution)/shard_map/while/body/eval_jaxpr/ppermute | solution.py:11
  81.2 9.8 %collective-permute-start = (bf16[16,8192]{1,0:T(8,128)(2,1)S(1)}, bf16[16,8192]{1,0:T(8,128)(2,1)S(1)}, u32[]{:S(2)}, u32[]{:S(2)}) collective-permute-start(bf16[16,8192]{1,0:T(8,128)(2,1)S(1)} %get-tuple-element.590), channel_id=1, source_target_pairs={{0,16},{16,32},{32,48},{48,64},{64,80},{80,96},{96,112},{112,0},{1... | collective-permute-start | bytes 786440 | tf_op jit(solution)/shard_map/while/body/eval_jaxpr/ppermute | solution.py:11
  95.1 8.9 %collective-permute-start = (bf16[16,8192]{1,0:T(8,128)(2,1)S(1)}, bf16[16,8192]{1,0:T(8,128)(2,1)S(1)}, u32[]{:S(2)}, u32[]{:S(2)}) collective-permute-start(bf16[16,8192]{1,0:T(8,128)(2,1)S(1)} %get-tuple-element.590), channel_id=1, source_target_pairs={{0,16},{16,32},{32,48},{48,64},{64,80},{80,96},{96,112},{112,0},{1... | collective-permute-start | bytes 786440 | tf_op jit(solution)/shard_map/while/body/eval_jaxpr/ppermute | solution.py:11
  108.0 8.6 %collective-permute-start = (bf16[16,8192]{1,0:T(8,128)(2,1)S(1)}, bf16[16,8192]{1,0:T(8,128)(2,1)S(1)}, u32[]{:S(2)}, u32[]{:S(2)}) collective-permute-start(bf16[16,8192]{1,0:T(8,128)(2,1)S(1)} %get-tuple-element.590), channel_id=1, source_target_pairs={{0,16},{16,32},{32,48},{48,64},{64,80},{80,96},{96,112},{112,0},{1... | collective-permute-start | bytes 786440 | tf_op jit(solution)/shard_map/while/body/eval_jaxpr/ppermute | solution.py:11
  120.6 8.6 %collective-permute-start = (bf16[16,8192]{1,0:T(8,128)(2,1)S(1)}, bf16[16,8192]{1,0:T(8,128)(2,1)S(1)}, u32[]{:S(2)}, u32[]{:S(2)}) collective-permute-start(bf16[16,8192]{1,0:T(8,128)(2,1)S(1)} %get-tuple-element.590), channel_id=1, source_target_pairs={{0,16},{16,32},{32,48},{48,64},{64,80},{80,96},{96,112},{112,0},{1... | collective-permute-start | bytes 786440 | tf_op jit(solution)/shard_map/while/body/eval_jaxpr/ppermute | solution.py:11
  133.2 8.6 %collective-permute-start = (bf16[16,8192]{1,0:T(8,128)(2,1)S(1)}, bf16[16,8192]{1,0:T(8,128)(2,1)S(1)}, u32[]{:S(2)}, u32[]{:S(2)}) collective-permute-start(bf16[16,8192]{1,0:T(8,128)(2,1)S(1)} %get-tuple-element.590), channel_id=1, source_target_pairs={{0,16},{16,32},{32,48},{48,64},{64,80},{80,96},{96,112},{112,0},{1... | collective-permute-start | bytes 786440 | tf_op jit(solution)/shard_map/while/body/eval_jaxpr/ppermute | solution.py:11
  145.8 8.6 %collective-permute-start = (bf16[16,8192]{1,0:T(8,128)(2,1)S(1)}, bf16[16,8192]{1,0:T(8,128)(2,1)S(1)}, u32[]{:S(2)}, u32[]{:S(2)}) collective-permute-start(bf16[16,8192]{1,0:T(8,128)(2,1)S(1)} %get-tuple-element.590), channel_id=1, source_target_pairs={{0,16},{16,32},{32,48},{48,64},{64,80},{80,96},{96,112},{112,0},{1... | collective-permute-start | bytes 786440 | tf_op jit(solution)/shard_map/while/body/eval_jaxpr/ppermute | solution.py:11
  163.0 14.4 %collective-permute-start.1 = (f32[16,8192]{1,0:T(8,128)S(1)}, f32[16,8192]{1,0:T(8,128)S(1)}, u32[]{:S(2)}, u32[]{:S(2)}) collective-permute-start(f32[16,8192]{1,0:T(8,128)S(1)} %get-tuple-element.625), channel_id=1, source_target_pairs={{0,112},{16,0},{32,16},{48,32},{64,48},{80,64},{96,80},{112,96},{1... | collective-permute-start | bytes 1572872 | tf_op jit(solution)/shard_map/while/body/eval_jaxpr/ppermute | solution.py:11
  177.8 14.2 %collective-permute-start.1 = (f32[16,8192]{1,0:T(8,128)S(1)}, f32[16,8192]{1,0:T(8,128)S(1)}, u32[]{:S(2)}, u32[]{:S(2)}) collective-permute-start(f32[16,8192]{1,0:T(8,128)S(1)} %get-tuple-element.625), channel_id=1, source_target_pairs={{0,112},{16,0},{32,16},{48,32},{64,48},{80,64},{96,80},{112,96},{1... | collective-permute-start | bytes 1572872 | tf_op jit(solution)/shard_map/while/body/eval_jaxpr/ppermute | solution.py:11
  192.5 13.4 %collective-permute-start.1 = (f32[16,8192]{1,0:T(8,128)S(1)}, f32[16,8192]{1,0:T(8,128)S(1)}, u32[]{:S(2)}, u32[]{:S(2)}) collective-permute-start(f32[16,8192]{1,0:T(8,128)S(1)} %get-tuple-element.625), channel_id=1, source_target_pairs={{0,112},{16,0},{32,16},{48,32},{64,48},{80,64},{96,80},{112,96},{1... | collective-permute-start | bytes 1572872 | tf_op jit(solution)/shard_map/while/body/eval_jaxpr/ppermute | solution.py:11
  206.3 16.1 %collective-permute-start.1 = (f32[16,8192]{1,0:T(8,128)S(1)}, f32[16,8192]{1,0:T(8,128)S(1)}, u32[]{:S(2)}, u32[]{:S(2)}) collective-permute-start(f32[16,8192]{1,0:T(8,128)S(1)} %get-tuple-element.625), channel_id=1, source_target_pairs={{0,112},{16,0},{32,16},{48,32},{64,48},{80,64},{96,80},{112,96},{1... | collective-permute-start | bytes 1572872 | tf_op jit(solution)/shard_map/while/body/eval_jaxpr/ppermute | solution.py:11
  222.9 15.3 %collective-permute-start.1 = (f32[16,8192]{1,0:T(8,128)S(1)}, f32[16,8192]{1,0:T(8,128)S(1)}, u32[]{:S(2)}, u32[]{:S(2)}) collective-permute-start(f32[16,8192]{1,0:T(8,128)S(1)} %get-tuple-element.625), channel_id=1, source_target_pairs={{0,112},{16,0},{32,16},{48,32},{64,48},{80,64},{96,80},{112,96},{1... | collective-permute-start | bytes 1572872 | tf_op jit(solution)/shard_map/while/body/eval_jaxpr/ppermute | solution.py:11
  238.6 14.4 %collective-permute-start.1 = (f32[16,8192]{1,0:T(8,128)S(1)}, f32[16,8192]{1,0:T(8,128)S(1)}, u32[]{:S(2)}, u32[]{:S(2)}) collective-permute-start(f32[16,8192]{1,0:T(8,128)S(1)} %get-tuple-element.625), channel_id=1, source_target_pairs={{0,112},{16,0},{32,16},{48,32},{64,48},{80,64},{96,80},{112,96},{1... | collective-permute-start | bytes 1572872 | tf_op jit(solution)/shard_map/while/body/eval_jaxpr/ppermute | solution.py:11
  253.4 11.4 %collective-permute-start.1 = (f32[16,8192]{1,0:T(8,128)S(1)}, f32[16,8192]{1,0:T(8,128)S(1)}, u32[]{:S(2)}, u32[]{:S(2)}) collective-permute-start(f32[16,8192]{1,0:T(8,128)S(1)} %get-tuple-element.625), channel_id=1, source_target_pairs={{0,112},{16,0},{32,16},{48,32},{64,48},{80,64},{96,80},{112,96},{1... | collective-permute-start | bytes 1572872 | tf_op jit(solution)/shard_map/while/body/eval_jaxpr/ppermute | solution.py:11
  273.5 1.6 copy-start.1
Sparse Core Ops, SparseCore 0:
  10.5 50.0 all-gather.1
  273.7 81.0 reduce-scatter.3
where the time goes:
time: 367 us; the launch traced here: 365 us
  waiting for transfers between devices  186 us (51%)
  matrix products  48.6 us (13%)
  local copies, waits for them, and re-layouts  42.1 us (11%)
  other arithmetic  29.5 us (8%)
  starting transfers between devices  22.1 us (6%)
  blocking collectives  21 us (6%)
  between operations  14.2 us (4%)
    ppermute x14, waiting for transfers between devices, passed_along(): return lax.ppermute(x, axis, [(i, (i + by) % count) for i in range(count)])  81 us
    unnamed x3, waiting for transfers between devices  57.6 us
    all_gather x1, waiting for transfers between devices, local(): full_in = lax.all_gather(features, 'feat', axis=0, tiled=True)  47.9 us
    ppermute x14, starting transfers between devices, passed_along(): return lax.ppermute(x, axis, [(i, (i + by) % count) for i in range(count)])  22.1 us
    psum x1, blocking collectives, local(): weight_term, bias_term = lax.psum((weight_term, bias_term), 'node')  21 us
    dot_general x8, matrix products, forward_part(): jnp.einsum('ftc,trc->ftr', picked, tile_block, preferred_element_type=jnp...  18.9 us
    dot_general x8, matrix products, backward_part(): jnp.einsum('ftr,trc->ftc', picked, tile_block, preferred_element_type=jnp...  15.8 us
    unnamed x14, local copies, waits for them, and re-layouts  10.8 us
  transfers between devices with their start and end apart: 16, of which 16 were waited for; matrix products, arithmetic and copies ran while one was open for 18% of the time, Pallas kernels for 0%

commit v1 on v0

v1 whole, which is shorter than its diff:
```python
import functools

import jax
import jax.numpy as jnp
from jax import lax
from jax.experimental import pallas as pl
from jax.experimental.pallas import tpu as pltpu
from jax.sharding import PartitionSpec as P

MESH = pl.DeviceIdType.MESH
VMEM = pltpu.VMEM
BF16 = jnp.bfloat16
F32 = jnp.float32
TILE = 128
GROUP = 8


def around():
    n, f = lax.axis_index("node"), lax.axis_index("feat")
    nx = lax.axis_size("node") // 2
    x, y = lax.rem(n, nx), n // nx

    def at(dx, dy):
        return (lax.rem(y + dy, 2)) * nx + lax.rem(x + dx + nx, nx)

    return n, f, at


def remote(src, dst, send, recv, node, feat):
    return pltpu.make_async_remote_copy(
        src_ref=src, dst_ref=dst, send_sem=send, recv_sem=recv, device_id=(node, feat), device_id_type=MESH
    )


def greet(n, f, nodes, n_feat):
    barrier = pltpu.get_barrier_semaphore()
    for d in range(1, n_feat):
        pl.semaphore_signal(barrier, inc=1, device_id=(n, lax.rem(f + d, n_feat)), device_id_type=MESH)
    for m in nodes:
        pl.semaphore_signal(barrier, inc=1, device_id=(m, f), device_id_type=MESH)
    pl.semaphore_wait(barrier, n_feat - 1 + len(nodes))


def gather_kernel(
    x_ref, w_ref, proj_ref, fin_out, wt_out, fin, wts, pst,
    w_send, w_recv, x_send, x_recv, p_send, p_recv, own_sem, n_send, n_recv,
):
    n, f, at = around()
    n_feat = fin.shape[0]
    span = fin.shape[2]
    per = pst.shape[1]
    channels = pst.shape[2]
    half = proj_ref.shape[1] // 2
    right, left, other = at(1, 0), at(-1, 0), at(0, 1)

    greet(n, f, (right, left, other), n_feat)

    def cols(p):
        return pl.ds(pl.multiple_of(p * span, span), span)

    wts[f] = w_ref[...].astype(F32).T.astype(BF16)
    sent = []
    for d in range(1, n_feat):
        p = lax.rem(f + d, n_feat)
        sent.append(remote(wts.at[f], wts.at[f], w_send.at[d], w_recv.at[d], n, p))
        sent[-1].start()
        sent.append(remote(x_ref.at[:, cols(p)], fin.at[f], x_send.at[d], x_recv.at[d], n, p))
        sent[-1].start()
    fin[f] = x_ref[:, cols(f)]
    for d in range(1, n_feat):
        p = lax.rem(f - d + n_feat, n_feat)
        remote(wts.at[p], wts.at[p], w_send.at[d], w_recv.at[d], n, p).wait_recv()
        remote(fin.at[p], fin.at[p], x_send.at[d], x_recv.at[d], n, p).wait_recv()

    xin = fin[...].astype(F32).reshape(n_feat * fin.shape[1], span).astype(BF16)
    wt = wts[...].reshape(n_feat * channels, wts.shape[2])
    fin_out[...] = xin
    wt_out[...] = wt
    proj = jnp.dot(wt, xin, preferred_element_type=F32).astype(BF16)
    for p in range(n_feat):
        for t in range(per):
            pst[p, t] = proj[p * channels:(p + 1) * channels, t * TILE:(t + 1) * TILE]

    for d in range(1, n_feat):
        p = lax.rem(f + d, n_feat)
        sent.append(remote(pst.at[p], proj_ref.at[n, pl.ds(f * per, per)], p_send.at[d], p_recv.at[d], n, p))
        sent[-1].start()
    mine = pltpu.make_async_copy(pst.at[f], proj_ref.at[n, pl.ds(f * per, per)], own_sem)
    mine.start()
    for d in range(1, n_feat):
        p = lax.rem(f - d + n_feat, n_feat)
        piece = proj_ref.at[n, pl.ds(p * per, per)]
        remote(piece, piece, p_send.at[d], p_recv.at[d], n, p).wait_recv()
    mine.wait()

    def whole(m):
        return proj_ref.at[m]

    def first(m):
        return proj_ref.at[m, pl.ds(0, half)]

    def second(m):
        return proj_ref.at[m, pl.ds(half, half)]

    def push(block, k, to):
        sent.append(remote(block, block, n_send.at[k], n_recv.at[k], to, f))
        sent[-1].start()

    def arrived(block, k):
        remote(block, block, n_send.at[k], n_recv.at[k], other, f).wait_recv()

    push(whole(n), 0, right)
    push(whole(n), 1, left)
    push(whole(n), 2, other)
    arrived(whole(left), 0)
    push(first(left), 3, right)
    arrived(whole(right), 1)
    push(second(right), 4, left)
    arrived(whole(other), 2)
    push(whole(other), 5, right)
    push(whole(other), 6, left)
    far = at(2, 0)
    arrived(first(far), 3)
    push(first(far), 7, other)
    arrived(second(far), 4)
    push(second(far), 8, other)
    arrived(whole(at(-1, 1)), 5)
    arrived(whole(at(1, 1)), 6)
    arrived(first(at(2, 1)), 7)
    arrived(second(at(2, 1)), 8)
    for copy in sent:
        copy.wait_send()


def layer_kernel(
    count_ref, rows_ref, cols_ref, bias_ref, cot_ref, proj_ref, tiles_ref,
    out_ref, part_ref, own_ref, gbias_ref,
    proj, tiles, acc, gpre, proj_sem, tile_sem,
):
    n = lax.axis_index("node")
    n_node, slots = tiles.shape[0], tiles.shape[1]
    row_tiles, channels = acc.shape[0], acc.shape[1]

    def shard(s):
        return lax.rem(n + s, n_node)

    def chunks(j):
        return (count_ref[j] + (GROUP - 1)) // GROUP

    def proj_copy(j):
        return pltpu.make_async_copy(proj_ref.at[j], proj.at[j], proj_sem.at[j])

    def tile_copy(j, c):
        span = pl.ds(c * GROUP, GROUP)
        return pltpu.make_async_copy(tiles_ref.at[j, span], tiles.at[j, span], tile_sem.at[j, c])

    @pl.loop(0, n_node)
    def _(s):
        j = shard(s)
        proj_copy(j).start()

        @pl.loop(0, chunks(j))
        def _(c):
            tile_copy(j, c).start()

    def products(j, c, source, index_ref, dims):
        made = []
        for u in range(GROUP):
            k = c * GROUP + u
            x = source(j, index_ref[j * slots + k])
            x = jnp.where(k < count_ref[j], x, jnp.zeros_like(x))
            made.append(lax.dot_general(x, tiles[j, k], (dims, ((), ())), preferred_element_type=F32))
        return made

    proj_copy(n).wait()
    bias = jnp.broadcast_to(bias_ref[...], (TILE, channels)).T
    for t in range(row_tiles):
        acc[t] = proj[n, t].astype(F32) + bias

    @pl.loop(0, n_node)
    def _(s):
        j = shard(s)

        @pl.when(s > 0)
        def _():
            proj_copy(j).wait()

        @pl.loop(0, chunks(j))
        def _(c):
            tile_copy(j, c).wait()
            made = products(j, c, lambda j, t: proj[j, t], cols_ref, ((1,), (1,)))
            for u in range(GROUP):
                r = rows_ref[j * slots + c * GROUP + u]
                acc[r] = acc[r] + made[u]

    total = jnp.zeros((channels, TILE), F32)
    for t in range(row_tiles):
        span = slice(t * TILE, (t + 1) * TILE)
        v = acc[t]
        s = jax.nn.sigmoid(v)
        out_ref[:, span] = (v * s).astype(BF16)
        g = (cot_ref[:, span].astype(F32) * s * (1.0 + v * (1.0 - s))).astype(BF16)
        gpre[t] = g
        wide = g.astype(F32)
        own_ref[t] = wide
        total = total + wide
    gbias_ref[...] = total

    def spread(j, target):
        @pl.loop(0, chunks(j))
        def _(c):
            made = products(j, c, lambda j, t: gpre[t], rows_ref, ((1,), (0,)))
            for u in range(GROUP):
                r = cols_ref[j * slots + c * GROUP + u]
                target[r] = target[r] + made[u]

    @pl.loop(1, n_node)
    def _(s):
        j = shard(s)
        acc[...] = jnp.zeros_like(acc)
        spread(j, acc)
        part_ref[j] = acc[...].astype(BF16)

    spread(n, own_ref)
    part_ref[n] = jnp.zeros(part_ref.shape[1:], BF16)


def reduce_kernel(
    norm, part_ref, own_ref, gbias_ref, fin_ref, wt_ref,
    gf_ref, gw_ref, gb_ref,
    far_in, dl_in, dr_in, hl_in, hr_in, fl_in, fr_in, fy_in,
    far_out, y_out, r_out, l_out, gp, gall, gst, wst, wall, nst, nall, ball,
    n_send, n_recv, b_send, b_recv, g_send, g_recv, f_send, f_recv, w_send, w_recv, a_send, a_recv, own_sem,
):
    n, f, at = around()
    n_node = part_ref.shape[0]
    half = part_ref.shape[1] // 2
    n_feat, per, channels = gall.shape[0], gall.shape[1], gall.shape[2]
    span = gst.shape[2]
    right, left, other = at(1, 0), at(-1, 0), at(0, 1)
    others = [lax.rem(n + d, n_node) for d in range(1, n_node)]

    greet(n, f, others, n_feat)

    sent = []

    def push(src, dst, send, recv, node, feat):
        sent.append(remote(src, dst, send, recv, node, feat))
        sent[-1].start()

    def arrived(dst, send, recv):
        remote(dst, dst, send, recv, other, f).wait_recv()

    def add(*terms):
        total = terms[0].astype(F32)
        for term in terms[1:]:
            total = total + term.astype(F32)
        return total

    push(part_ref.at[at(2, 1)], far_in, n_send.at[0], n_recv.at[0], other, f)
    push(part_ref.at[at(1, 1)], dl_in, n_send.at[1], n_recv.at[1], right, f)
    push(part_ref.at[at(-1, 1)], dr_in, n_send.at[2], n_recv.at[2], left, f)
    ball[n] = gbias_ref[...]
    for d in range(1, n_node):
        push(gbias_ref, ball.at[n], b_send.at[d], b_recv.at[d], others[d - 1], f)

    arrived(far_in, n_send.at[0], n_recv.at[0])
    far_out[...] = add(part_ref[at(2, 0)], far_in[...]).astype(BF16)
    push(far_out.at[pl.ds(0, half)], hl_in, n_send.at[3], n_recv.at[3], right, f)
    push(far_out.at[pl.ds(half, half)], hr_in, n_send.at[4], n_recv.at[4], left, f)
    arrived(dl_in, n_send.at[1], n_recv.at[1])
    arrived(dr_in, n_send.at[2], n_recv.at[2])
    y_out[...] = add(part_ref[other], dl_in[...], dr_in[...]).astype(BF16)
    push(y_out, fy_in, n_send.at[5], n_recv.at[5], other, f)
    arrived(hl_in, n_send.at[3], n_recv.at[3])
    r_out[pl.ds(0, half)] = add(part_ref[right, pl.ds(0, half)], hl_in[...]).astype(BF16)
    r_out[pl.ds(half, half)] = part_ref[right, pl.ds(half, half)]
    push(r_out, fl_in, n_send.at[6], n_recv.at[6], right, f)
    arrived(hr_in, n_send.at[4], n_recv.at[4])
    l_out[pl.ds(0, half)] = part_ref[left, pl.ds(0, half)]
    l_out[pl.ds(half, half)] = add(part_ref[left, pl.ds(half, half)], hr_in[...]).astype(BF16)
    push(l_out, fr_in, n_send.at[7], n_recv.at[7], left, f)
    arrived(fy_in, n_send.at[5], n_recv.at[5])
    arrived(fl_in, n_send.at[6], n_recv.at[6])
    arrived(fr_in, n_send.at[7], n_recv.at[7])
    gp[...] = add(own_ref[...], fl_in[...], fr_in[...], fy_in[...]).astype(BF16)

    for d in range(1, n_feat):
        p = lax.rem(f + d, n_feat)
        push(gp.at[pl.ds(p * per, per)], gall.at[f], g_send.at[d], g_recv.at[d], n, p)
    gall[f] = gp[pl.ds(f * per, per)]
    for d in range(1, n_feat):
        p = lax.rem(f - d + n_feat, n_feat)
        arrived(gall.at[p], g_send.at[d], g_recv.at[d])

    hidden = n_feat * channels
    g = jnp.concatenate([gall[:, t].reshape(hidden, TILE) for t in range(per)], axis=1)
    gf = lax.dot_general(wt_ref[...], g, (((0,), (0,)), ((), ())), preferred_element_type=F32)
    rows = gst.shape[1]
    for p in range(n_feat):
        gst[p] = gf[p * rows:(p + 1) * rows].astype(BF16)

    def cols(p):
        return pl.ds(pl.multiple_of(p * span, span), span)

    for d in range(1, n_feat):
        p = lax.rem(f + d, n_feat)
        push(gst.at[p], gf_ref.at[:, cols(f)], f_send.at[d], f_recv.at[d], n, p)
    mine = pltpu.make_async_copy(gst.at[f], gf_ref.at[:, cols(f)], own_sem)
    mine.start()

    gw = lax.dot_general(g, fin_ref[...], (((1,), (1,)), ((), ())), preferred_element_type=F32) * norm
    wst[...] = gw.reshape(wst.shape)
    for d in range(1, n_feat):
        p = lax.rem(f + d, n_feat)
        push(wst.at[p], wall.at[f], w_send.at[d], w_recv.at[d], n, p)
    wall[f] = wst[f]
    for d in range(1, n_feat):
        p = lax.rem(f - d + n_feat, n_feat)
        arrived(wall.at[p], w_send.at[d], w_recv.at[d])
    nst[...] = jnp.sum(wall[...], axis=0)
    for d in range(1, n_node):
        push(nst, nall.at[n], a_send.at[d], a_recv.at[d], others[d - 1], f)
    nall[n] = nst[...]
    for d in range(1, n_node):
        m = lax.rem(n - d + n_node, n_node)
        arrived(ball.at[m], b_send.at[d], b_recv.at[d])
        arrived(nall.at[m], a_send.at[d], a_recv.at[d])
    gw_ref[...] = jnp.sum(nall[...], axis=0).T
    gb_ref[...] = jnp.sum(jnp.sum(ball[...], axis=0).T, axis=0, keepdims=True) * norm
    for d in range(1, n_feat):
        p = lax.rem(f - d + n_feat, n_feat)
        arrived(gf_ref.at[:, cols(p)], f_send.at[d], f_recv.at[d])
    mine.wait()
    for copy in sent:
        copy.wait_send()


def local(features, weight, bias, tile_values, tile_rows, tile_cols, tile_count, cotangent):
    n_node, n_feat = lax.axis_size("node"), lax.axis_size("feat")
    rows, nodes = features.shape
    inputs, channels = weight.shape
    hidden = channels * n_feat
    row_tiles = nodes // TILE
    per = row_tiles // n_feat
    span = per * TILE
    slots = tile_rows.shape[2]
    dma = pltpu.SemaphoreType.DMA
    in_vmem = pl.BlockSpec(memory_space=VMEM)
    in_smem = pl.BlockSpec(memory_space=pltpu.SMEM)
    anywhere = pl.BlockSpec(memory_space=pl.ANY)
    block = (row_tiles, channels, TILE)

    proj, fin, wt = pl.pallas_call(
        gather_kernel,
        out_shape=(
            jax.ShapeDtypeStruct((n_node,) + block, BF16),
            jax.ShapeDtypeStruct((inputs, span), BF16),
            jax.ShapeDtypeStruct((hidden, inputs), BF16),
        ),
        in_specs=[in_vmem] * 2,
        out_specs=(anywhere, in_vmem, in_vmem),
        scratch_shapes=[
            VMEM((n_feat, rows, span), BF16),
            VMEM((n_feat, channels, inputs), BF16),
            VMEM((n_feat, per, channels, TILE), BF16),
        ] + [dma((n_feat,))] * 6 + [dma(()), dma((9,)), dma((9,))],
        compiler_params=pltpu.CompilerParams(
            collective_id=0, has_side_effects=True, vmem_limit_bytes=16 << 20
        ),
        name="gather",
    )(features, weight)

    out, part, own, gbias = pl.pallas_call(
        layer_kernel,
        out_shape=(
            jax.ShapeDtypeStruct((channels, nodes), BF16),
            jax.ShapeDtypeStruct((n_node,) + block, BF16),
            jax.ShapeDtypeStruct(block, F32),
            jax.ShapeDtypeStruct((channels, TILE), F32),
        ),
        in_specs=[in_smem] * 3 + [in_vmem] * 2 + [anywhere] * 2,
        out_specs=(in_vmem,) * 4,
        scratch_shapes=[
            VMEM((n_node,) + block, BF16),
            VMEM((n_node, slots, TILE, TILE), BF16),
            VMEM(block, F32),
            VMEM(block, BF16),
            dma((n_node,)),
            dma((n_node, slots // GROUP)),
        ],
        compiler_params=pltpu.CompilerParams(vmem_limit_bytes=40 << 20),
        name="layer",
    )(
        tile_count.reshape(-1), tile_rows.reshape(-1), tile_cols.reshape(-1),
        bias.reshape(1, channels), cotangent, proj, tile_values[0],
    )

    def blocks(k):
        return [VMEM(block, BF16)] * k

    half = (row_tiles // 2,) + block[1:]
    gf, gw, gb = pl.pallas_call(
        functools.partial(reduce_kernel, 1.0 / float(nodes * n_node) ** 0.5),
        out_shape=(
            jax.ShapeDtypeStruct((rows, nodes), BF16),
            jax.ShapeDtypeStruct((inputs, channels), F32),
            jax.ShapeDtypeStruct((1, channels), F32),
        ),
        in_specs=[in_vmem] * 5,
        out_specs=(anywhere, in_vmem, in_vmem),
        scratch_shapes=blocks(3) + [VMEM(half, BF16)] * 2 + blocks(8) + [
            VMEM((n_feat, per, channels, TILE), BF16),
            VMEM((n_feat, rows, span), BF16),
            VMEM((n_feat, channels, inputs), F32),
            VMEM((n_feat, channels, inputs), F32),
            VMEM((channels, inputs), F32),
            VMEM((n_node, channels, inputs), F32),
            VMEM((n_node, channels, TILE), F32),
            dma((8,)), dma((8,)), dma((n_node,)), dma((n_node,)),
        ] + [dma((n_feat,))] * 6 + [dma((n_node,)), dma((n_node,)), dma(())],
        compiler_params=pltpu.CompilerParams(
            collective_id=1, has_side_effects=True, vmem_limit_bytes=24 << 20
        ),
        name="reduce",
    )(part, own, gbias, fin, wt)
    return out, gf, gw, gb.reshape(channels)


def solution(mesh):
    return jax.shard_map(
        local,
        mesh=mesh,
        in_specs=(
            P("feat", "node"),
            P(None, "feat"),
            P("feat"),
            P("node", None, None, None, None),
            P("node", None, None),
            P("node", None, None),
            P("node", None),
            P("feat", "node"),
        ),
        out_specs=(P("feat", "node"), P("feat", "node"), P(None, "feat"), P("feat")),
        check_vma=False,
    )
```

time: 367 us -> 99.5 us (0.27)
  waiting for transfers between devices: 186 us -> 0 us
  Pallas kernels: 0 us -> 91.1 us
  matrix products: 48.6 us -> 0 us
  local copies, waits for them, and re-layouts: 42.1 us -> 7.33 us
  other arithmetic: 29.5 us -> 0 us
  starting transfers between devices: 22.1 us -> 0 us
  blocking collectives: 21 us -> 0 us
  between operations: 14.2 us -> 0.67 us
    pallas_call x0 -> x3, Pallas kernels: none -> 91.1 us  [the longest x1 41.8 us: local(): pl.pallas_call(functools.partial(reduce_kernel, 1.0 / float(nodes * n_nod...]
    ppermute x14 -> x0, waiting for transfers between devices: 81 us -> none  [passed_along(): return lax.ppermute(x, axis, [(i, (i + by) % count) for i in range(count)])]
    unnamed x3 -> x0, waiting for transfers between devices: 57.6 us -> none
    dot_general x35 -> x0, matrix products: 48.6 us -> none  [the longest x8 18.9 us: forward_part(): jnp.einsum('ftc,trc->ftr', picked, tile_block, preferred_element_type=jnp...]
    all_gather x1 -> x0, waiting for transfers between devices: 47.9 us -> none  [local(): full_in = lax.all_gather(features, 'feat', axis=0, tiled=True)]
    ppermute x14 -> x0, starting transfers between devices: 22.1 us -> none  [passed_along(): return lax.ppermute(x, axis, [(i, (i + by) % count) for i in range(count)])]
    psum x1 -> x0, blocking collectives: 21 us -> none  [local(): weight_term, bias_term = lax.psum((weight_term, bias_term), 'node')]
    eq x16 -> x0, local copies, waits for them, and re-layouts: 11.2 us -> none  [the longest x8 5.58 us: backward_part(): col_list[None, :] == jnp.arange(row_tiles)[:, None]]
  transfers between devices with their start and end apart: 16 -> 0, of which waited for: 16 -> 0; matrix products, arithmetic and copies ran while one was open for 18% -> 0% of each run, Pallas kernels for 0% -> 0%
where the time goes in v1:
time: 99.5 us; the launch traced here: 99.1 us
  Pallas kernels  91.1 us (92%)
  local copies, waits for them, and re-layouts  7.33 us (7%)
    pallas_call x1, Pallas kernels, local(): pl.pallas_call(functools.partial(reduce_kernel, 1.0 / float(nodes * n_nod...  41.8 us
    pallas_call x1, Pallas kernels, local(): pl.pallas_call(gather_kernel, out_shape=(jax.ShapeDtypeStruct((n_node,) +...  39.1 us
    pallas_call x1, Pallas kernels, local(): pl.pallas_call(layer_kernel, out_shape=(jax.ShapeDtypeStruct((channels, n...  10.2 us
    unnamed x12, local copies, waits for them, and re-layouts  5.81 us

profile of v1, /device:TPU:0, one launch (start us, length us, event | category | flops | bytes accessed | tf_op | source)
XLA Modules:
  0.0 99.1 jit_solution(15054118243247721535)
XLA Ops:
  0.6 0.8 reshape.24.rows_ref
  1.4 0.8 reshape.25.cols_ref
  2.2 0.8 copy.12.w_ref
  3.0 0.0 copy-start.1
  3.0 0.9 copy-done.1
  3.9 39.1 %gather.1 = (bf16[8,64,16,128]{3,2,1,0:T(8,128)(2,1)S(1)}, bf16[128,512]{1,0:T(8,128)(2,1)S(1)}, bf16[256,128]{1,0:T(8,128)(2,1)S(1)}) custom-call(bf16[8,8192]{1,0:T(8,128)(2,1)S(1)} %copy-done.1, bf16[128,16]{1,0:T(8,128)(2,1)S(1)} %copy.12.w_ref), custom_call_target="tpu_custom_call" | custom-call | tf_op jit(solution)/shard_map/gather/pallas_call | solution.py:354
  43.0 0.0 copy-start
  43.0 0.9 copy-done
  44.0 0.0 copy-start.2
  44.0 0.7 copy-done.2
  44.6 0.0 copy-start.3
  44.6 0.7 copy-done.3
  45.3 10.2 %layer.1 = (bf16[16,8192]{1,0:T(8,128)(2,1)}, bf16[8,64,16,128]{3,2,1,0:T(8,128)(2,1)S(1)}, f32[64,16,128]{2,1,0:T(8,128)S(1)}, f32[16,128]{1,0:T(8,128)S(1)}) custom-call(s32[8]{0:T(128)S(1)} %bitcast.4, s32[384]{0:T(512)S(1)} %reshape.24.rows_ref, s32[384]{0:T(512)S(1)} %reshape.25.cols_ref, f32[1,16]{1,0:T(1,128)S(1)} %bitcast.5, ...), custom_call_target="tpu_custom_call" | custom-call | tf_op jit(solution)/shard_map/layer/pallas_call | solution.py:374
  55.4 41.8 %reduce.1 = (bf16[8,8192]{1,0:T(8,128)(2,1)S(1)}, f32[128,16]{1,0:T(8,128)S(1)}, f32[1,16]{1,0:T(1,128)S(1)}) custom-call(bf16[8,64,16,128]{3,2,1,0:T(8,128)(2,1)S(1)} %get-tuple-element.16.part_ref, f32[64,16,128]{2,1,0:T(8,128)S(1)} %get-tuple-element.17.own_ref, f32[16,128]{1,0:T(8,128)S(1)} %get-tuple-element.18.gbias_ref, ...), custom_call_target="tpu_custom_call" | custom-call | tf_op jit(solution)/shard_map/reduce/pallas_call | solution.py:403
  97.3 0.7 copy.13
  97.9 0.7 copy.16
  98.6 0.5 copy.17
Async XLA Ops:
  3.0 0.9 copy-start.1
  43.0 1.0 copy-start
  44.0 0.7 copy-start.2
  44.6 0.7 copy-start.3

commit v2 on v0

v2 whole, which is shorter than its diff:
```python
import functools

import jax
import jax.numpy as jnp
from jax import lax
from jax.experimental import pallas as pl
from jax.experimental.pallas import tpu as pltpu
from jax.sharding import PartitionSpec as P

MESH = pl.DeviceIdType.MESH
VMEM = pltpu.VMEM
BF16 = jnp.bfloat16
F32 = jnp.float32
TILE = 128
GROUP = 8


def around():
    n, f = lax.axis_index("node"), lax.axis_index("feat")
    nx = lax.axis_size("node") // 2
    x, y = lax.rem(n, nx), n // nx

    def at(dx, dy):
        return (lax.rem(y + dy, 2)) * nx + lax.rem(x + dx + nx, nx)

    return n, f, at


def remote(src, dst, send, recv, node, feat):
    return pltpu.make_async_remote_copy(
        src_ref=src, dst_ref=dst, send_sem=send, recv_sem=recv, device_id=(node, feat), device_id_type=MESH
    )


def greet(places):
    barrier = pltpu.get_barrier_semaphore()
    for place in places:
        pl.semaphore_signal(barrier, inc=1, device_id=place, device_id_type=MESH)
    pl.semaphore_wait(barrier, len(places))


def lanes(t, width):
    return pl.ds(pl.multiple_of(t * width, width), width)


class Sender:
    def __init__(self):
        self.sent = []

    def push(self, src, dst, send, recv, node, feat):
        self.sent.append(remote(src, dst, send, recv, node, feat))
        self.sent[-1].start()

    def arrived(self, dst, send, recv):
        remote(dst, dst, send, recv, lax.axis_index("node"), lax.axis_index("feat")).wait_recv()

    def finish(self):
        for copy in self.sent:
            copy.wait_send()


def gather_kernel(x_ref, all_ref, own_sem, send, recv):
    n, f, at = around()
    half = x_ref.shape[1] // 2
    right, left, other, far = at(1, 0), at(-1, 0), at(0, 1), at(2, 0)
    link = Sender()
    greet([(right, f), (left, f), (other, f)])

    def whole(m):
        return all_ref.at[m]

    def first(m):
        return all_ref.at[m, :, pl.ds(0, half)]

    def second(m):
        return all_ref.at[m, :, pl.ds(half, half)]

    def push(block, k, to, src=None):
        link.push(block if src is None else src, block, send.at[k], recv.at[k], to, f)

    def arrived(block, k):
        link.arrived(block, send.at[k], recv.at[k])

    push(whole(n), 0, right, x_ref)
    push(whole(n), 1, left, x_ref)
    push(whole(n), 2, other, x_ref)
    mine = pltpu.make_async_copy(x_ref, whole(n), own_sem)
    mine.start()
    arrived(whole(left), 0)
    push(first(left), 3, right)
    arrived(whole(right), 1)
    push(second(right), 4, left)
    arrived(whole(other), 2)
    push(whole(other), 5, right)
    push(whole(other), 6, left)
    arrived(first(far), 3)
    push(first(far), 7, other)
    arrived(second(far), 4)
    push(second(far), 8, other)
    arrived(whole(at(-1, 1)), 5)
    arrived(whole(at(1, 1)), 6)
    arrived(first(at(2, 1)), 7)
    arrived(second(at(2, 1)), 8)
    mine.wait()
    link.finish()


def tile_stream(count, tiles_ref, tiles, sems):
    def chunks(j):
        return (count[0, j] + (GROUP - 1)) // GROUP

    def copy(j, c):
        span = pl.ds(c * GROUP, GROUP)
        return pltpu.make_async_copy(tiles_ref.at[j, span], tiles.at[j, span], sems.at[j, c])

    return chunks, copy


def products(count, index_ref, tiles, source, j, c, dims):
    made = []
    for u in range(GROUP):
        k = c * GROUP + u
        x = source(index_ref[0, j, k])
        x = jnp.where(k < count[0, j], x, jnp.zeros_like(x))
        made.append(lax.dot_general(x, tiles[j, k], (dims, ((), ())), preferred_element_type=F32))
    return made


def forward_kernel(count, rows, cols, x_ref, tiles_ref, z_ref, tiles, acc, sems):
    n = lax.axis_index("node")
    n_node = tiles.shape[0]
    chunks, copy = tile_stream(count, tiles_ref, tiles, sems)

    @pl.loop(0, n_node)
    def _(s):
        j = lax.rem(n + s, n_node)

        @pl.loop(0, chunks(j))
        def _(c):
            copy(j, c).start()

    for t in range(acc.shape[0]):
        acc[t] = x_ref[n, :, t * TILE:(t + 1) * TILE].astype(F32)

    @pl.loop(0, n_node)
    def _(s):
        j = lax.rem(n + s, n_node)

        @pl.loop(0, chunks(j))
        def _(c):
            copy(j, c).wait()
            made = products(
                count, cols, tiles, lambda t: x_ref[j, :, lanes(t, TILE)], j, c, ((1,), (1,))
            )
            for u in range(GROUP):
                r = rows[0, j, c * GROUP + u]
                acc[r] = acc[r] + made[u]

    for t in range(acc.shape[0]):
        z_ref[:, t * TILE:(t + 1) * TILE] = acc[t].astype(BF16)


def dense_kernel(
    norm, z_ref, cot_ref, wt_ref, bias_ref,
    h_ref, out_ref, gw_ref,
    zin, cin, win, wst, hst, ost, gst, gin,
    z_send, z_recv, c_send, c_recv, w_send, w_recv, h_send, h_recv, o_send, o_recv, g_send, g_recv, own_sem,
):
    n, f, _ = around()
    n_feat, rows, span = zin.shape
    channels, inputs = wt_ref.shape
    hidden = n_feat * channels
    link = Sender()
    ahead = [lax.rem(f + d, n_feat) for d in range(n_feat)]
    behind = [lax.rem(f - d + n_feat, n_feat) for d in range(n_feat)]
    partners = range(1, n_feat)

    wst[0] = wt_ref[...].astype(F32)
    wst[1] = jnp.broadcast_to(bias_ref[...], (inputs, channels)).T
    own_cot = pltpu.make_async_copy(cot_ref.at[:, lanes(f, span)], cin.at[f], own_sem.at[0])
    own_cot.start()
    win[f] = wst[...]
    zin[f] = z_ref[:, lanes(f, span)]
    greet([(n, p) for p in ahead[1:]])
    for d in partners:
        p = ahead[d]
        link.push(z_ref.at[:, lanes(p, span)], zin.at[f], z_send.at[d], z_recv.at[d], n, p)
    for d in partners:
        link.push(wst, win.at[f], w_send.at[d], w_recv.at[d], n, ahead[d])
    for d in partners:
        p = ahead[d]
        link.push(cot_ref.at[:, lanes(p, span)], cin.at[f], c_send.at[d], c_recv.at[d], n, p)
    for d in partners:
        p = behind[d]
        link.arrived(zin.at[p], z_send.at[d], z_recv.at[d])
        link.arrived(win.at[p], w_send.at[d], w_recv.at[d])
    z = zin[...].astype(F32).reshape(n_feat * rows, span).astype(BF16)
    wt = win[:, 0].reshape(hidden, inputs).astype(BF16)
    bias = win[:, 1].reshape(hidden, inputs)[:, :1]
    pre = jnp.dot(wt, z, preferred_element_type=F32) + bias
    for d in partners:
        link.arrived(cin.at[behind[d]], c_send.at[d], c_recv.at[d])
    own_cot.wait()
    s = jax.nn.sigmoid(pre)
    cot = cin[...].reshape(hidden, span).astype(F32)
    g = (cot * s * (1.0 + pre * (1.0 - s))).astype(BF16)
    h = lax.dot_general(wt, g, (((0,), (0,)), ((), ())), preferred_element_type=F32)
    hst[...] = h.reshape(n_feat, rows, span).astype(BF16)
    for d in partners:
        p = ahead[d]
        link.push(hst.at[p], h_ref.at[:, lanes(f, span)], h_send.at[d], h_recv.at[d], n, p)
    own_h = pltpu.make_async_copy(hst.at[f], h_ref.at[:, lanes(f, span)], own_sem.at[1])
    own_h.start()
    gst[:, 0] = (
        lax.dot_general(g, z, (((1,), (1,)), ((), ())), preferred_element_type=F32) * norm
    ).reshape(n_feat, channels, inputs)
    wide = g.astype(F32)
    gb = wide[:, :TILE]
    for t in range(1, span // TILE):
        gb = gb + wide[:, t * TILE:(t + 1) * TILE]
    gst[:, 1] = jnp.broadcast_to(
        jnp.sum(gb, axis=1, keepdims=True) * norm, (hidden, inputs)
    ).reshape(n_feat, channels, inputs)
    for d in partners:
        p = ahead[d]
        link.push(gst.at[p], gin.at[f], g_send.at[d], g_recv.at[d], n, p)
    gin[f] = gst[f]
    ost[...] = (pre * s).astype(BF16).reshape(n_feat, channels, span)
    for d in partners:
        p = ahead[d]
        link.push(ost.at[p], out_ref.at[:, lanes(f, span)], o_send.at[d], o_recv.at[d], n, p)
    own_out = pltpu.make_async_copy(ost.at[f], out_ref.at[:, lanes(f, span)], own_sem.at[2])
    own_out.start()
    for d in partners:
        link.arrived(gin.at[behind[d]], g_send.at[d], g_recv.at[d])
    gw_ref[...] = jnp.sum(gin[...], axis=0)
    for d in partners:
        p = behind[d]
        link.arrived(h_ref.at[:, lanes(p, span)], h_send.at[d], h_recv.at[d])
        link.arrived(out_ref.at[:, lanes(p, span)], o_send.at[d], o_recv.at[d])
    own_h.wait()
    own_out.wait()
    link.finish()


def backward_kernel(
    count, rows, cols, h_ref, tiles_ref, made_out,
    part_ref, own_ref, out_ref, tiles, acc, sems, out_sem,
):
    n = lax.axis_index("node")
    n_node = tiles.shape[0]
    tile_count = acc.shape[0]
    chunks, copy = tile_stream(count, tiles_ref, tiles, sems)

    @pl.loop(1, n_node + 1)
    def _(s):
        j = lax.rem(n + s, n_node)

        @pl.loop(0, chunks(j))
        def _(c):
            copy(j, c).start()

    moved = pltpu.make_async_copy(made_out, out_ref, out_sem)
    moved.start()

    def spread(j):
        @pl.loop(0, chunks(j))
        def _(c):
            copy(j, c).wait()
            made = products(
                count, rows, tiles, lambda t: h_ref[:, lanes(t, TILE)], j, c, ((1,), (0,))
            )
            for u in range(GROUP):
                t = cols[0, j, c * GROUP + u]
                acc[t] = acc[t] + made[u]

    @pl.loop(1, n_node)
    def _(s):
        j = lax.rem(n + s, n_node)
        acc[...] = jnp.zeros_like(acc)
        spread(j)
        for t in range(tile_count):
            part_ref[j, :, t * TILE:(t + 1) * TILE] = acc[t].astype(BF16)

    for t in range(tile_count):
        acc[t] = h_ref[:, t * TILE:(t + 1) * TILE].astype(F32)
    spread(n)
    for t in range(tile_count):
        own_ref[:, t * TILE:(t + 1) * TILE] = acc[t]
    part_ref[n] = jnp.zeros(part_ref.shape[1:], BF16)
    moved.wait()


def reduce_kernel(
    part_ref, own_ref, gw_ref,
    gf_ref, gw_out, gb_out,
    far_in, dl_in, dr_in, hl_in, hr_in, fl_in, fr_in, fy_in,
    far_out, y_out, r_out, l_out, gy, gx, gsum,
    send, recv, g_send, g_recv,
):
    n, f, at = around()
    half = part_ref.shape[2] // 2
    right, left, other, far = at(1, 0), at(-1, 0), at(0, 1), at(2, 0)
    place = lax.rem(n, gx.shape[0])
    link = Sender()
    greet([(right, f), (left, f), (other, f), (far, f)])

    def push(src, dst, k, to):
        link.push(src, dst, send.at[k], recv.at[k], to, f)

    def arrived(dst, k):
        link.arrived(dst, send.at[k], recv.at[k])

    def add(*terms):
        total = terms[0].astype(F32)
        for term in terms[1:]:
            total = total + term.astype(F32)
        return total

    low, high = pl.ds(0, half), pl.ds(half, half)
    push(part_ref.at[at(2, 1)], far_in, 0, other)
    push(part_ref.at[at(1, 1)], dl_in, 1, right)
    push(part_ref.at[at(-1, 1)], dr_in, 2, left)
    link.push(gw_ref, gy, g_send.at[0], g_recv.at[0], other, f)

    arrived(far_in, 0)
    far_out[...] = add(part_ref[far], far_in[...]).astype(BF16)
    push(far_out.at[:, low], hl_in, 3, right)
    push(far_out.at[:, high], hr_in, 4, left)
    arrived(dl_in, 1)
    arrived(dr_in, 2)
    y_out[...] = add(part_ref[other], dl_in[...], dr_in[...]).astype(BF16)
    push(y_out, fy_in, 5, other)
    link.arrived(gy, g_send.at[0], g_recv.at[0])
    gsum[...] = gw_ref[...] + gy[...]
    link.push(gsum, gx.at[place], g_send.at[1], g_recv.at[1], right, f)
    link.push(gsum, gx.at[place], g_send.at[2], g_recv.at[2], left, f)
    link.push(gsum, gx.at[place], g_send.at[3], g_recv.at[3], far, f)
    gx[place] = gsum[...]
    arrived(hl_in, 3)
    r_out[:, low] = add(part_ref[right, :, low], hl_in[...]).astype(BF16)
    r_out[:, high] = part_ref[right, :, high]
    push(r_out, fl_in, 6, right)
    arrived(hr_in, 4)
    l_out[:, low] = part_ref[left, :, low]
    l_out[:, high] = add(part_ref[left, :, high], hr_in[...]).astype(BF16)
    push(l_out, fr_in, 7, left)
    nx = gx.shape[0]
    for k, m in ((1, left), (2, right), (3, far)):
        link.arrived(gx.at[lax.rem(m, nx)], g_send.at[k], g_recv.at[k])
    total = jnp.sum(gx[...], axis=0)
    gw_out[...] = total[0]
    gb_out[...] = total[1].T[:1]
    arrived(fy_in, 5)
    arrived(fl_in, 6)
    arrived(fr_in, 7)
    gf_ref[...] = add(own_ref[...], fl_in[...], fr_in[...], fy_in[...]).astype(BF16)
    link.finish()


def local(features, weight, bias, tile_values, tile_rows, tile_cols, tile_count, cotangent):
    n_node, n_feat = lax.axis_size("node"), lax.axis_size("feat")
    rows, nodes = features.shape
    inputs, channels = weight.shape
    row_tiles = nodes // TILE
    span = row_tiles // n_feat * TILE
    slots = tile_rows.shape[2]
    dma = pltpu.SemaphoreType.DMA
    in_vmem = pl.BlockSpec(memory_space=VMEM)
    in_smem = pl.BlockSpec(memory_space=pltpu.SMEM)
    in_hbm = pl.BlockSpec(memory_space=pltpu.HBM)
    anywhere = pl.BlockSpec(memory_space=pl.ANY)
    shape = jax.ShapeDtypeStruct
    tiles = tile_values[0]

    x_all = pl.pallas_call(
        gather_kernel,
        out_shape=shape((n_node, rows, nodes), BF16),
        in_specs=[in_hbm],
        out_specs=anywhere,
        scratch_shapes=[dma(()), dma((9,)), dma((9,))],
        compiler_params=pltpu.CompilerParams(
            collective_id=0, has_side_effects=True, vmem_limit_bytes=4 << 20
        ),
        name="gather",
    )(features)

    stream = [
        VMEM((n_node, slots, TILE, TILE), BF16),
        VMEM((row_tiles, rows, TILE), F32),
        dma((n_node, slots // GROUP)),
    ]
    z = pl.pallas_call(
        forward_kernel,
        out_shape=shape((rows, nodes), BF16),
        in_specs=[in_smem] * 3 + [in_vmem, in_hbm],
        out_specs=in_vmem,
        scratch_shapes=stream,
        compiler_params=pltpu.CompilerParams(vmem_limit_bytes=24 << 20),
        name="forward",
    )(tile_count, tile_rows, tile_cols, x_all, tiles)

    h, out, gw = pl.pallas_call(
        functools.partial(dense_kernel, 1.0 / float(nodes * n_node) ** 0.5),
        out_shape=(
            shape((rows, nodes), BF16),
            shape((channels, nodes), BF16),
            shape((2, channels, inputs), F32),
        ),
        in_specs=[in_vmem, in_hbm, in_vmem, in_vmem],
        out_specs=(anywhere, anywhere, in_vmem),
        scratch_shapes=[
            VMEM((n_feat, rows, span), BF16),
            VMEM((n_feat, channels, span), BF16),
            VMEM((n_feat, 2, channels, inputs), F32),
            VMEM((2, channels, inputs), F32),
            VMEM((n_feat, rows, span), BF16),
            VMEM((n_feat, channels, span), BF16),
            VMEM((n_feat, 2, channels, inputs), F32),
            VMEM((n_feat, 2, channels, inputs), F32),
        ] + [dma((n_feat,))] * 12 + [dma((3,))],
        compiler_params=pltpu.CompilerParams(
            collective_id=1, has_side_effects=True, vmem_limit_bytes=24 << 20
        ),
        name="dense",
    )(z, cotangent, weight.T, bias.reshape(1, channels))

    part, own, out = pl.pallas_call(
        backward_kernel,
        out_shape=(
            shape((n_node, rows, nodes), BF16),
            shape((rows, nodes), F32),
            shape((channels, nodes), BF16),
        ),
        in_specs=[in_smem] * 3 + [in_vmem, in_hbm, anywhere],
        out_specs=(in_vmem, in_vmem, in_hbm),
        scratch_shapes=stream + [dma(())],
        compiler_params=pltpu.CompilerParams(vmem_limit_bytes=24 << 20),
        name="backward",
    )(tile_count, tile_rows, tile_cols, h, tiles, out)

    block, half = VMEM((rows, nodes), BF16), VMEM((rows, nodes // 2), BF16)
    pair = (2, channels, inputs)
    gf, gwt, gb = pl.pallas_call(
        reduce_kernel,
        out_shape=(
            shape((rows, nodes), BF16),
            shape((channels, inputs), F32),
            shape((1, channels), F32),
        ),
        in_specs=[in_vmem] * 3,
        out_specs=(in_vmem,) * 3,
        scratch_shapes=[block] * 3 + [half] * 2 + [block] * 7 + [
            VMEM(pair, F32), VMEM((n_node // 2,) + pair, F32), VMEM(pair, F32),
            dma((8,)), dma((8,)), dma((4,)), dma((4,)),
        ],
        compiler_params=pltpu.CompilerParams(
            collective_id=2, has_side_effects=True, vmem_limit_bytes=16 << 20
        ),
        name="reduce",
    )(part, own, gw)
    return out, gf, gwt.T, gb.reshape(channels)


def solution(mesh):
    return jax.shard_map(
        local,
        mesh=mesh,
        in_specs=(
            P("feat", "node"),
            P(None, "feat"),
            P("feat"),
            P("node", None, None, None, None),
            P("node", None, None),
            P("node", None, None),
            P("node", None),
            P("feat", "node"),
        ),
        out_specs=(P("feat", "node"), P("feat", "node"), P(None, "feat"), P("feat")),
        check_vma=False,
    )
```

time: 367 us -> 81.1 us (0.22)
  waiting for transfers between devices: 186 us -> 0 us
  Pallas kernels: 0 us -> 70.6 us
  matrix products: 48.6 us -> 0 us
  local copies, waits for them, and re-layouts: 42.1 us -> 9.32 us
  other arithmetic: 29.5 us -> 0 us
  starting transfers between devices: 22.1 us -> 0 us
  blocking collectives: 21 us -> 0 us
  between operations: 14.2 us -> 0.73 us
    ppermute x14 -> x0, waiting for transfers between devices: 81 us -> none  [passed_along(): return lax.ppermute(x, axis, [(i, (i + by) % count) for i in range(count)])]
    pallas_call x0 -> x5, Pallas kernels: none -> 70.6 us  [the longest x1 28.9 us: local(): pl.pallas_call(functools.partial(dense_kernel, 1.0 / float(nodes * n_node...]
    unnamed x3 -> x0, waiting for transfers between devices: 57.6 us -> none
    dot_general x35 -> x0, matrix products: 48.6 us -> none  [the longest x8 18.9 us: forward_part(): jnp.einsum('ftc,trc->ftr', picked, tile_block, preferred_element_type=jnp...]
    all_gather x1 -> x0, waiting for transfers between devices: 47.9 us -> none  [local(): full_in = lax.all_gather(features, 'feat', axis=0, tiled=True)]
    ppermute x14 -> x0, starting transfers between devices: 22.1 us -> none  [passed_along(): return lax.ppermute(x, axis, [(i, (i + by) % count) for i in range(count)])]
    psum x1 -> x0, blocking collectives: 21 us -> none  [local(): weight_term, bias_term = lax.psum((weight_term, bias_term), 'node')]
    eq x16 -> x0, local copies, waits for them, and re-layouts: 11.2 us -> none  [the longest x8 5.58 us: backward_part(): col_list[None, :] == jnp.arange(row_tiles)[:, None]]
  transfers between devices with their start and end apart: 16 -> 0, of which waited for: 16 -> 0; matrix products, arithmetic and copies ran while one was open for 18% -> 0% of each run, Pallas kernels for 0% -> 0%
where the time goes in v2:
time: 81.1 us; the launch traced here: 80.7 us
  Pallas kernels  70.6 us (87%)
  local copies, waits for them, and re-layouts  9.32 us (11%)
    pallas_call x1, Pallas kernels, local(): pl.pallas_call(functools.partial(dense_kernel, 1.0 / float(nodes * n_node...  28.9 us
    pallas_call x1, Pallas kernels, local(): pl.pallas_call(gather_kernel, out_shape=shape((n_node, rows, nodes), BF16...  15.6 us
    pallas_call x1, Pallas kernels, local(): pl.pallas_call(reduce_kernel, out_shape=(shape((rows, nodes), BF16), shap...  14.8 us
    unnamed x21, local copies, waits for them, and re-layouts  9.32 us
    pallas_call x1, Pallas kernels, local(): pl.pallas_call(forward_kernel, out_shape=shape((rows, nodes), BF16), in_s...  6.09 us
    pallas_call x1, Pallas kernels, local(): pl.pallas_call(backward_kernel, out_shape=(shape((n_node, rows, nodes), B...  5.2 us

profile of v2, /device:TPU:0, one launch (start us, length us, event | category | flops | bytes accessed | tf_op | source)
XLA Modules:
  0.0 80.7 jit_solution(9060557960041681883)
XLA Ops:
  0.6 0.0 copy-start.2
  0.6 0.0 copy-start.3
  0.7 0.9 %copy-done.3 = bf16[8,8192]{1,0:T(8,128)(2,1)S(1)} copy-done((bf16[8,8192]{1,0:T(8,128)(2,1)S(1)}, bf16[8,8192]{1,0:T(8,128)(2,1)}, u32[]{:S(2)}) %copy-start.3) | copy-done | bytes 131096
  1.6 0.0 copy-start.6
  1.6 0.0 copy-start.8
  1.6 15.6 %gather.1.x_ref = bf16[8,8,8192]{2,1,0:T(8,128)(2,1)S(1)} custom-call(bf16[8,8192]{1,0:T(8,128)(2,1)S(1)} %copy-done.3), custom_call_target="tpu_custom_call" | custom-call | tf_op jit(solution)/shard_map/gather/pallas_call | solution.py:376
  17.2 0.0 copy-start
  17.3 4.6 %copy-done = bf16[1,8,48,128,128]{4,3,2,1,0:T(8,128)(2,1)S(1)} copy-done((bf16[1,8,48,128,128]{4,3,2,1,0:T(8,128)(2,1)S(1)}, bf16[1,8,48,128,128]{4,3,2,1,0:T(8,128)(2,1)}, u32[]{:S(2)}) %copy-start) | copy-done | bytes 12582936
  21.8 0.0 copy-start.4
  21.8 0.7 copy-done.4
  22.5 0.0 copy-start.5
  22.5 0.7 copy-done.5
  23.2 0.0 copy-start.7
  23.2 0.7 copy-done.7
  23.9 0.0 copy-start.1
  23.9 6.1 %forward.1.z_ref = bf16[8,8192]{1,0:T(8,128)(2,1)S(1)} custom-call(s32[1,8]{1,0:T(1,128)S(1)} %copy-done.7, s32[1,8,48]{2,1,0:T(8,128)S(1)} %copy-done.4, s32[1,8,48]{2,1,0:T(8,128)S(1)} %copy-done.5, bf16[8,8,8192]{2,1,0:T(8,128)(2,1)S(1)} %gather.1.x_ref, bf16[8,48,128,128]{3,2,1,0:T(8,128)(2,1)S(1)} %bitcast.5), custom_call_target="tpu_custom_call" | custom-call | tf_op jit(solution)/shard_map/forward/pallas_call | solution.py:393
  30.0 0.0 copy-done.2
  30.0 0.0 copy-done.6
  30.0 0.0 copy-done.8
  30.0 28.9 %dense.1 = (bf16[8,8192]{1,0:T(8,128)(2,1)S(1)}, bf16[16,8192]{1,0:T(8,128)(2,1)S(1)}, f32[2,16,128]{2,1,0:T(8,128)S(1)}) custom-call(bf16[8,8192]{1,0:T(8,128)(2,1)S(1)} %forward.1.z_ref, bf16[16,8192]{1,0:T(8,128)(2,1)S(1)} %copy-done.2, bf16[16,128]{1,0:T(8,128)(2,1)S(1)} %bitcast.8, f32[1,16]{1,0:T(1,128)S(1)} %bitcast.9), custom_call_target="tpu_custom_call" | custom-call | tf_op jit(solution)/shard_map/dense/pallas_call | solution.py:403
  58.9 0.0 copy-done.1
  58.9 5.2 %backward.1 = (bf16[8,8,8192]{2,1,0:T(8,128)(2,1)S(1)}, f32[8,8192]{1,0:T(8,128)S(1)}, bf16[16,8192]{1,0:T(8,128)(2,1)}) custom-call(s32[1,8]{1,0:T(1,128)S(1)} %copy-done.7, s32[1,8,48]{2,1,0:T(8,128)S(1)} %copy-done.4, s32[1,8,48]{2,1,0:T(8,128)S(1)} %copy-done.5, bf16[8,8192]{1,0:T(8,128)(2,1)S(1)} %get-tuple-element.13.h_ref, ...), custom_call_target="tpu_custom_call" | custom-call | tf_op jit(solution)/shard_map/backward/pallas_call | solution.py:428
  64.1 14.8 %reduce.1 = (bf16[8,8192]{1,0:T(8,128)(2,1)S(1)}, f32[16,128]{1,0:T(8,128)S(1)}, f32[1,16]{1,0:T(1,128)S(1)}) custom-call(bf16[8,8,8192]{2,1,0:T(8,128)(2,1)S(1)} %get-tuple-element.16.part_ref, f32[8,8192]{1,0:T(8,128)S(1)} %get-tuple-element.17.own_ref, f32[2,16,128]{2,1,0:T(8,128)S(1)} %get-tuple-element.18.gw_ref), custom_call_target="tpu_custom_call" | custom-call | tf_op jit(solution)/shard_map/reduce/pallas_call | solution.py:444
  78.9 0.7 copy.15
  79.5 0.6 copy.16
  80.1 0.5 copy.17
Async XLA Ops:
  0.6 29.3 %copy-start.2 = (bf16[16,8192]{1,0:T(8,128)(2,1)S(1)}, bf16[16,8192]{1,0:T(8,128)(2,1)}, u32[]{:S(2)}) copy-start(bf16[16,8192]{1,0:T(8,128)(2,1)} %cot_ref.1) | copy-start | bytes 786436
  0.6 0.9 %copy-start.3 = (bf16[8,8192]{1,0:T(8,128)(2,1)S(1)}, bf16[8,8192]{1,0:T(8,128)(2,1)}, u32[]{:S(2)}) copy-start(bf16[8,8192]{1,0:T(8,128)(2,1)} %x_ref.1) | copy-start | bytes 393220
  1.6 28.4 %copy-start.6 = (bf16[128,16]{0,1:T(8,128)(2,1)S(1)}, bf16[128,16]{0,1:T(8,128)(2,1)}, u32[]{:S(2)}) copy-start(bf16[128,16]{0,1:T(8,128)(2,1)} %param.9) | copy-start | bytes 12292
  1.6 28.4 %copy-start.8 = (f32[16]{0:T(128)S(1)}, f32[16]{0:T(128)}, u32[]{:S(2)}) copy-start(f32[16]{0:T(128)} %param.10) | copy-start | bytes 196
  17.2 4.6 %copy-start = (bf16[1,8,48,128,128]{4,3,2,1,0:T(8,128)(2,1)S(1)}, bf16[1,8,48,128,128]{4,3,2,1,0:T(8,128)(2,1)}, u32[]{:S(2)}) copy-start(bf16[1,8,48,128,128]{4,3,2,1,0:T(8,128)(2,1)} %param.11) | copy-start | bytes 37748740
  21.8 0.7 copy-start.4
  22.5 0.7 copy-start.5
  23.2 0.7 copy-start.7
  23.9 35.0 %copy-start.1 = (bf16[1,8,48,128,128]{4,3,2,1,0:T(8,128)(2,1)S(1)}, bf16[1,8,48,128,128]{4,3,2,1,0:T(8,128)(2,1)}, u32[]{:S(2)}) copy-start(bf16[1,8,48,128,128]{4,3,2,1,0:T(8,128)(2,1)} %param.11) | copy-start | bytes 37748740

commit v3 on v2

v3 whole, which is shorter than its diff:
```python
import functools

import jax
import jax.numpy as jnp
from jax import lax
from jax.experimental import pallas as pl
from jax.experimental.pallas import tpu as pltpu
from jax.sharding import PartitionSpec as P

MESH = pl.DeviceIdType.MESH
VMEM = pltpu.VMEM
BF16 = jnp.bfloat16
F32 = jnp.float32
TILE = 128
GROUP = 8


def around():
    n, f = lax.axis_index("node"), lax.axis_index("feat")
    nx = lax.axis_size("node") // 2
    x, y = lax.rem(n, nx), n // nx

    def at(dx, dy):
        return (lax.rem(y + dy, 2)) * nx + lax.rem(x + dx + nx, nx)

    return n, f, at


def remote(src, dst, send, recv, node, feat):
    return pltpu.make_async_remote_copy(
        src_ref=src, dst_ref=dst, send_sem=send, recv_sem=recv, device_id=(node, feat), device_id_type=MESH
    )


def greet(places):
    barrier = pltpu.get_barrier_semaphore()
    for place in places:
        pl.semaphore_signal(barrier, inc=1, device_id=place, device_id_type=MESH)
    pl.semaphore_wait(barrier, len(places))


def lanes(t, width):
    return pl.ds(pl.multiple_of(t * width, width), width)


class Sender:
    def __init__(self):
        self.sent = []

    def push(self, src, dst, send, recv, node, feat):
        self.sent.append(remote(src, dst, send, recv, node, feat))
        self.sent[-1].start()

    def arrived(self, dst, send, recv):
        remote(dst, dst, send, recv, lax.axis_index("node"), lax.axis_index("feat")).wait_recv()

    def finish(self):
        for copy in self.sent:
            copy.wait_send()


def meeting(n, f, at, n_feat):
    other = at(0, 1)
    near = [(at(1, 0), f), (at(-1, 0), f), (other, f)]
    if n_feat != 16:
        return near + [(n, lax.rem(f + d, n_feat)) for d in range(1, n_feat)], []
    z, y, core = f // 4, lax.rem(f // 2, 2), lax.rem(f, 2)
    along_y = [(other, f), (other, z * 4 + (1 - y) * 2 + core)]
    along_z = [(n, lax.rem(z + d, 4) * 4 + y * 2 + core) for d in (1, 3)]
    beside = [(n, f + 1 - 2 * core)]
    return near + along_y[1:] + along_z + beside, [along_y, along_z, along_z, beside]


def relay(rounds, sems, first, last):
    for i in range(first, min(last, len(rounds))):
        for place in rounds[i]:
            pl.semaphore_signal(sems.at[i], inc=1, device_id=place, device_id_type=MESH)
        pl.semaphore_wait(sems.at[i], len(rounds[i]))


def ring(f, n_feat):
    ahead = [lax.rem(f + d, n_feat) for d in range(n_feat)]
    behind = [lax.rem(f - d + n_feat, n_feat) for d in range(n_feat)]
    return ahead, behind, range(1, n_feat)


def split(x):
    high = x.astype(BF16).astype(F32)
    mid = (x - high).astype(BF16).astype(F32)
    lane = lax.broadcasted_iota(jnp.int32, x.shape, 1)
    rest = jnp.where(lane == 1, mid, jnp.where(lane == 2, x - high - mid, 0.0))
    return jnp.where(lane == 0, high, rest).astype(BF16)


def by_tile(x_ref, out_ref):
    for t in range(out_ref.shape[0]):
        out_ref[t] = x_ref[:, t * TILE:(t + 1) * TILE]


def own_products(index, x_ref, tiles, n, out_ref, dims):
    @pl.loop(0, out_ref.shape[0] // GROUP)
    def _(c):
        for u in range(GROUP):
            k = c * GROUP + u
            x = x_ref[index[0, n, k]]
            out_ref[k] = lax.dot_general(x, tiles[n, k], (dims, ((), ())), preferred_element_type=F32)


def gather_kernel(
    x_ref, tiles_ref, cot_ref, count_ref, rows_ref, cols_ref, wt_ref, bias_ref,
    all_ref, tiles, made, cin, win, count_out, rows_out, cols_out,
    x_own, x_tiles, cols, wst, met, local_sem, tile_sem, send, recv, c_send, c_recv, w_send, w_recv,
):
    n, f, at = around()
    n_feat, channels, span = cin.shape
    inputs = wt_ref.shape[1]
    n_node = tiles.shape[0]
    half = x_ref.shape[1] // 2
    right, left, other, far = at(1, 0), at(-1, 0), at(0, 1), at(2, 0)
    ahead, behind, partners = ring(f, n_feat)
    link = Sender()
    here = [
        pltpu.make_async_copy(x_ref, x_own, local_sem.at[0]),
        pltpu.make_async_copy(cols_ref, cols, local_sem.at[1]),
        pltpu.make_async_copy(x_ref, all_ref.at[n], local_sem.at[2]),
        pltpu.make_async_copy(cot_ref.at[:, lanes(f, span)], cin.at[f], local_sem.at[3]),
        pltpu.make_async_copy(count_ref, count_out, local_sem.at[4]),
        pltpu.make_async_copy(rows_ref, rows_out, local_sem.at[5]),
        pltpu.make_async_copy(cols_ref, cols_out, local_sem.at[6]),
    ]
    places, rounds = meeting(n, f, at, n_feat)
    greet(places)

    def whole(m):
        return all_ref.at[m]

    def first(m):
        return all_ref.at[m, :, pl.ds(0, half)]

    def second(m):
        return all_ref.at[m, :, pl.ds(half, half)]

    def push(block, k, to, src=None):
        link.push(block if src is None else src, block, send.at[k], recv.at[k], to, f)

    def arrived(block, k):
        link.arrived(block, send.at[k], recv.at[k])

    push(whole(n), 0, right, x_ref)
    push(whole(n), 1, left, x_ref)
    push(whole(n), 2, other, x_ref)
    for copy in here:
        copy.start()
    moved = [
        pltpu.make_async_copy(tiles_ref.at[j], tiles.at[j], tile_sem.at[s])
        for s, j in enumerate([n] + [lax.rem(n + s, n_node) for s in range(1, n_node)])
    ]
    for copy in moved:
        copy.start()
    wst[0] = wt_ref[...]
    bias = jnp.broadcast_to(bias_ref[...], (inputs, channels)).T
    wst[1] = split(bias)
    win[f] = wst[...]
    relay(rounds, met, 0, 3)
    arrived(whole(left), 0)
    push(first(left), 3, right)
    arrived(whole(right), 1)
    push(second(right), 4, left)
    arrived(whole(other), 2)
    push(whole(other), 5, right)
    push(whole(other), 6, left)
    relay(rounds, met, 3, 4)
    for d in partners:
        p = ahead[d]
        link.push(cot_ref.at[:, lanes(p, span)], cin.at[f], c_send.at[d], c_recv.at[d], n, p)
        link.push(wst, win.at[f], w_send.at[d], w_recv.at[d], n, p)
    here[0].wait()
    here[1].wait()
    moved[0].wait()
    by_tile(x_own, x_tiles)
    own_products(cols, x_tiles, tiles, n, made, ((1,), (1,)))
    arrived(first(far), 3)
    push(first(far), 7, other)
    arrived(second(far), 4)
    push(second(far), 8, other)
    arrived(whole(at(-1, 1)), 5)
    arrived(whole(at(1, 1)), 6)
    for d in partners:
        p = behind[d]
        link.arrived(cin.at[p], c_send.at[d], c_recv.at[d])
        link.arrived(win.at[p], w_send.at[d], w_recv.at[d])
    for copy in here[2:] + moved[1:]:
        copy.wait()
    arrived(first(at(2, 1)), 7)
    arrived(second(at(2, 1)), 8)
    link.finish()


def add_products(count, index, target, tiles, source, acc, j, dims):
    @pl.loop(0, (count[0, j] + (GROUP - 1)) // GROUP)
    def _(c):
        made = []
        for u in range(GROUP):
            k = c * GROUP + u
            x = source(index[0, j, k])
            x = jnp.where(k < count[0, j], x, jnp.zeros_like(x))
            made.append(lax.dot_general(x, tiles[j, k], (dims, ((), ())), preferred_element_type=F32))
        for u in range(GROUP):
            t = target[0, j, c * GROUP + u]
            acc[t] = acc[t] + made[u]


def place_products(target, made, acc, n):
    @pl.loop(0, made.shape[0] // GROUP)
    def _(c):
        for u in range(GROUP):
            t = target[0, n, c * GROUP + u]
            acc[t] = acc[t] + made[c * GROUP + u]


def forward_kernel(count, rows, cols, x_ref, tiles, made, z_ref, acc):
    n = lax.axis_index("node")
    n_node = tiles.shape[0]
    for t in range(acc.shape[0]):
        acc[t] = x_ref[n, :, t * TILE:(t + 1) * TILE].astype(F32)
    place_products(rows, made, acc, n)

    @pl.loop(1, n_node)
    def _(s):
        j = lax.rem(n + s, n_node)
        add_products(
            count, cols, rows, tiles, lambda t: x_ref[j, :, lanes(t, TILE)], acc, j, ((1,), (1,))
        )

    for t in range(acc.shape[0]):
        z_ref[:, t * TILE:(t + 1) * TILE] = acc[t].astype(BF16)


def dense_kernel(
    norm, z_ref, cin, win,
    h_ref, ost, gw_ref,
    zin, hst, gst, gin,
    z_send, z_recv, h_send, h_recv, g_send, g_recv, own_sem,
):
    n, f, _ = around()
    n_feat, rows, span = zin.shape
    channels, inputs = win.shape[2:]
    hidden = n_feat * channels
    link = Sender()
    ahead, behind, partners = ring(f, n_feat)

    zin[f] = z_ref[:, lanes(f, span)]
    greet([(n, p) for p in ahead[1:]])
    for d in partners:
        p = ahead[d]
        link.push(z_ref.at[:, lanes(p, span)], zin.at[f], z_send.at[d], z_recv.at[d], n, p)
    wt = win[:, 0].reshape(hidden, inputs)
    bias = jnp.sum(win[:, 1].reshape(hidden, inputs).astype(F32), axis=1, keepdims=True)
    cot = cin[...].reshape(hidden, span)
    for d in partners:
        link.arrived(zin.at[behind[d]], z_send.at[d], z_recv.at[d])
    z = zin[...].astype(F32).reshape(n_feat * rows, span).astype(BF16)
    pre = jnp.dot(wt, z, preferred_element_type=F32) + bias
    s = jax.nn.sigmoid(pre)
    g = (cot.astype(F32) * s * (1.0 + pre * (1.0 - s))).astype(BF16)
    h = lax.dot_general(wt, g, (((0,), (0,)), ((), ())), preferred_element_type=F32)
    hst[...] = h.reshape(n_feat, rows, span).astype(BF16)
    for d in partners:
        p = ahead[d]
        link.push(hst.at[p], h_ref.at[:, lanes(f, span)], h_send.at[d], h_recv.at[d], n, p)
    own_h = pltpu.make_async_copy(hst.at[f], h_ref.at[:, lanes(f, span)], own_sem)
    own_h.start()
    gst[:, 0] = (
        lax.dot_general(g, z, (((1,), (1,)), ((), ())), preferred_element_type=F32) * norm
    ).astype(BF16).reshape(n_feat, channels, inputs)
    wide = g.astype(F32)
    gb = wide[:, :TILE]
    for t in range(1, span // TILE):
        gb = gb + wide[:, t * TILE:(t + 1) * TILE]
    gb = jnp.sum(gb, axis=1, keepdims=True) * norm
    gst[:, 1] = split(jnp.broadcast_to(gb, (hidden, inputs))).reshape(n_feat, channels, inputs)
    for d in partners:
        p = ahead[d]
        link.push(gst.at[p], gin.at[f], g_send.at[d], g_recv.at[d], n, p)
    gin[f] = gst[f]
    ost[...] = (pre * s).astype(BF16).reshape(n_feat, channels, span)
    for d in partners:
        p = behind[d]
        link.arrived(h_ref.at[:, lanes(p, span)], h_send.at[d], h_recv.at[d])
        link.arrived(gin.at[p], g_send.at[d], g_recv.at[d])
    own_h.wait()
    gw_ref[...] = jnp.sum(gin[...].astype(F32), axis=0)
    link.finish()


def backward_kernel(count, rows, cols, h_ref, tiles, part_ref, acc):
    n = lax.axis_index("node")
    n_node = tiles.shape[0]

    @pl.loop(1, n_node)
    def _(s):
        j = lax.rem(n + s, n_node)
        acc[...] = jnp.zeros_like(acc)
        add_products(count, rows, cols, tiles, lambda t: h_ref[:, lanes(t, TILE)], acc, j, ((1,), (0,)))
        for t in range(acc.shape[0]):
            part_ref[j, :, t * TILE:(t + 1) * TILE] = acc[t].astype(BF16)

    part_ref[n] = jnp.zeros(part_ref.shape[1:], BF16)


def reduce_kernel(
    rows, part_ref, h_ref, tiles, gw_ref, ost,
    fl_in, fr_in, fy_in, made, gw_out, gb_out, out_ref,
    far_in, dl_in, dr_in, hl_in, hr_in, far_out, y_out, r_out, l_out, gy, gx, gsum, h_tiles,
    met, send, recv, g_send, g_recv, o_send, o_recv, own_sem,
):
    n, f, at = around()
    n_feat, _, span = ost.shape
    half = part_ref.shape[2] // 2
    right, left, other, far = at(1, 0), at(-1, 0), at(0, 1), at(2, 0)
    nx = gx.shape[0]
    place = lax.rem(n, nx)
    ahead, behind, partners = ring(f, n_feat)
    link = Sender()
    places, rounds = meeting(n, f, at, n_feat)
    greet(places)

    def push(src, dst, k, to):
        link.push(src, dst, send.at[k], recv.at[k], to, f)

    def arrived(dst, k):
        link.arrived(dst, send.at[k], recv.at[k])

    def add(*terms):
        total = terms[0].astype(F32)
        for term in terms[1:]:
            total = total + term.astype(F32)
        return total

    low, high = pl.ds(0, half), pl.ds(half, half)
    push(part_ref.at[at(2, 1)], far_in, 0, other)
    push(part_ref.at[at(1, 1)], dl_in, 1, right)
    push(part_ref.at[at(-1, 1)], dr_in, 2, left)
    link.push(gw_ref, gy, g_send.at[0], g_recv.at[0], other, f)
    own_out = pltpu.make_async_copy(ost.at[f], out_ref.at[:, lanes(f, span)], own_sem)
    own_out.start()
    relay(rounds, met, 0, 3)

    arrived(far_in, 0)
    far_out[...] = add(part_ref[far], far_in[...]).astype(BF16)
    push(far_out.at[:, low], hl_in, 3, right)
    push(far_out.at[:, high], hr_in, 4, left)
    arrived(dl_in, 1)
    arrived(dr_in, 2)
    y_out[...] = add(part_ref[other], dl_in[...], dr_in[...]).astype(BF16)
    push(y_out, fy_in, 5, other)
    link.arrived(gy, g_send.at[0], g_recv.at[0])
    gsum[...] = gw_ref[...] + gy[...]
    link.push(gsum, gx.at[place], g_send.at[1], g_recv.at[1], right, f)
    link.push(gsum, gx.at[place], g_send.at[2], g_recv.at[2], left, f)
    gx[place] = gsum[...]
    arrived(hl_in, 3)
    r_out[:, low] = add(part_ref[right, :, low], hl_in[...]).astype(BF16)
    r_out[:, high] = part_ref[right, :, high]
    push(r_out, fl_in, 6, right)
    arrived(hr_in, 4)
    l_out[:, low] = part_ref[left, :, low]
    l_out[:, high] = add(part_ref[left, :, high], hr_in[...]).astype(BF16)
    push(l_out, fr_in, 7, left)
    link.push(gsum, gx.at[place], g_send.at[3], g_recv.at[3], far, f)
    relay(rounds, met, 3, 4)
    for d in partners:
        p = ahead[d]
        link.push(ost.at[p], out_ref.at[:, lanes(f, span)], o_send.at[d], o_recv.at[d], n, p)
    by_tile(h_ref, h_tiles)
    own_products(rows, h_tiles, tiles, n, made, ((1,), (0,)))
    for k, m in ((1, left), (2, right), (3, far)):
        link.arrived(gx.at[lax.rem(m, nx)], g_send.at[k], g_recv.at[k])
    total = jnp.sum(gx[...], axis=0)
    gw_out[...] = total[0]
    gb_out[...] = jnp.sum(total[1].T, axis=0, keepdims=True)
    arrived(fy_in, 5)
    arrived(fl_in, 6)
    arrived(fr_in, 7)
    for d in partners:
        link.arrived(out_ref.at[:, lanes(behind[d], span)], o_send.at[d], o_recv.at[d])
    own_out.wait()
    link.finish()


def final_kernel(
    cols, h_ref, fl, fr, fy, made, gw_ref, gb_ref, made_out,
    gf_ref, gw_out, gb_out, out_ref, acc, out_sem,
):
    n = lax.axis_index("node")
    moved = pltpu.make_async_copy(made_out, out_ref, out_sem)
    moved.start()
    for t in range(acc.shape[0]):
        span = slice(t * TILE, (t + 1) * TILE)
        acc[t] = (
            h_ref[:, span].astype(F32) + fl[:, span].astype(F32)
            + fr[:, span].astype(F32) + fy[:, span].astype(F32)
        )
    place_products(cols, made, acc, n)
    for t in range(acc.shape[0]):
        gf_ref[:, t * TILE:(t + 1) * TILE] = acc[t].astype(BF16)
    gw_out[...] = gw_ref[...]
    gb_out[...] = gb_ref[...]
    moved.wait()


def local(features, weight, bias, tile_values, tile_rows, tile_cols, tile_count, cotangent):
    n_node, n_feat = lax.axis_size("node"), lax.axis_size("feat")
    rows, nodes = features.shape
    inputs, channels = weight.shape
    row_tiles = nodes // TILE
    span = row_tiles // n_feat * TILE
    slots = tile_rows.shape[2]
    dma = pltpu.SemaphoreType.DMA
    in_vmem = pl.BlockSpec(memory_space=VMEM)
    in_smem = pl.BlockSpec(memory_space=pltpu.SMEM)
    in_hbm = pl.BlockSpec(memory_space=pltpu.HBM)
    shape = jax.ShapeDtypeStruct
    block = (rows, nodes)
    pair = (2, channels, inputs)

    def params(mib, **more):
        return pltpu.CompilerParams(vmem_limit_bytes=mib << 20, **more)

    def keep(x):
        return pltpu.with_memory_space_constraint(x, pltpu.HBM)

    def pairs(k):
        return [dma((n_feat,))] * k

    met = pltpu.SemaphoreType.REGULAR((4,))
    x_all, tiles, made, cin, win, count, row_list, col_list = pl.pallas_call(
        gather_kernel,
        out_shape=(
            shape((n_node,) + block, BF16),
            shape(tile_values.shape[1:], BF16),
            shape((slots, rows, TILE), F32),
            shape((n_feat, channels, span), BF16),
            shape((n_feat,) + pair, BF16),
            shape(tile_count.shape, jnp.int32),
            shape(tile_rows.shape, jnp.int32),
            shape(tile_cols.shape, jnp.int32),
        ),
        in_specs=[in_hbm] * 6 + [in_vmem] * 2,
        out_specs=(in_vmem,) * 8,
        scratch_shapes=[
            VMEM(block, BF16), VMEM((row_tiles, rows, TILE), BF16), pltpu.SMEM(tile_cols.shape, jnp.int32), VMEM(pair, BF16),
            met, dma((7,)), dma((n_node,)), dma((9,)), dma((9,)),
        ] + pairs(4),
        compiler_params=params(20, collective_id=0, has_side_effects=True),
        name="gather",
    )(
        keep(features), keep(tile_values[0]), keep(cotangent),
        keep(tile_count), keep(tile_rows), keep(tile_cols),
        weight.T, bias.reshape(1, channels),
    )

    acc = VMEM((row_tiles, rows, TILE), F32)
    z = pl.pallas_call(
        forward_kernel,
        out_shape=shape(block, BF16),
        in_specs=[in_smem] * 3 + [in_vmem] * 3,
        out_specs=in_vmem,
        scratch_shapes=[acc],
        compiler_params=params(16),
        name="forward",
    )(count, row_list, col_list, x_all, tiles, made)

    h, ost, gw = pl.pallas_call(
        functools.partial(dense_kernel, 1.0 / float(nodes * n_node) ** 0.5),
        out_shape=(
            shape(block, BF16),
            shape((n_feat, channels, span), BF16),
            shape(pair, F32),
        ),
        in_specs=[in_vmem] * 3,
        out_specs=(in_vmem,) * 3,
        scratch_shapes=[
            VMEM((n_feat, rows, span), BF16),
            VMEM((n_feat, rows, span), BF16),
            VMEM((n_feat,) + pair, BF16),
            VMEM((n_feat,) + pair, BF16),
        ] + pairs(6) + [dma(())],
        compiler_params=params(16, collective_id=1, has_side_effects=True),
        name="dense",
    )(z, cin, win)

    part = pl.pallas_call(
        backward_kernel,
        out_shape=shape((n_node,) + block, BF16),
        in_specs=[in_smem] * 3 + [in_vmem] * 2,
        out_specs=in_vmem,
        scratch_shapes=[acc],
        compiler_params=params(16),
        name="backward",
    )(count, row_list, col_list, h, tiles)

    whole, half = VMEM(block, BF16), VMEM((rows, nodes // 2), BF16)
    fl, fr, fy, made, gwt, gb, out = pl.pallas_call(
        reduce_kernel,
        out_shape=(
            shape(block, BF16),
            shape(block, BF16),
            shape(block, BF16),
            shape((slots, rows, TILE), F32),
            shape((channels, inputs), F32),
            shape((1, channels), F32),
            shape((channels, nodes), BF16),
        ),
        in_specs=[in_smem] + [in_vmem] * 5,
        out_specs=(in_vmem,) * 7,
        scratch_shapes=[whole] * 3 + [half] * 2 + [whole] * 4 + [
            VMEM(pair, F32), VMEM((n_node // 2,) + pair, F32), VMEM(pair, F32),
            VMEM((row_tiles, rows, TILE), BF16),
            met, dma((8,)), dma((8,)), dma((4,)), dma((4,)),
        ] + pairs(2) + [dma(())],
        compiler_params=params(16, collective_id=2, has_side_effects=True),
        name="reduce",
    )(row_list, part, h, tiles, gw, ost)

    gf, gwt, gb, out = pl.pallas_call(
        final_kernel,
        out_shape=(
            shape(block, BF16),
            shape((channels, inputs), F32),
            shape((1, channels), F32),
            shape((channels, nodes), BF16),
        ),
        in_specs=[in_smem] + [in_vmem] * 8,
        out_specs=(in_vmem,) * 3 + (in_hbm,),
        scratch_shapes=[acc, dma(())],
        compiler_params=params(16),
        name="final",
    )(col_list, h, fl, fr, fy, made, gwt, gb, out)
    return out, gf, gwt.T, gb.reshape(channels)


def solution(mesh):
    return jax.shard_map(
        local,
        mesh=mesh,
        in_specs=(
            P("feat", "node"),
            P(None, "feat"),
            P("feat"),
            P("node", None, None, None, None),
            P("node", None, None),
            P("node", None, None),
            P("node", None),
            P("feat", "node"),
        ),
        out_specs=(P("feat", "node"), P("feat", "node"), P(None, "feat"), P("feat")),
        check_vma=False,
    )
```

time: 81.1 us -> 68.4 us (0.84)
  local copies, waits for them, and re-layouts: 9.32 us -> 1.33 us
  Pallas kernels: 70.6 us -> 65.1 us
    pallas_call x1, Pallas kernels: 28.9 us -> 16.8 us  [local(): pl.pallas_call(functools.partial(dense_kernel, 1.0 / float(nodes * n_node...]
    unnamed x21 -> x4, local copies, waits for them, and re-layouts: 9.32 us -> 1.33 us
    pallas_call x4 -> x5, Pallas kernels: 41.7 us -> 48.3 us  [the longest x1 21.4 us: local(): pl.pallas_call(gather_kernel, out_shape=(shape((n_node,) + block, BF16),...]
where the time goes in v3:
time: 68.4 us; the launch traced here: 67.1 us
  Pallas kernels  65.1 us (95%)
  local copies, waits for them, and re-layouts  1.33 us (2%)
    pallas_call x1, Pallas kernels, local(): pl.pallas_call(gather_kernel, out_shape=(shape((n_node,) + block, BF16),...  21.4 us
    pallas_call x1, Pallas kernels, local(): pl.pallas_call(reduce_kernel, out_shape=(shape(block, BF16), shape(block,...  18.6 us
    pallas_call x1, Pallas kernels, local(): pl.pallas_call(functools.partial(dense_kernel, 1.0 / float(nodes * n_node...  16.8 us
    pallas_call x1, Pallas kernels, local(): pl.pallas_call(forward_kernel, out_shape=shape(block, BF16), in_specs=[in...  3.48 us
    pallas_call x1, Pallas kernels, local(): pl.pallas_call(backward_kernel, out_shape=shape((n_node,) + block, BF16),...  2.78 us
    pallas_call x1, Pallas kernels, local(): pl.pallas_call(final_kernel, out_shape=(shape(block, BF16), shape((channe...  1.97 us

profile of v3, /device:TPU:0, one launch (start us, length us, event | category | flops | bytes accessed | tf_op | source)
XLA Modules:
  0.0 67.1 jit_solution(14937934066371814118)
XLA Ops:
  0.6 0.0 copy-start
  0.6 0.7 %copy-done = bf16[128,16]{0,1:T(8,128)(2,1)S(1)} copy-done((bf16[128,16]{0,1:T(8,128)(2,1)S(1)}, bf16[128,16]{0,1:T(8,128)(2,1)}, u32[]{:S(2)}) %copy-start) | copy-done | bytes 4120
  1.3 0.0 copy-start.1
  1.3 0.7 copy-done.1
  2.0 21.4 %gather.1 = (bf16[8,8,8192]{2,1,0:T(8,128)(2,1)S(1)}, bf16[8,48,128,128]{3,2,1,0:T(8,128)(2,1)S(1)}, f32[48,8,128]{2,1,0:T(8,128)S(1)}, bf16[16,16,512]{2,1,0:T(...) custom-call(bf16[8,8192]{1,0:T(8,128)(2,1)} %x_ref.1, ...), custom_call_target="tpu_custom_call" | custom-call | tf_op jit(solution)/shard_map/gather/pallas_call | solution.py:437
  23.4 3.5 %forward.1.z_ref = bf16[8,8192]{1,0:T(8,128)(2,1)S(1)} custom-call(s32[1,8]{1,0:T(1,128)S(1)} %get-tuple-element.27.count, s32[1,8,48]{2,1,0:T(8,128)S(1)} %get-tuple-element.28.rows, s32[1,8,48]{2,1,0:T(8,128)S(1)} %get-tuple-element.26.cols, bf16[8,8,8192]{2,1,0:T(8,128)(2,1)S(1)} %get-tuple-element.29.x_ref, ...), custom_call_target="tpu_custom_call" | custom-call | tf_op jit(solution)/shard_map/forward/pallas_call | solution.py:464
  26.9 16.8 %dense.1 = (bf16[8,8192]{1,0:T(8,128)(2,1)S(1)}, bf16[16,16,512]{2,1,0:T(8,128)(2,1)S(1)}, f32[2,16,128]{2,1,0:T(8,128)S(1)}) custom-call(bf16[8,8192]{1,0:T(8,128)(2,1)S(1)} %forward.1.z_ref, bf16[16,16,512]{2,1,0:T(8,128)(2,1)S(1)} %get-tuple-element.32.cin, bf16[16,2,16,128]{3,2,1,0:T(8,128)(2,1)S(1)} %get-tuple-element.33.win), custom_call_target="tpu_custom_call" | custom-call | tf_op jit(solution)/shard_map/dense/pallas_call | solution.py:474
  43.8 2.8 %backward.1.part_ref = bf16[8,8,8192]{2,1,0:T(8,128)(2,1)S(1)} custom-call(s32[1,8]{1,0:T(1,128)S(1)} %get-tuple-element.27.count, s32[1,8,48]{2,1,0:T(8,128)S(1)} %get-tuple-element.28.rows, s32[1,8,48]{2,1,0:T(8,128)S(1)} %get-tuple-element.26.cols, bf16[8,8192]{1,0:T(8,128)(2,1)S(1)} %get-tuple-element.34.h_ref, ...), custom_call_target="tpu_custom_call" | custom-call | tf_op jit(solution)/shard_map/backward/pallas_call | solution.py:493
  46.6 18.6 %reduce.1 = (bf16[8,8192]{1,0:T(8,128)(2,1)S(1)}, bf16[8,8192]{1,0:T(8,128)(2,1)S(1)}, bf16[8,8192]{1,0:T(8,128)(2,1)S(1)}, f32[48,8,128]{2,1,0:T(8,128)S(1)}, f...) custom-call(s32[1,8,48]{2,1,0:T(8,128)S(1)} %get-tuple-element.28.rows, ...), custom_call_target="tpu_custom_call" | custom-call | tf_op jit(solution)/shard_map/reduce/pallas_call | solution.py:504
  65.2 2.0 %final.1 = (bf16[8,8192]{1,0:T(8,128)(2,1)}, f32[16,128]{1,0:T(8,128)}, f32[1,16]{1,0:T(1,128)}, bf16[16,8192]{1,0:T(8,128)(2,1)}) custom-call(s32[1,8,48]{2,1,0:T(8,128)S(1)} %get-tuple-element.26.cols, bf16[8,8192]{1,0:T(8,128)(2,1)S(1)} %get-tuple-element.34.h_ref, bf16[8,8192]{1,0:T(8,128)(2,1)S(1)} %get-tuple-element.37.fl, ...), custom_call_target="tpu_custom_call" | custom-call | tf_op jit(solution)/shard_map/final/pallas_call | solution.py:526
Async XLA Ops:
  0.6 0.7 %copy-start = (bf16[128,16]{0,1:T(8,128)(2,1)S(1)}, bf16[128,16]{0,1:T(8,128)(2,1)}, u32[]{:S(2)}) copy-start(bf16[128,16]{0,1:T(8,128)(2,1)} %param.9) | copy-start | bytes 12292
  1.3 0.7 copy-start.1

commit v4 on v3

v4 whole, which is shorter than its diff:
```python
import functools

import jax
import jax.numpy as jnp
from jax import lax
from jax.experimental import pallas as pl
from jax.experimental.pallas import tpu as pltpu
from jax.sharding import PartitionSpec as P

MESH = pl.DeviceIdType.MESH
VMEM = pltpu.VMEM
BF16 = jnp.bfloat16
F32 = jnp.float32
TILE = 128
GROUP = 8
LONG = 16


def around():
    n, f = lax.axis_index("node"), lax.axis_index("feat")
    nx = lax.axis_size("node") // 2
    x, y = lax.rem(n, nx), n // nx

    def at(dx, dy):
        return (lax.rem(y + dy, 2)) * nx + lax.rem(x + dx + nx, nx)

    return n, f, at


def remote(src, dst, send, recv, node, feat):
    return pltpu.make_async_remote_copy(
        src_ref=src, dst_ref=dst, send_sem=send, recv_sem=recv, device_id=(node, feat), device_id_type=MESH
    )


def greet(places):
    barrier = pltpu.get_barrier_semaphore()
    for place in places:
        pl.semaphore_signal(barrier, inc=1, device_id=place, device_id_type=MESH)


def met(places):
    pl.semaphore_wait(pltpu.get_barrier_semaphore(), len(places))


def lanes(t, width):
    return pl.ds(pl.multiple_of(t * width, width), width)


class Sender:
    def __init__(self):
        self.sent = []

    def push(self, src, dst, send, recv, node, feat):
        self.sent.append(remote(src, dst, send, recv, node, feat))
        self.sent[-1].start()

    def arrived(self, dst, send, recv):
        remote(dst, dst, send, recv, lax.axis_index("node"), lax.axis_index("feat")).wait_recv()

    def finish(self):
        for copy in self.sent:
            copy.wait_send()


def ring(f, n_feat):
    if n_feat != 16:
        return [(d, lax.rem(f + d, n_feat), lax.rem(f - d + n_feat, n_feat)) for d in range(1, n_feat)]
    z, y, core = f // 4, lax.rem(f // 2, 2), lax.rem(f, 2)

    def by(dz, dy, dc):
        return lax.rem(z + dz + 4, 4) * 4 + lax.rem(y + dy, 2) * 2 + lax.rem(core + dc, 2)

    offsets = [(dz, dy, dc) for dz in (2, 1, 3, 0) for dy in (1, 0) for dc in (1, 0)][:-1]
    offsets.sort(key=lambda d: -(min(d[0], 4 - d[0]) + 2 * d[1] + d[2]))
    return [(dz * 4 + dy * 2 + dc, by(dz, dy, dc), by(-dz, dy, dc)) for dz, dy, dc in offsets]


def everyone(n, f, at, partners):
    near = [(at(1, 0), f), (at(-1, 0), f), (at(0, 1), f)]
    return near + [(n, p) for _, p, _ in partners]


def split(x):
    high = x.astype(BF16).astype(F32)
    mid = (x - high).astype(BF16).astype(F32)
    lane = lax.broadcasted_iota(jnp.int32, x.shape, 1)
    rest = jnp.where(lane == 1, mid, jnp.where(lane == 2, x - high - mid, 0.0))
    return jnp.where(lane == 0, high, rest).astype(BF16)


def by_tile(x_ref, out_ref):
    for t in range(out_ref.shape[0]):
        out_ref[t] = x_ref[:, t * TILE:(t + 1) * TILE]


def own_products(index, x_ref, tiles, n, out_ref, dims):
    @pl.loop(0, out_ref.shape[0] // GROUP)
    def _(c):
        for u in range(GROUP):
            k = c * GROUP + u
            x = x_ref[index(k)]
            out_ref[k] = lax.dot_general(x, tiles[n * out_ref.shape[0] + k], (dims, ((), ())), preferred_element_type=F32)


def slot_list(count, rows, cols, n, n_node, out_ref):
    slots = rows.shape[2]
    width = out_ref.shape[1]
    q = lax.broadcasted_iota(jnp.int32, (slots, width), 1)
    k = lax.broadcasted_iota(jnp.int32, (slots, width), 0)
    line = lax.broadcasted_iota(jnp.int32, (8, slots), 0)
    number = lax.broadcasted_iota(jnp.int32, (8, slots), 1)
    total = jnp.zeros((8, width), F32)
    base = 0
    for s in range(1, n_node):
        j = lax.rem(n + s, n_node)
        used = count[0, j]
        hit = jnp.where((q == k + base) & (k < used), 1.0, 0.0).astype(BF16)
        mine = jnp.where(line == 0, number, jnp.where(line == 1, j, 0))
        mine = jnp.where(line == 2, rows[0, pl.ds(j, 1)], jnp.where(line == 3, cols[0, pl.ds(j, 1)], mine))
        total = total + jnp.dot(mine.astype(F32).astype(BF16), hit, preferred_element_type=F32)
        base = base + used
    out_ref[...] = jnp.where(
        lax.broadcasted_iota(jnp.int32, out_ref.shape, 0) == 6, base, total.astype(jnp.int32)
    )
    out_ref[4:5, :slots] = rows[0, pl.ds(n, 1)]
    out_ref[5:6, :slots] = cols[0, pl.ds(n, 1)]


def gather_kernel(
    x_ref, tiles_ref, cot_ref, count_ref, rows_ref, cols_ref, wt_ref, bias_ref,
    all_ref, tiles, made, cin, win, list_out,
    x_own, x_tiles, count, cols, rows_in, cols_in, wt, bias_in, wst,
    local_sem, tile_sem, send, recv, c_send, c_recv, w_send, w_recv,
):
    n, f, at = around()
    n_feat, channels, span = cin.shape
    inputs = wt_ref.shape[1]
    n_node = count_ref.shape[1]
    slots = made.shape[0]
    half = x_ref.shape[1] // 2
    right, left, other, far = at(1, 0), at(-1, 0), at(0, 1), at(2, 0)
    link = Sender()
    here = [
        pltpu.make_async_copy(src, dst, local_sem.at[i])
        for i, (src, dst) in enumerate([
            (wt_ref, wt), (bias_ref, bias_in), (count_ref, count), (rows_ref, rows_in), (cols_ref, cols_in),
            (cols_ref, cols), (x_ref, x_own),
            (x_ref, all_ref.at[n]), (cot_ref.at[:, lanes(f, span)], cin.at[f]),
        ])
    ]
    moved = [
        pltpu.make_async_copy(
            tiles_ref.at[pl.ds(j * slots, slots)], tiles.at[pl.ds(j * slots, slots)], tile_sem.at[s]
        )
        for s, j in enumerate([n] + [lax.rem(n + s, n_node) for s in range(1, n_node)])
    ]
    partners = ring(f, n_feat)
    places = everyone(n, f, at, partners)
    greet(places)
    for copy in here:
        copy.start()
    met(places)

    low, high = pl.ds(0, half), pl.ds(half, half)

    def push(m, part, k, to, src=None):
        block = all_ref.at[m, :, part]
        link.push(block if src is None else src.at[:, part], block, send.at[k], recv.at[k], to, f)

    def arrived(m, part, k):
        link.arrived(all_ref.at[m, :, part], send.at[k], recv.at[k])

    push(n, low, 0, right, x_ref)
    push(n, high, 1, left, x_ref)
    push(n, low, 2, other, x_ref)
    push(n, high, 3, right, x_ref)
    push(n, low, 4, left, x_ref)
    push(n, high, 5, other, x_ref)
    for d, p, _ in partners:
        link.push(cot_ref.at[:, lanes(p, span)], cin.at[f], c_send.at[d], c_recv.at[d], n, p)
    for copy in here[:2]:
        copy.wait()
    wst[0] = wt[...]
    wst[1] = split(jnp.broadcast_to(bias_in[...], (inputs, channels)).T)
    win[f] = wst[...]
    for d, p, _ in partners:
        link.push(wst, win.at[f], w_send.at[d], w_recv.at[d], n, p)
    for copy in moved:
        copy.start()
    arrived(left, low, 0)
    push(left, low, 6, right)
    arrived(right, high, 1)
    push(right, high, 7, left)
    arrived(other, low, 2)
    push(other, low, 8, right)
    push(other, low, 9, left)
    arrived(other, high, 5)
    push(other, high, 10, right)
    push(other, high, 11, left)
    for copy in here[2:7]:
        copy.wait()
    slot_list(count, rows_in, cols_in, n, n_node, list_out)
    arrived(far, low, 6)
    push(far, low, 12, other)
    arrived(far, high, 7)
    push(far, high, 13, other)
    moved[0].wait()
    by_tile(x_own, x_tiles)
    own_products(lambda k: cols[0, n, k], x_tiles, tiles, n, made, ((1,), (1,)))
    arrived(left, high, 3)
    arrived(right, low, 4)
    for m, k in ((at(-1, 1), 0), (at(1, 1), 1)):
        arrived(m, low, 8 + k)
        arrived(m, high, 10 + k)
    for d, _, p in partners:
        link.arrived(cin.at[p], c_send.at[d], c_recv.at[d])
        link.arrived(win.at[p], w_send.at[d], w_recv.at[d])
    for copy in here[7:] + moved[1:]:
        copy.wait()
    arrived(at(2, 1), low, 12)
    arrived(at(2, 1), high, 13)
    link.finish()


def add_products(slots, listed, tiles, source, target, acc, dims):
    total = listed[6, 0]

    @pl.loop(0, (total + (LONG - 1)) // LONG)
    def _(c):
        made = []
        for u in range(LONG):
            q = c * LONG + u
            k, j = listed[0, q], listed[1, q]
            x = source(j, listed[2, q], listed[3, q])
            x = jnp.where(q < total, x, jnp.zeros_like(x))
            made.append(
                lax.dot_general(x, tiles[j * slots + k], (dims, ((), ())), preferred_element_type=F32)
            )
        for u in range(LONG):
            q = c * LONG + u
            t = target(listed[1, q], listed[2, q], listed[3, q])
            acc[t] = acc[t] + made[u]


def place_products(listed, line, made, acc):
    @pl.loop(0, made.shape[0] // GROUP)
    def _(c):
        for u in range(GROUP):
            t = listed[line, c * GROUP + u]
            acc[t] = acc[t] + made[c * GROUP + u]


def forward_kernel(listed, x_ref, tiles, made, z_ref, acc):
    n = lax.axis_index("node")
    for t in range(acc.shape[0]):
        acc[t] = x_ref[n, :, t * TILE:(t + 1) * TILE].astype(F32)
    place_products(listed, 4, made, acc)
    add_products(
        made.shape[0], listed, tiles,
        lambda j, r, c: x_ref[j, :, lanes(c, TILE)], lambda j, r, c: r, acc, ((1,), (1,)),
    )
    for t in range(acc.shape[0]):
        z_ref[:, t * TILE:(t + 1) * TILE] = acc[t].astype(BF16)


def dense_kernel(
    norm, z_ref, cin, win,
    h_ref, ost, gw_ref,
    zin, hst, gst, gin,
    z_send, z_recv, h_send, h_recv, g_send, g_recv, own_sem,
):
    n, f, _ = around()
    n_feat, rows, span = zin.shape
    channels, inputs = win.shape[2:]
    hidden = n_feat * channels
    link = Sender()
    partners = ring(f, n_feat)
    places = [(n, p) for _, p, _ in partners]
    greet(places)
    zin[f] = z_ref[:, lanes(f, span)]
    met(places)
    for d, p, _ in partners:
        link.push(z_ref.at[:, lanes(p, span)], zin.at[f], z_send.at[d], z_recv.at[d], n, p)
    wt = win[:, 0].reshape(hidden, inputs)
    bias = jnp.sum(win[:, 1].reshape(hidden, inputs).astype(F32), axis=1, keepdims=True)
    cot = cin[...].reshape(hidden, span)
    for d, _, p in partners:
        link.arrived(zin.at[p], z_send.at[d], z_recv.at[d])
    z = zin[...].astype(F32).reshape(n_feat * rows, span).astype(BF16)
    pre = jnp.dot(wt, z, preferred_element_type=F32) + bias
    s = jax.nn.sigmoid(pre)
    g = (cot.astype(F32) * s * (1.0 + pre * (1.0 - s))).astype(BF16)
    h = lax.dot_general(wt, g, (((0,), (0,)), ((), ())), preferred_element_type=F32)
    hst[...] = h.reshape(n_feat, rows, span).astype(BF16)
    for d, p, _ in partners:
        link.push(hst.at[p], h_ref.at[:, lanes(f, span)], h_send.at[d], h_recv.at[d], n, p)
    own_h = pltpu.make_async_copy(hst.at[f], h_ref.at[:, lanes(f, span)], own_sem)
    own_h.start()
    both = jnp.concatenate([z, jnp.ones_like(z)], axis=0)
    sums = lax.dot_general(g, both, (((1,), (1,)), ((), ())), preferred_element_type=F32) * norm
    gst[:, 0] = sums[:, :inputs].astype(BF16).reshape(n_feat, channels, inputs)
    gst[:, 1] = split(sums[:, inputs:]).reshape(n_feat, channels, inputs)
    for d, p, _ in partners:
        link.push(gst.at[p], gin.at[f], g_send.at[d], g_recv.at[d], n, p)
    gin[f] = gst[f]
    ost[...] = (pre * s).astype(BF16).reshape(n_feat, channels, span)
    for d, _, p in partners:
        link.arrived(h_ref.at[:, lanes(p, span)], h_send.at[d], h_recv.at[d])
        link.arrived(gin.at[p], g_send.at[d], g_recv.at[d])
    own_h.wait()
    gw_ref[...] = jnp.sum(gin[...].astype(F32), axis=0)
    link.finish()


def backward_kernel(listed, h_ref, tiles, part_ref, acc):
    n_node = part_ref.shape[0]
    row_tiles = acc.shape[0] // n_node
    acc[...] = jnp.zeros_like(acc)
    add_products(
        tiles.shape[0] // n_node, listed, tiles,
        lambda j, r, c: h_ref[:, lanes(r, TILE)], lambda j, r, c: j * row_tiles + c, acc, ((1,), (0,)),
    )
    for j in range(n_node):
        for t in range(row_tiles):
            part_ref[j, :, t * TILE:(t + 1) * TILE] = acc[j * row_tiles + t].astype(BF16)


def reduce_kernel(
    listed, part_ref, h_ref, tiles, gw_ref, ost,
    fl_in, fr_in, fy_in, made, gw_out, gb_out, out_ref,
    far_in, dl_in, dr_in, hl_in, hr_in, hl_out, hr_out, y_out, r_out, l_out, g_in, g_out, h_tiles,
    send, recv, g_send, g_recv, o_send, o_recv, own_sem,
):
    n, f, at = around()
    n_feat, _, span = ost.shape
    n_node, _, nodes = part_ref.shape
    half = nodes // 2
    right, left, other, far = at(1, 0), at(-1, 0), at(0, 1), at(2, 0)
    x = lax.rem(n, n_node // 2)
    first = at(1 - 2 * lax.rem(x, 2), 0)
    second = at(2 * lax.rem(x, 2) - 1, 0)
    link = Sender()
    partners = ring(f, n_feat)
    places = everyone(n, f, at, partners)
    greet(places)
    met(places)

    def push(src, dst, k, to):
        link.push(src, dst, send.at[k], recv.at[k], to, f)

    def arrived(dst, k):
        link.arrived(dst, send.at[k], recv.at[k])

    def add(*terms):
        total = terms[0].astype(F32)
        for term in terms[1:]:
            total = total + term.astype(F32)
        return total.astype(BF16)

    low, high = pl.ds(0, half), pl.ds(half, half)
    halves = (low, high)
    for i, part in enumerate(halves):
        push(part_ref.at[at(2, 1), :, part], far_in.at[:, part], i, other)
        push(part_ref.at[at(1, 1), :, part], dl_in.at[:, part], 2 + i, right)
        push(part_ref.at[at(-1, 1), :, part], dr_in.at[:, part], 4 + i, left)
    link.push(gw_ref, g_in.at[0], g_send.at[0], g_recv.at[0], first, f)
    own_out = pltpu.make_async_copy(ost.at[f], out_ref.at[:, lanes(f, span)], own_sem)
    own_out.start()
    for d, p, _ in partners:
        link.push(ost.at[p], out_ref.at[:, lanes(f, span)], o_send.at[d], o_recv.at[d], n, p)
    arrived(far_in.at[:, low], 0)
    hl_out[...] = add(part_ref[far, :, low], far_in[:, low])
    push(hl_out, hl_in, 6, right)
    arrived(far_in.at[:, high], 1)
    hr_out[...] = add(part_ref[far, :, high], far_in[:, high])
    push(hr_out, hr_in, 7, left)
    push(part_ref.at[right, :, high], fl_in.at[:, high], 8, right)
    push(part_ref.at[left, :, low], fr_in.at[:, low], 9, left)
    link.arrived(g_in.at[0], g_send.at[0], g_recv.at[0])
    g_out[0] = gw_ref[...] + g_in[0]
    link.push(g_out.at[0], g_in.at[1], g_send.at[1], g_recv.at[1], second, f)
    for i, part in enumerate(halves):
        arrived(dl_in.at[:, part], 2 + i)
        arrived(dr_in.at[:, part], 4 + i)
        y_out[:, part] = add(part_ref[other, :, part], dl_in[:, part], dr_in[:, part])
        push(y_out.at[:, part], fy_in.at[:, part], 10 + i, other)
    link.arrived(g_in.at[1], g_send.at[1], g_recv.at[1])
    g_out[1] = g_out[0] + g_in[1]
    link.push(g_out.at[1], g_in.at[2], g_send.at[2], g_recv.at[2], other, f)
    arrived(hl_in, 6)
    r_out[...] = add(part_ref[right, :, low], hl_in[...])
    push(r_out, fl_in.at[:, low], 12, right)
    arrived(hr_in, 7)
    l_out[...] = add(part_ref[left, :, high], hr_in[...])
    push(l_out, fr_in.at[:, high], 13, left)
    by_tile(h_ref, h_tiles)
    own_products(lambda k: listed[4, k], h_tiles, tiles, n, made, ((1,), (0,)))
    link.arrived(g_in.at[2], g_send.at[2], g_recv.at[2])
    total = g_out[1] + g_in[2]
    gw_out[...] = total[0]
    gb_out[...] = jnp.sum(total[1].T, axis=0, keepdims=True)
    for i, part in enumerate(halves):
        arrived(fy_in.at[:, part], 10 + i)
    arrived(fl_in.at[:, high], 8)
    arrived(fr_in.at[:, low], 9)
    arrived(fl_in.at[:, low], 12)
    arrived(fr_in.at[:, high], 13)
    for d, _, p in partners:
        link.arrived(out_ref.at[:, lanes(p, span)], o_send.at[d], o_recv.at[d])
    own_out.wait()
    link.finish()


def final_kernel(
    listed, h_ref, fl, fr, fy, made, gw_ref, gb_ref, made_out,
    gf_ref, gw_out, gb_out, out_ref, acc, out_sem,
):
    moved = pltpu.make_async_copy(made_out, out_ref, out_sem)
    moved.start()
    for t in range(acc.shape[0]):
        span = slice(t * TILE, (t + 1) * TILE)
        acc[t] = (
            h_ref[:, span].astype(F32) + fl[:, span].astype(F32)
            + fr[:, span].astype(F32) + fy[:, span].astype(F32)
        )
    place_products(listed, 5, made, acc)
    for t in range(acc.shape[0]):
        gf_ref[:, t * TILE:(t + 1) * TILE] = acc[t].astype(BF16)
    gw_out[...] = gw_ref[...]
    gb_out[...] = gb_ref[...]
    moved.wait()


def local(features, weight, bias, tile_values, tile_rows, tile_cols, tile_count, cotangent):
    n_node, n_feat = lax.axis_size("node"), lax.axis_size("feat")
    rows, nodes = features.shape
    inputs, channels = weight.shape
    row_tiles = nodes // TILE
    span = row_tiles // n_feat * TILE
    slots = tile_rows.shape[2]
    dma = pltpu.SemaphoreType.DMA
    in_vmem = pl.BlockSpec(memory_space=VMEM)
    in_smem = pl.BlockSpec(memory_space=pltpu.SMEM)
    in_hbm = pl.BlockSpec(memory_space=pltpu.HBM)
    shape = jax.ShapeDtypeStruct
    block = (rows, nodes)
    pair = (2, channels, inputs)

    def params(mib, **more):
        return pltpu.CompilerParams(vmem_limit_bytes=mib << 20, **more)

    def keep(x):
        return pltpu.with_memory_space_constraint(x, pltpu.HBM)

    def pairs(k):
        return [dma((n_feat,))] * k

    x_all, tiles, made, cin, win, listed = pl.pallas_call(
        gather_kernel,
        out_shape=(
            shape((n_node,) + block, BF16),
            shape((n_node * slots, TILE, TILE), BF16),
            shape((slots, rows, TILE), F32),
            shape((n_feat, channels, span), BF16),
            shape((n_feat,) + pair, BF16),
            shape((8, n_node * slots), jnp.int32),
        ),
        in_specs=[in_hbm] * 8,
        out_specs=(in_vmem,) * 6,
        scratch_shapes=[
            VMEM(block, BF16), VMEM((row_tiles, rows, TILE), BF16),
            pltpu.SMEM(tile_count.shape, jnp.int32), pltpu.SMEM(tile_cols.shape, jnp.int32),
            VMEM(tile_rows.shape, jnp.int32), VMEM(tile_cols.shape, jnp.int32),
            VMEM((channels, inputs), BF16), VMEM((1, channels), F32), VMEM(pair, BF16),
            dma((9,)), dma((n_node,)), dma((14,)), dma((14,)),
        ] + pairs(4),
        compiler_params=params(20, collective_id=0, has_side_effects=True),
        name="gather",
    )(
        keep(features), keep(tile_values.reshape(n_node * slots, TILE, TILE)), keep(cotangent),
        keep(tile_count), keep(tile_rows), keep(tile_cols),
        keep(weight.T), keep(bias.reshape(1, channels)),
    )

    acc = VMEM((row_tiles, rows, TILE), F32)
    z = pl.pallas_call(
        forward_kernel,
        out_shape=shape(block, BF16),
        in_specs=[in_smem] + [in_vmem] * 3,
        out_specs=in_vmem,
        scratch_shapes=[acc],
        compiler_params=params(16),
        name="forward",
    )(listed, x_all, tiles, made)

    h, ost, gw = pl.pallas_call(
        functools.partial(dense_kernel, 1.0 / float(nodes * n_node) ** 0.5),
        out_shape=(
            shape(block, BF16),
            shape((n_feat, channels, span), BF16),
            shape(pair, F32),
        ),
        in_specs=[in_vmem] * 3,
        out_specs=(in_vmem,) * 3,
        scratch_shapes=[
            VMEM((n_feat, rows, span), BF16),
            VMEM((n_feat, rows, span), BF16),
            VMEM((n_feat,) + pair, BF16),
            VMEM((n_feat,) + pair, BF16),
        ] + pairs(6) + [dma(())],
        compiler_params=params(16, collective_id=1, has_side_effects=True),
        name="dense",
    )(z, cin, win)

    part = pl.pallas_call(
        backward_kernel,
        out_shape=shape((n_node,) + block, BF16),
        in_specs=[in_smem] + [in_vmem] * 2,
        out_specs=in_vmem,
        scratch_shapes=[VMEM((n_node * row_tiles, rows, TILE), F32)],
        compiler_params=params(16),
        name="backward",
    )(listed, h, tiles)

    whole, half = VMEM(block, BF16), VMEM((rows, nodes // 2), BF16)
    fl, fr, fy, made, gwt, gb, out = pl.pallas_call(
        reduce_kernel,
        out_shape=(
            shape(block, BF16),
            shape(block, BF16),
            shape(block, BF16),
            shape((slots, rows, TILE), F32),
            shape((channels, inputs), F32),
            shape((1, channels), F32),
            shape((channels, nodes), BF16),
        ),
        in_specs=[in_smem] + [in_vmem] * 5,
        out_specs=(in_vmem,) * 7,
        scratch_shapes=[whole] * 3 + [half] * 4 + [whole] + [half] * 2 + [
            VMEM((3,) + pair, F32), VMEM((2,) + pair, F32),
            VMEM((row_tiles, rows, TILE), BF16),
            dma((14,)), dma((14,)), dma((3,)), dma((3,)),
        ] + pairs(2) + [dma(())],
        compiler_params=params(16, collective_id=2, has_side_effects=True),
        name="reduce",
    )(listed, part, h, tiles, gw, ost)

    gf, gwt, gb, out = pl.pallas_call(
        final_kernel,
        out_shape=(
            shape(block, BF16),
            shape((channels, inputs), F32),
            shape((1, channels), F32),
            shape((channels, nodes), BF16),
        ),
        in_specs=[in_smem] + [in_vmem] * 8,
        out_specs=(in_vmem,) * 3 + (in_hbm,),
        scratch_shapes=[acc, dma(())],
        compiler_params=params(16),
        name="final",
    )(listed, h, fl, fr, fy, made, gwt, gb, out)
    return out, gf, gwt.T, gb.reshape(channels)


def solution(mesh):
    return jax.shard_map(
        local,
        mesh=mesh,
        in_specs=(
            P("feat", "node"),
            P(None, "feat"),
            P("feat"),
            P("node", None, None, None, None),
            P("node", None, None),
            P("node", None, None),
            P("node", None),
            P("feat", "node"),
        ),
        out_specs=(P("feat", "node"), P("feat", "node"), P(None, "feat"), P("feat")),
        check_vma=False,
    )
```

time: 68.4 us -> 64.4 us (0.942); the launches traced: 67.1 us -> 64.3 us
  Pallas kernels: 65.1 us -> 63.6 us
  local copies, waits for them, and re-layouts: 1.33 us -> 0 us
    pallas_call x1, Pallas kernels: 18.6 us -> 20.9 us  [local(): pl.pallas_call(reduce_kernel, out_shape=(shape(block, BF16), shape(block,...]
    unnamed x4 -> x0, local copies, waits for them, and re-layouts: 1.33 us -> none
    pallas_call x1, Pallas kernels: 3.48 us -> 2.18 us  [local(): pl.pallas_call(forward_kernel, out_shape=shape(block, BF16), in_specs=[in...]
    pallas_call x1, Pallas kernels: 16.8 us -> 15.6 us  [local(): pl.pallas_call(functools.partial(dense_kernel, 1.0 / float(nodes * n_node...]
    pallas_call x1, Pallas kernels: 2.78 us -> 1.76 us  [local(): pl.pallas_call(backward_kernel, out_shape=shape((n_node,) + block, BF16),...]
where the time goes in v4:
time: 64.4 us; the launch traced here: 64.3 us
  Pallas kernels  63.6 us (99%)
  between operations  0.67 us (1%)
    pallas_call x1, Pallas kernels, local(): pl.pallas_call(gather_kernel, out_shape=(shape((n_node,) + block, BF16),...  21 us
    pallas_call x1, Pallas kernels, local(): pl.pallas_call(reduce_kernel, out_shape=(shape(block, BF16), shape(block,...  20.9 us
    pallas_call x1, Pallas kernels, local(): pl.pallas_call(functools.partial(dense_kernel, 1.0 / float(nodes * n_node...  15.6 us
    pallas_call x1, Pallas kernels, local(): pl.pallas_call(forward_kernel, out_shape=shape(block, BF16), in_specs=[in...  2.18 us
    pallas_call x1, Pallas kernels, local(): pl.pallas_call(final_kernel, out_shape=(shape(block, BF16), shape((channe...  2.11 us
    pallas_call x1, Pallas kernels, local(): pl.pallas_call(backward_kernel, out_shape=shape((n_node,) + block, BF16),...  1.76 us

profile of v4, /device:TPU:0, one launch (start us, length us, event | category | flops | bytes accessed | tf_op | source)
XLA Modules:
  0.0 64.3 jit_solution(7974421156924745906)
XLA Ops:
  0.6 21.0 %gather.1 = (bf16[8,8,8192]{2,1,0:T(8,128)(2,1)S(1)}, bf16[384,128,128]{2,1,0:T(8,128)(2,1)S(1)}, f32[48,8,128]{2,1,0:T(8,128)S(1)}, bf16[16,16,512]{2,1,0:T(8,1...) custom-call(bf16[8,8192]{1,0:T(8,128)(2,1)} %x_ref.1, bf16[384,128,128]{2,1,0:T(8,128)(2,1)} %bitcast.5, ...), custom_call_target="tpu_custom_call" | custom-call | tf_op jit(solution)/shard_map/gather/pallas_call | solution.py:459
  21.6 2.2 %forward.1.z_ref = bf16[8,8192]{1,0:T(8,128)(2,1)S(1)} custom-call(s32[8,384]{1,0:T(8,128)S(1)} %get-tuple-element.24.listed, bf16[8,8,8192]{2,1,0:T(8,128)(2,1)S(1)} %get-tuple-element.25.x_ref, bf16[384,128,128]{2,1,0:T(8,128)(2,1)S(1)} %get-tuple-element.26.tiles, f32[48,8,128]{2,1,0:T(8,128)S(1)} %get-tuple-element.27.made), custom_call_target="tpu_custom_call" | custom-call | tf_op jit(solution)/shard_map/forward/pallas_call | solution.py:487
  23.8 15.6 %dense.1 = (bf16[8,8192]{1,0:T(8,128)(2,1)S(1)}, bf16[16,16,512]{2,1,0:T(8,128)(2,1)S(1)}, f32[2,16,128]{2,1,0:T(8,128)S(1)}) custom-call(bf16[8,8192]{1,0:T(8,128)(2,1)S(1)} %forward.1.z_ref, bf16[16,16,512]{2,1,0:T(8,128)(2,1)S(1)} %get-tuple-element.28.cin, bf16[16,2,16,128]{3,2,1,0:T(8,128)(2,1)S(1)} %get-tuple-element.29.win), custom_call_target="tpu_custom_call" | custom-call | tf_op jit(solution)/shard_map/dense/pallas_call | solution.py:497
  39.5 1.8 %backward.1.part_ref = bf16[8,8,8192]{2,1,0:T(8,128)(2,1)S(1)} custom-call(s32[8,384]{1,0:T(8,128)S(1)} %get-tuple-element.24.listed, bf16[8,8192]{1,0:T(8,128)(2,1)S(1)} %get-tuple-element.30.h_ref, bf16[384,128,128]{2,1,0:T(8,128)(2,1)S(1)} %get-tuple-element.26.tiles), custom_call_target="tpu_custom_call" | custom-call | tf_op jit(solution)/shard_map/backward/pallas_call | solution.py:516
  41.2 20.9 %reduce.1 = (bf16[8,8192]{1,0:T(8,128)(2,1)S(1)}, bf16[8,8192]{1,0:T(8,128)(2,1)S(1)}, bf16[8,8192]{1,0:T(8,128)(2,1)S(1)}, f32[48,8,128]{2,1,0:T(8,128)S(1)}, f...) custom-call(s32[8,384]{1,0:T(8,128)S(1)} %get-tuple-element.24.listed, ...), custom_call_target="tpu_custom_call" | custom-call | tf_op jit(solution)/shard_map/reduce/pallas_call | solution.py:527
  62.2 2.1 %final.1 = (bf16[8,8192]{1,0:T(8,128)(2,1)}, f32[16,128]{1,0:T(8,128)}, f32[1,16]{1,0:T(1,128)}, bf16[16,8192]{1,0:T(8,128)(2,1)}) custom-call(s32[8,384]{1,0:T(8,128)S(1)} %get-tuple-element.24.listed, bf16[8,8192]{1,0:T(8,128)(2,1)S(1)} %get-tuple-element.30.h_ref, bf16[8,8192]{1,0:T(8,128)(2,1)S(1)} %get-tuple-element.33.fl, ...), custom_call_target="tpu_custom_call" | custom-call | tf_op jit(solution)/shard_map/final/pallas_call | solution.py:549

commit v5 on v4

--- a/solution.py
+++ b/solution.py
@@ -13,7 +13,7 @@
 F32 = jnp.float32
 TILE = 128
 GROUP = 8
-LONG = 16
+LONG = 32
 
 
 def around():
@@ -103,7 +103,7 @@
             out_ref[k] = lax.dot_general(x, tiles[n * out_ref.shape[0] + k], (dims, ((), ())), preferred_element_type=F32)
 
 
-def slot_list(count, rows, cols, n, n_node, out_ref):
+def slot_list(count, rows, cols, n, n_node, row_tiles, out_ref):
     slots = rows.shape[2]
     width = out_ref.shape[1]
     q = lax.broadcasted_iota(jnp.int32, (slots, width), 1)
@@ -123,6 +123,9 @@
     out_ref[...] = jnp.where(
         lax.broadcasted_iota(jnp.int32, out_ref.shape, 0) == 6, base, total.astype(jnp.int32)
     )
+    whole = total.astype(jnp.int32)
+    out_ref[0:1] = whole[0:1] + whole[1:2] * slots
+    out_ref[7:8] = whole[1:2] * row_tiles + whole[3:4]
     out_ref[4:5, :slots] = rows[0, pl.ds(n, 1)]
     out_ref[5:6, :slots] = cols[0, pl.ds(n, 1)]
 
@@ -200,7 +203,7 @@
     push(other, high, 11, left)
     for copy in here[2:7]:
         copy.wait()
-    slot_list(count, rows_in, cols_in, n, n_node, list_out)
+    slot_list(count, rows_in, cols_in, n, n_node, x_tiles.shape[0], list_out)
     arrived(far, low, 6)
     push(far, low, 12, other)
     arrived(far, high, 7)
@@ -223,7 +226,7 @@
     link.finish()
 
 
-def add_products(slots, listed, tiles, source, target, acc, dims):
+def add_products(listed, line, tiles, source, acc, dims):
     total = listed[6, 0]
 
     @pl.loop(0, (total + (LONG - 1)) // LONG)
@@ -231,15 +234,13 @@
         made = []
         for u in range(LONG):
             q = c * LONG + u
-            k, j = listed[0, q], listed[1, q]
-            x = source(j, listed[2, q], listed[3, q])
+            x = source(q)
             x = jnp.where(q < total, x, jnp.zeros_like(x))
             made.append(
-                lax.dot_general(x, tiles[j * slots + k], (dims, ((), ())), preferred_element_type=F32)
+                lax.dot_general(x, tiles[listed[0, q]], (dims, ((), ())), preferred_element_type=F32)
             )
         for u in range(LONG):
-            q = c * LONG + u
-            t = target(listed[1, q], listed[2, q], listed[3, q])
+            t = listed[line, c * LONG + u]
             acc[t] = acc[t] + made[u]
 
 
@@ -251,14 +252,16 @@
             acc[t] = acc[t] + made[c * GROUP + u]
 
 
-def forward_kernel(listed, x_ref, tiles, made, z_ref, acc):
+def forward_kernel(list_ref, x_ref, tiles, made, z_ref, acc, listed, sem):
+    moved = pltpu.make_async_copy(list_ref, listed, sem)
+    moved.start()
     n = lax.axis_index("node")
     for t in range(acc.shape[0]):
         acc[t] = x_ref[n, :, t * TILE:(t + 1) * TILE].astype(F32)
+    moved.wait()
     place_products(listed, 4, made, acc)
     add_products(
-        made.shape[0], listed, tiles,
-        lambda j, r, c: x_ref[j, :, lanes(c, TILE)], lambda j, r, c: r, acc, ((1,), (1,)),
+        listed, 2, tiles, lambda q: x_ref[listed[1, q], :, lanes(listed[3, q], TILE)], acc, ((1,), (1,))
     )
     for t in range(acc.shape[0]):
         z_ref[:, t * TILE:(t + 1) * TILE] = acc[t].astype(BF16)
@@ -266,9 +269,9 @@
 
 def dense_kernel(
     norm, z_ref, cin, win,
-    h_ref, ost, gw_ref,
-    zin, hst, gst, gin,
-    z_send, z_recv, h_send, h_recv, g_send, g_recv, own_sem,
+    h_ref, ost, gst,
+    zin, hst,
+    z_send, z_recv, h_send, h_recv, own_sem,
 ):
     n, f, _ = around()
     n_feat, rows, span = zin.shape
@@ -285,41 +288,44 @@
     wt = win[:, 0].reshape(hidden, inputs)
     bias = jnp.sum(win[:, 1].reshape(hidden, inputs).astype(F32), axis=1, keepdims=True)
     cot = cin[...].reshape(hidden, span)
+    w = wt.astype(F32).T.astype(BF16)
     for d, _, p in partners:
         link.arrived(zin.at[p], z_send.at[d], z_recv.at[d])
     z = zin[...].astype(F32).reshape(n_feat * rows, span).astype(BF16)
-    pre = jnp.dot(wt, z, preferred_element_type=F32) + bias
-    s = jax.nn.sigmoid(pre)
-    g = (cot.astype(F32) * s * (1.0 + pre * (1.0 - s))).astype(BF16)
-    h = lax.dot_general(wt, g, (((0,), (0,)), ((), ())), preferred_element_type=F32)
-    hst[...] = h.reshape(n_feat, rows, span).astype(BF16)
+    parts = []
+    for t in range(span // TILE):
+        part = slice(t * TILE, (t + 1) * TILE)
+        pre = jnp.dot(wt, z[:, part], preferred_element_type=F32) + bias
+        s = jax.nn.sigmoid(pre)
+        g = (cot[:, part].astype(F32) * s * (1.0 + pre * (1.0 - s))).astype(BF16)
+        h = jnp.dot(w, g, preferred_element_type=F32)
+        hst[:, :, part] = h.reshape(n_feat, rows, TILE).astype(BF16)
+        ost[:, :, part] = (pre * s).astype(BF16).reshape(n_feat, channels, TILE)
+        parts.append(g)
     for d, p, _ in partners:
         link.push(hst.at[p], h_ref.at[:, lanes(f, span)], h_send.at[d], h_recv.at[d], n, p)
     own_h = pltpu.make_async_copy(hst.at[f], h_ref.at[:, lanes(f, span)], own_sem)
     own_h.start()
+    g = jnp.concatenate(parts, axis=1)
     both = jnp.concatenate([z, jnp.ones_like(z)], axis=0)
     sums = lax.dot_general(g, both, (((1,), (1,)), ((), ())), preferred_element_type=F32) * norm
     gst[:, 0] = sums[:, :inputs].astype(BF16).reshape(n_feat, channels, inputs)
     gst[:, 1] = split(sums[:, inputs:]).reshape(n_feat, channels, inputs)
-    for d, p, _ in partners:
-        link.push(gst.at[p], gin.at[f], g_send.at[d], g_recv.at[d], n, p)
-    gin[f] = gst[f]
-    ost[...] = (pre * s).astype(BF16).reshape(n_feat, channels, span)
     for d, _, p in partners:
         link.arrived(h_ref.at[:, lanes(p, span)], h_send.at[d], h_recv.at[d])
-        link.arrived(gin.at[p], g_send.at[d], g_recv.at[d])
     own_h.wait()
-    gw_ref[...] = jnp.sum(gin[...].astype(F32), axis=0)
     link.finish()
 
 
-def backward_kernel(listed, h_ref, tiles, part_ref, acc):
+def backward_kernel(list_ref, h_ref, tiles, part_ref, acc, listed, sem):
+    moved = pltpu.make_async_copy(list_ref, listed, sem)
+    moved.start()
     n_node = part_ref.shape[0]
     row_tiles = acc.shape[0] // n_node
     acc[...] = jnp.zeros_like(acc)
+    moved.wait()
     add_products(
-        tiles.shape[0] // n_node, listed, tiles,
-        lambda j, r, c: h_ref[:, lanes(r, TILE)], lambda j, r, c: j * row_tiles + c, acc, ((1,), (0,)),
+        listed, 7, tiles, lambda q: h_ref[:, lanes(listed[2, q], TILE)], acc, ((1,), (0,))
     )
     for j in range(n_node):
         for t in range(row_tiles):
@@ -327,22 +333,19 @@
 
 
 def reduce_kernel(
-    listed, part_ref, h_ref, tiles, gw_ref, ost,
+    listed, part_ref, h_ref, tiles, gst, ost,
     fl_in, fr_in, fy_in, made, gw_out, gb_out, out_ref,
-    far_in, dl_in, dr_in, hl_in, hr_in, hl_out, hr_out, y_out, r_out, l_out, g_in, g_out, h_tiles,
-    send, recv, g_send, g_recv, o_send, o_recv, own_sem,
+    far_in, dl_in, dr_in, hl_in, hr_in, hl_out, hr_out, y_out, r_out, l_out, gin, sums, h_tiles,
+    send, recv, s_send, s_recv, g_send, g_recv, o_send, o_recv, own_sem,
 ):
     n, f, at = around()
     n_feat, _, span = ost.shape
     n_node, _, nodes = part_ref.shape
     half = nodes // 2
     right, left, other, far = at(1, 0), at(-1, 0), at(0, 1), at(2, 0)
-    x = lax.rem(n, n_node // 2)
-    first = at(1 - 2 * lax.rem(x, 2), 0)
-    second = at(2 * lax.rem(x, 2) - 1, 0)
     link = Sender()
     partners = ring(f, n_feat)
-    places = everyone(n, f, at, partners)
+    places = [(lax.rem(n + d, n_node), f) for d in range(1, n_node)] + [(n, p) for _, p, _ in partners]
     greet(places)
     met(places)
 
@@ -364,7 +367,9 @@
         push(part_ref.at[at(2, 1), :, part], far_in.at[:, part], i, other)
         push(part_ref.at[at(1, 1), :, part], dl_in.at[:, part], 2 + i, right)
         push(part_ref.at[at(-1, 1), :, part], dr_in.at[:, part], 4 + i, left)
-    link.push(gw_ref, g_in.at[0], g_send.at[0], g_recv.at[0], first, f)
+    for d, p, _ in partners:
+        link.push(gst.at[p], gin.at[f], g_send.at[d], g_recv.at[d], n, p)
+    gin[f] = gst[f]
     own_out = pltpu.make_async_copy(ost.at[f], out_ref.at[:, lanes(f, span)], own_sem)
     own_out.start()
     for d, p, _ in partners:
@@ -377,27 +382,27 @@
     push(hr_out, hr_in, 7, left)
     push(part_ref.at[right, :, high], fl_in.at[:, high], 8, right)
     push(part_ref.at[left, :, low], fr_in.at[:, low], 9, left)
-    link.arrived(g_in.at[0], g_send.at[0], g_recv.at[0])
-    g_out[0] = gw_ref[...] + g_in[0]
-    link.push(g_out.at[0], g_in.at[1], g_send.at[1], g_recv.at[1], second, f)
     for i, part in enumerate(halves):
         arrived(dl_in.at[:, part], 2 + i)
         arrived(dr_in.at[:, part], 4 + i)
         y_out[:, part] = add(part_ref[other, :, part], dl_in[:, part], dr_in[:, part])
         push(y_out.at[:, part], fy_in.at[:, part], 10 + i, other)
-    link.arrived(g_in.at[1], g_send.at[1], g_recv.at[1])
-    g_out[1] = g_out[0] + g_in[1]
-    link.push(g_out.at[1], g_in.at[2], g_send.at[2], g_recv.at[2], other, f)
     arrived(hl_in, 6)
     r_out[...] = add(part_ref[right, :, low], hl_in[...])
     push(r_out, fl_in.at[:, low], 12, right)
     arrived(hr_in, 7)
     l_out[...] = add(part_ref[left, :, high], hr_in[...])
     push(l_out, fr_in.at[:, high], 13, left)
+    for d, _, p in partners:
+        link.arrived(gin.at[p], g_send.at[d], g_recv.at[d])
+    sums[n] = jnp.sum(gin[...].astype(F32), axis=0)
+    for d in range(1, n_node):
+        link.push(sums.at[n], sums.at[n], s_send.at[d], s_recv.at[d], lax.rem(n + d, n_node), f)
     by_tile(h_ref, h_tiles)
     own_products(lambda k: listed[4, k], h_tiles, tiles, n, made, ((1,), (0,)))
-    link.arrived(g_in.at[2], g_send.at[2], g_recv.at[2])
-    total = g_out[1] + g_in[2]
+    for d in range(1, n_node):
+        link.arrived(sums.at[lax.rem(n - d + n_node, n_node)], s_send.at[d], s_recv.at[d])
+    total = jnp.sum(sums[...], axis=0)
     gw_out[...] = total[0]
     gb_out[...] = jnp.sum(total[1].T, axis=0, keepdims=True)
     for i, part in enumerate(halves):
@@ -413,9 +418,11 @@
 
 
 def final_kernel(
-    listed, h_ref, fl, fr, fy, made, gw_ref, gb_ref, made_out,
-    gf_ref, gw_out, gb_out, out_ref, acc, out_sem,
+    list_ref, h_ref, fl, fr, fy, made, gw_ref, gb_ref, made_out,
+    gf_ref, gw_out, gb_out, out_ref, acc, listed, sem, out_sem,
 ):
+    scalars = pltpu.make_async_copy(list_ref, listed, sem)
+    scalars.start()
     moved = pltpu.make_async_copy(made_out, out_ref, out_sem)
     moved.start()
     for t in range(acc.shape[0]):
@@ -424,6 +431,7 @@
             h_ref[:, span].astype(F32) + fl[:, span].astype(F32)
             + fr[:, span].astype(F32) + fy[:, span].astype(F32)
         )
+    scalars.wait()
     place_products(listed, 5, made, acc)
     for t in range(acc.shape[0]):
         gf_ref[:, t * TILE:(t + 1) * TILE] = acc[t].astype(BF16)
@@ -484,31 +492,30 @@
     )
 
     acc = VMEM((row_tiles, rows, TILE), F32)
+    scalars = [pltpu.SMEM((8, n_node * slots), jnp.int32), dma(())]
     z = pl.pallas_call(
         forward_kernel,
         out_shape=shape(block, BF16),
-        in_specs=[in_smem] + [in_vmem] * 3,
+        in_specs=[in_vmem] * 4,
         out_specs=in_vmem,
-        scratch_shapes=[acc],
+        scratch_shapes=[acc] + scalars,
         compiler_params=params(16),
         name="forward",
     )(listed, x_all, tiles, made)
 
-    h, ost, gw = pl.pallas_call(
+    h, ost, gst = pl.pallas_call(
         functools.partial(dense_kernel, 1.0 / float(nodes * n_node) ** 0.5),
         out_shape=(
             shape(block, BF16),
             shape((n_feat, channels, span), BF16),
-            shape(pair, F32),
+            shape((n_feat,) + pair, BF16),
         ),
         in_specs=[in_vmem] * 3,
         out_specs=(in_vmem,) * 3,
         scratch_shapes=[
             VMEM((n_feat, rows, span), BF16),
             VMEM((n_feat, rows, span), BF16),
-            VMEM((n_feat,) + pair, BF16),
-            VMEM((n_feat,) + pair, BF16),
-        ] + pairs(6) + [dma(())],
+        ] + pairs(4) + [dma(())],
         compiler_params=params(16, collective_id=1, has_side_effects=True),
         name="dense",
     )(z, cin, win)
@@ -516,9 +523,9 @@
     part = pl.pallas_call(
         backward_kernel,
         out_shape=shape((n_node,) + block, BF16),
-        in_specs=[in_smem] + [in_vmem] * 2,
+        in_specs=[in_vmem] * 3,
         out_specs=in_vmem,
-        scratch_shapes=[VMEM((n_node * row_tiles, rows, TILE), F32)],
+        scratch_shapes=[VMEM((n_node * row_tiles, rows, TILE), F32)] + scalars,
         compiler_params=params(16),
         name="backward",
     )(listed, h, tiles)
@@ -538,13 +545,13 @@
         in_specs=[in_smem] + [in_vmem] * 5,
         out_specs=(in_vmem,) * 7,
         scratch_shapes=[whole] * 3 + [half] * 4 + [whole] + [half] * 2 + [
-            VMEM((3,) + pair, F32), VMEM((2,) + pair, F32),
+            VMEM((n_feat,) + pair, BF16), VMEM((n_node,) + pair, F32),
             VMEM((row_tiles, rows, TILE), BF16),
-            dma((14,)), dma((14,)), dma((3,)), dma((3,)),
-        ] + pairs(2) + [dma(())],
+            dma((14,)), dma((14,)), dma((n_node,)), dma((n_node,)),
+        ] + pairs(4) + [dma(())],
         compiler_params=params(16, collective_id=2, has_side_effects=True),
         name="reduce",
-    )(listed, part, h, tiles, gw, ost)
+    )(listed, part, h, tiles, gst, ost)
 
     gf, gwt, gb, out = pl.pallas_call(
         final_kernel,
@@ -554,9 +561,9 @@
             shape((1, channels), F32),
             shape((channels, nodes), BF16),
         ),
-        in_specs=[in_smem] + [in_vmem] * 8,
+        in_specs=[in_vmem] * 9,
         out_specs=(in_vmem,) * 3 + (in_hbm,),
-        scratch_shapes=[acc, dma(())],
+        scratch_shapes=[acc] + scalars + [dma(())],
         compiler_params=params(16),
         name="final",
     )(listed, h, fl, fr, fy, made, gwt, gb, out)

time: 64.4 us -> 60.9 us (0.946)
  Pallas kernels: 63.6 us -> 60.1 us
    pallas_call x1, Pallas kernels: 20.9 us -> 19.4 us  [local(): pl.pallas_call(reduce_kernel, out_shape=(shape(block, BF16), shape(block,...]
    pallas_call x1, Pallas kernels: 15.6 us -> 14.1 us  [local(): pl.pallas_call(functools.partial(dense_kernel, 1.0 / float(nodes * n_node...]
where the time goes in v5:
time: 60.9 us; the launch traced here: 60.8 us
  Pallas kernels  60.1 us (99%)
  between operations  0.67 us (1%)
    pallas_call x1, Pallas kernels, local(): pl.pallas_call(gather_kernel, out_shape=(shape((n_node,) + block, BF16),...  21 us
    pallas_call x1, Pallas kernels, local(): pl.pallas_call(reduce_kernel, out_shape=(shape(block, BF16), shape(block,...  19.4 us
    pallas_call x1, Pallas kernels, local(): pl.pallas_call(functools.partial(dense_kernel, 1.0 / float(nodes * n_node...  14.1 us
    pallas_call x1, Pallas kernels, local(): pl.pallas_call(forward_kernel, out_shape=shape(block, BF16), in_specs=[in...  2.32 us
    pallas_call x1, Pallas kernels, local(): pl.pallas_call(backward_kernel, out_shape=shape((n_node,) + block, BF16),...  1.66 us
    pallas_call x1, Pallas kernels, local(): pl.pallas_call(final_kernel, out_shape=(shape(block, BF16), shape((channe...  1.63 us

profile of v5, /device:TPU:0, one launch (start us, length us, event | category | flops | bytes accessed | tf_op | source)
XLA Modules:
  0.0 60.8 jit_solution(5568545812030210818)
XLA Ops:
  0.6 21.0 %gather.1 = (bf16[8,8,8192]{2,1,0:T(8,128)(2,1)S(1)}, bf16[384,128,128]{2,1,0:T(8,128)(2,1)S(1)}, f32[48,8,128]{2,1,0:T(8,128)S(1)}, bf16[16,16,512]{2,1,0:T(8,1...) custom-call(bf16[8,8192]{1,0:T(8,128)(2,1)} %x_ref.1, bf16[384,128,128]{2,1,0:T(8,128)(2,1)} %bitcast.5, ...), custom_call_target="tpu_custom_call" | custom-call | tf_op jit(solution)/shard_map/gather/pallas_call | solution.py:467
  21.6 2.3 %forward.1.z_ref = bf16[8,8192]{1,0:T(8,128)(2,1)S(1)} custom-call(s32[8,384]{1,0:T(8,128)S(1)} %get-tuple-element.24.list_ref.listed, bf16[8,8,8192]{2,1,0:T(8,128)(2,1)S(1)} %get-tuple-element.25.x_ref, bf16[384,128,128]{2,1,0:T(8,128)(2,1)S(1)} %get-tuple-element.26.tiles, f32[48,8,128]{2,1,0:T(8,128)S(1)} %get-tuple-element.27.made), custom_call_target="tpu_custom_call" | custom-call | tf_op jit(solution)/shard_map/forward/pallas_call | solution.py:496
  24.0 14.1 %dense.1 = (bf16[8,8192]{1,0:T(8,128)(2,1)S(1)}, bf16[16,16,512]{2,1,0:T(8,128)(2,1)S(1)}, bf16[16,2,16,128]{3,2,1,0:T(8,128)(2,1)S(1)}) custom-call(bf16[8,8192]{1,0:T(8,128)(2,1)S(1)} %forward.1.z_ref, bf16[16,16,512]{2,1,0:T(8,128)(2,1)S(1)} %get-tuple-element.28.cin, bf16[16,2,16,128]{3,2,1,0:T(8,128)(2,1)S(1)} %get-tuple-element.29.win), custom_call_target="tpu_custom_call" | custom-call | tf_op jit(solution)/shard_map/dense/pallas_call | solution.py:506
  38.1 1.7 %backward.1.part_ref = bf16[8,8,8192]{2,1,0:T(8,128)(2,1)S(1)} custom-call(s32[8,384]{1,0:T(8,128)S(1)} %get-tuple-element.24.list_ref.listed, bf16[8,8192]{1,0:T(8,128)(2,1)S(1)} %get-tuple-element.30.h_ref, bf16[384,128,128]{2,1,0:T(8,128)(2,1)S(1)} %get-tuple-element.26.tiles), custom_call_target="tpu_custom_call" | custom-call | tf_op jit(solution)/shard_map/backward/pallas_call | solution.py:523
  39.7 19.4 %reduce.1 = (bf16[8,8192]{1,0:T(8,128)(2,1)S(1)}, bf16[8,8192]{1,0:T(8,128)(2,1)S(1)}, bf16[8,8192]{1,0:T(8,128)(2,1)S(1)}, f32[48,8,128]{2,1,0:T(8,128)S(1)}, f...) custom-call(s32[8,384]{1,0:T(8,128)S(1)} %get-tuple-element.24.list_ref.listed, ...), custom_call_target="tpu_custom_call" | custom-call | tf_op jit(solution)/shard_map/reduce/pallas_call | solution.py:534
  59.1 1.6 %final.1 = (bf16[8,8192]{1,0:T(8,128)(2,1)}, f32[16,128]{1,0:T(8,128)}, f32[1,16]{1,0:T(1,128)}, bf16[16,8192]{1,0:T(8,128)(2,1)}) custom-call(s32[8,384]{1,0:T(8,128)S(1)} %get-tuple-element.24.list_ref.listed, bf16[8,8192]{1,0:T(8,128)(2,1)S(1)} %get-tuple-element.30.h_ref, bf16[8,8192]{1,0:T(8,128)(2,1)S(1)} %get-tuple-element.33.fl, ...), custom_call_target="tpu_custom_call" | custom-call | tf_op jit(solution)/shard_map/final/pallas_call | solution.py:556

commit v6 on v5

--- a/solution.py
+++ b/solution.py
@@ -12,7 +12,7 @@
 BF16 = jnp.bfloat16
 F32 = jnp.float32
 TILE = 128
-GROUP = 8
+GROUP = 48
 LONG = 32
 
 
@@ -89,18 +89,31 @@
     return jnp.where(lane == 0, high, rest).astype(BF16)
 
 
-def by_tile(x_ref, out_ref):
-    for t in range(out_ref.shape[0]):
-        out_ref[t] = x_ref[:, t * TILE:(t + 1) * TILE]
-
-
-def own_products(index, x_ref, tiles, n, out_ref, dims):
+def by_tile(x_ref, upper, lower):
+    rows = x_ref.shape[0]
+    none = jnp.zeros((rows, TILE), F32)
+    for t in range(upper.shape[0]):
+        x = x_ref[:, t * TILE:(t + 1) * TILE].astype(F32)
+        upper[t] = jnp.concatenate([x, none], axis=0).astype(BF16)
+        lower[t] = jnp.concatenate([none, x], axis=0).astype(BF16)
+
+
+def two(x, y, a, b, across):
+    pair = jnp.concatenate([x, y], axis=1)
+    both = jnp.concatenate([a, b], axis=across)
+    return lax.dot_general(pair, both, (((1,), (across,)), ((), ())), preferred_element_type=F32)
+
+
+def own_products(index, upper, lower, tiles, first, out_ref):
+    rows = out_ref.shape[1]
+
     @pl.loop(0, out_ref.shape[0] // GROUP)
     def _(c):
-        for u in range(GROUP):
+        for u in range(0, GROUP, 2):
             k = c * GROUP + u
-            x = x_ref[index(k)]
-            out_ref[k] = lax.dot_general(x, tiles[n * out_ref.shape[0] + k], (dims, ((), ())), preferred_element_type=F32)
+            made = two(upper[index(k)], lower[index(k + 1)], tiles[first + k], tiles[first + k + 1], 0)
+            out_ref[k] = made[:rows]
+            out_ref[k + 1] = made[rows:]
 
 
 def slot_list(count, rows, cols, n, n_node, row_tiles, out_ref):
@@ -130,33 +143,68 @@
     out_ref[5:6, :slots] = cols[0, pl.ds(n, 1)]
 
 
-def gather_kernel(
-    x_ref, tiles_ref, cot_ref, count_ref, rows_ref, cols_ref, wt_ref, bias_ref,
-    all_ref, tiles, made, cin, win, list_out,
-    x_own, x_tiles, count, cols, rows_in, cols_in, wt, bias_in, wst,
-    local_sem, tile_sem, send, recv, c_send, c_recv, w_send, w_recv,
+def products(x_ref, upper, lower, cols, j, tiles, out_ref):
+    by_tile(x_ref, upper, lower)
+    rows = x_ref.shape[0]
+    slots = out_ref.shape[0] // rows
+
+    @pl.loop(0, slots // GROUP)
+    def _(c):
+        for u in range(0, GROUP, 2):
+            k = c * GROUP + u
+            out_ref[pl.ds(pl.multiple_of(k * rows, rows), 2 * rows)] = two(
+                upper[cols[0, j, k]], lower[cols[0, j, k + 1]],
+                tiles[j * slots + k], tiles[j * slots + k + 1], 1,
+            )
+
+
+def sum_rows(count, rows_in, j, made, z_ref):
+    slots = rows_in.shape[2]
+    rows = made.shape[0] // slots
+    row_tiles = z_ref.shape[0] // rows
+    t = lax.broadcasted_iota(jnp.int32, (row_tiles, slots), 0)
+    k = lax.broadcasted_iota(jnp.int32, (row_tiles, slots), 1)
+    hit = jnp.where((t == rows_in[0, pl.ds(j, 1)]) & (k < count[0, j]), 1.0, 0.0).astype(BF16)
+    for c in range(rows):
+        part = made[pl.ds(c, slots, stride=rows), :]
+        high = part.astype(BF16)
+        low = (part - high.astype(F32)).astype(BF16)
+        where = pl.ds(c, row_tiles, stride=rows)
+        z_ref[where, :] = z_ref[where, :] + (
+            jnp.dot(hit, high, preferred_element_type=F32) + jnp.dot(hit, low, preferred_element_type=F32)
+        )
+
+
+def forward_kernel(
+    norm, x_ref, tiles_ref, cot_ref, count_ref, rows_ref, cols_ref, wt_ref, bias_ref,
+    tiles, list_out, h_ref, ost, gst,
+    x_all, x_own, upper, lower, made, z_sum, z_ref, zin, hst, cin, win,
+    count, cols, rows_in, cols_in, wt_in, bias_in, wst,
+    local_sem, tile_sem, own_sem, send, recv, c_send, c_recv, w_send, w_recv, z_send, z_recv, h_send, h_recv,
 ):
     n, f, at = around()
     n_feat, channels, span = cin.shape
+    rows = x_ref.shape[0]
     inputs = wt_ref.shape[1]
+    hidden = n_feat * channels
     n_node = count_ref.shape[1]
-    slots = made.shape[0]
+    slots = tiles.shape[0] // n_node
     half = x_ref.shape[1] // 2
     right, left, other, far = at(1, 0), at(-1, 0), at(0, 1), at(2, 0)
+    order = [n, left, right, other, far, at(-1, 1), at(1, 1), at(2, 1)]
     link = Sender()
     here = [
         pltpu.make_async_copy(src, dst, local_sem.at[i])
         for i, (src, dst) in enumerate([
-            (wt_ref, wt), (bias_ref, bias_in), (count_ref, count), (rows_ref, rows_in), (cols_ref, cols_in),
-            (cols_ref, cols), (x_ref, x_own),
-            (x_ref, all_ref.at[n]), (cot_ref.at[:, lanes(f, span)], cin.at[f]),
+            (wt_ref, wt_in), (bias_ref, bias_in), (count_ref, count), (rows_ref, rows_in), (cols_ref, cols_in),
+            (cols_ref, cols), (x_ref, x_own), (cot_ref.at[:, lanes(f, span)], cin.at[f]),
         ])
     ]
     moved = [
         pltpu.make_async_copy(
             tiles_ref.at[pl.ds(j * slots, slots)], tiles.at[pl.ds(j * slots, slots)], tile_sem.at[s]
         )
-        for s, j in enumerate([n] + [lax.rem(n + s, n_node) for s in range(1, n_node)])
+        for s, j in enumerate(order)
     ]
     partners = ring(f, n_feat)
     places = everyone(n, f, at, partners)
@@ -168,11 +216,16 @@
     low, high = pl.ds(0, half), pl.ds(half, half)
 
     def push(m, part, k, to, src=None):
-        block = all_ref.at[m, :, part]
+        block = x_all.at[m, :, part]
         link.push(block if src is None else src.at[:, part], block, send.at[k], recv.at[k], to, f)
 
     def arrived(m, part, k):
-        link.arrived(all_ref.at[m, :, part], send.at[k], recv.at[k])
+        link.arrived(x_all.at[m, :, part], send.at[k], recv.at[k])
+
+    def work(s):
+        moved[s].wait()
+        products(x_own if s == 0 else x_all.at[order[s]], upper, lower, cols, order[s], tiles, made)
+        sum_rows(count, rows_in, order[s], made, z_sum)
 
     push(n, low, 0, right, x_ref)
     push(n, high, 1, left, x_ref)
@@ -184,13 +237,18 @@
         link.push(cot_ref.at[:, lanes(p, span)], cin.at[f], c_send.at[d], c_recv.at[d], n, p)
     for copy in here[:2]:
         copy.wait()
-    wst[0] = wt[...]
+    wst[0] = wt_in[...]
     wst[1] = split(jnp.broadcast_to(bias_in[...], (inputs, channels)).T)
     win[f] = wst[...]
     for d, p, _ in partners:
         link.push(wst, win.at[f], w_send.at[d], w_recv.at[d], n, p)
     for copy in moved:
         copy.start()
+    for copy in here[2:]:
+        copy.wait()
+    for t in range(upper.shape[0]):
+        z_sum[t * rows:(t + 1) * rows] = x_own[:, t * TILE:(t + 1) * TILE].astype(F32)
+    work(0)
     arrived(left, low, 0)
     push(left, low, 6, right)
     arrived(right, high, 1)
@@ -201,90 +259,34 @@
     arrived(other, high, 5)
     push(other, high, 10, right)
     push(other, high, 11, left)
-    for copy in here[2:7]:
-        copy.wait()
-    slot_list(count, rows_in, cols_in, n, n_node, x_tiles.shape[0], list_out)
+    arrived(left, high, 3)
+    work(1)
     arrived(far, low, 6)
     push(far, low, 12, other)
     arrived(far, high, 7)
     push(far, high, 13, other)
-    moved[0].wait()
-    by_tile(x_own, x_tiles)
-    own_products(lambda k: cols[0, n, k], x_tiles, tiles, n, made, ((1,), (1,)))
-    arrived(left, high, 3)
     arrived(right, low, 4)
-    for m, k in ((at(-1, 1), 0), (at(1, 1), 1)):
-        arrived(m, low, 8 + k)
-        arrived(m, high, 10 + k)
+    work(2)
+    work(3)
+    work(4)
+    arrived(at(-1, 1), low, 8)
+    arrived(at(-1, 1), high, 10)
+    work(5)
+    arrived(at(1, 1), low, 9)
+    arrived(at(1, 1), high, 11)
+    work(6)
+    arrived(at(2, 1), low, 12)
+    arrived(at(2, 1), high, 13)
+    work(7)
+    for t in range(upper.shape[0]):
+        z_ref[:, t * TILE:(t + 1) * TILE] = z_sum[t * rows:(t + 1) * rows].astype(BF16)
+    for d, p, _ in partners:
+        link.push(z_ref.at[:, lanes(p, span)], zin.at[f], z_send.at[d], z_recv.at[d], n, p)
+    zin[f] = z_ref[:, lanes(f, span)]
+    slot_list(count, rows_in, cols_in, n, n_node, upper.shape[0], list_out)
     for d, _, p in partners:
         link.arrived(cin.at[p], c_send.at[d], c_recv.at[d])
         link.arrived(win.at[p], w_send.at[d], w_recv.at[d])
-    for copy in here[7:] + moved[1:]:
-        copy.wait()
-    arrived(at(2, 1), low, 12)
-    arrived(at(2, 1), high, 13)
-    link.finish()
-
-
-def add_products(listed, line, tiles, source, acc, dims):
-    total = listed[6, 0]
-
-    @pl.loop(0, (total + (LONG - 1)) // LONG)
-    def _(c):
-        made = []
-        for u in range(LONG):
-            q = c * LONG + u
-            x = source(q)
-            x = jnp.where(q < total, x, jnp.zeros_like(x))
-            made.append(
-                lax.dot_general(x, tiles[listed[0, q]], (dims, ((), ())), preferred_element_type=F32)
-            )
-        for u in range(LONG):
-            t = listed[line, c * LONG + u]
-            acc[t] = acc[t] + made[u]
-
-
-def place_products(listed, line, made, acc):
-    @pl.loop(0, made.shape[0] // GROUP)
-    def _(c):
-        for u in range(GROUP):
-            t = listed[line, c * GROUP + u]
-            acc[t] = acc[t] + made[c * GROUP + u]
-
-
-def forward_kernel(list_ref, x_ref, tiles, made, z_ref, acc, listed, sem):
-    moved = pltpu.make_async_copy(list_ref, listed, sem)
-    moved.start()
-    n = lax.axis_index("node")
-    for t in range(acc.shape[0]):
-        acc[t] = x_ref[n, :, t * TILE:(t + 1) * TILE].astype(F32)
-    moved.wait()
-    place_products(listed, 4, made, acc)
-    add_products(
-        listed, 2, tiles, lambda q: x_ref[listed[1, q], :, lanes(listed[3, q], TILE)], acc, ((1,), (1,))
-    )
-    for t in range(acc.shape[0]):
-        z_ref[:, t * TILE:(t + 1) * TILE] = acc[t].astype(BF16)
-
-
-def dense_kernel(
-    norm, z_ref, cin, win,
-    h_ref, ost, gst,
-    zin, hst,
-    z_send, z_recv, h_send, h_recv, own_sem,
-):
-    n, f, _ = around()
-    n_feat, rows, span = zin.shape
-    channels, inputs = win.shape[2:]
-    hidden = n_feat * channels
-    link = Sender()
-    partners = ring(f, n_feat)
-    places = [(n, p) for _, p, _ in partners]
-    greet(places)
-    zin[f] = z_ref[:, lanes(f, span)]
-    met(places)
-    for d, p, _ in partners:
-        link.push(z_ref.at[:, lanes(p, span)], zin.at[f], z_send.at[d], z_recv.at[d], n, p)
     wt = win[:, 0].reshape(hidden, inputs)
     bias = jnp.sum(win[:, 1].reshape(hidden, inputs).astype(F32), axis=1, keepdims=True)
     cot = cin[...].reshape(hidden, span)
@@ -317,16 +319,45 @@
     link.finish()
 
 
-def backward_kernel(list_ref, h_ref, tiles, part_ref, acc, listed, sem):
+def add_products(listed, source, target, upper, lower, tiles, acc):
+    total = listed[6, 0]
+    rows = acc.shape[1]
+
+    def used(x, q):
+        return jnp.where(q < total, x, jnp.zeros_like(x))
+
+    @pl.loop(0, (total + (LONG - 1)) // LONG)
+    def _(c):
+        made = []
+        for u in range(0, LONG, 2):
+            q = c * LONG + u
+            made.append(two(
+                used(upper[listed[source, q]], q), used(lower[listed[source, q + 1]], q + 1),
+                tiles[listed[0, q]], tiles[listed[0, q + 1]], 0,
+            ))
+        for u in range(LONG):
+            t = listed[target, c * LONG + u]
+            part = made[u // 2]
+            acc[t] = acc[t] + (part[:rows] if u % 2 == 0 else part[rows:])
+
+
+def place_products(listed, line, made, acc):
+    @pl.loop(0, made.shape[0] // GROUP)
+    def _(c):
+        for u in range(GROUP):
+            t = listed[line, c * GROUP + u]
+            acc[t] = acc[t] + made[c * GROUP + u]
+
+
+def backward_kernel(list_ref, h_ref, tiles, part_ref, acc, upper, lower, listed, sem):
     moved = pltpu.make_async_copy(list_ref, listed, sem)
     moved.start()
     n_node = part_ref.shape[0]
     row_tiles = acc.shape[0] // n_node
     acc[...] = jnp.zeros_like(acc)
+    by_tile(h_ref, upper, lower)
     moved.wait()
-    add_products(
-        listed, 7, tiles, lambda q: h_ref[:, lanes(listed[2, q], TILE)], acc, ((1,), (0,))
-    )
+    add_products(listed, 2, 7, upper, lower, tiles, acc)
     for j in range(n_node):
         for t in range(row_tiles):
             part_ref[j, :, t * TILE:(t + 1) * TILE] = acc[j * row_tiles + t].astype(BF16)
@@ -335,7 +366,7 @@
 def reduce_kernel(
     listed, part_ref, h_ref, tiles, gst, ost,
     fl_in, fr_in, fy_in, made, gw_out, gb_out, out_ref,
-    far_in, dl_in, dr_in, hl_in, hr_in, hl_out, hr_out, y_out, r_out, l_out, gin, sums, h_tiles,
+    far_in, dl_in, dr_in, hl_in, hr_in, hl_out, hr_out, y_out, r_out, l_out, gin, sums, upper, lower,
     send, recv, s_send, s_recv, g_send, g_recv, o_send, o_recv, own_sem,
 ):
     n, f, at = around()
@@ -398,8 +429,8 @@
     sums[n] = jnp.sum(gin[...].astype(F32), axis=0)
     for d in range(1, n_node):
         link.push(sums.at[n], sums.at[n], s_send.at[d], s_recv.at[d], lax.rem(n + d, n_node), f)
-    by_tile(h_ref, h_tiles)
-    own_products(lambda k: listed[4, k], h_tiles, tiles, n, made, ((1,), (0,)))
+    by_tile(h_ref, upper, lower)
+    own_products(lambda k: listed[4, k], upper, lower, tiles, n * made.shape[0], made)
     for d in range(1, n_node):
         link.arrived(sums.at[lax.rem(n - d + n_node, n_node)], s_send.at[d], s_recv.at[d])
     total = jnp.sum(sums[...], axis=0)
@@ -464,27 +495,30 @@
     def pairs(k):
         return [dma((n_feat,))] * k
 
-    x_all, tiles, made, cin, win, listed = pl.pallas_call(
-        gather_kernel,
+    tiles, listed, h, ost, gst = pl.pallas_call(
+        functools.partial(forward_kernel, 1.0 / float(nodes * n_node) ** 0.5),
         out_shape=(
-            shape((n_node,) + block, BF16),
             shape((n_node * slots, TILE, TILE), BF16),
-            shape((slots, rows, TILE), F32),
+            shape((8, n_node * slots), jnp.int32),
+            shape(block, BF16),
             shape((n_feat, channels, span), BF16),
             shape((n_feat,) + pair, BF16),
-            shape((8, n_node * slots), jnp.int32),
         ),
         in_specs=[in_hbm] * 8,
-        out_specs=(in_vmem,) * 6,
+        out_specs=(in_vmem,) * 5,
         scratch_shapes=[
-            VMEM(block, BF16), VMEM((row_tiles, rows, TILE), BF16),
+            VMEM((n_node,) + block, BF16), VMEM(block, BF16),
+            VMEM((row_tiles, 2 * rows, TILE), BF16), VMEM((row_tiles, 2 * rows, TILE), BF16),
+            VMEM((slots * rows, TILE), F32), VMEM((row_tiles * rows, TILE), F32), VMEM(block, BF16),
+            VMEM((n_feat, rows, span), BF16), VMEM((n_feat, rows, span), BF16),
+            VMEM((n_feat, channels, span), BF16), VMEM((n_feat,) + pair, BF16),
             pltpu.SMEM(tile_count.shape, jnp.int32), pltpu.SMEM(tile_cols.shape, jnp.int32),
             VMEM(tile_rows.shape, jnp.int32), VMEM(tile_cols.shape, jnp.int32),
             VMEM((channels, inputs), BF16), VMEM((1, channels), F32), VMEM(pair, BF16),
-            dma((9,)), dma((n_node,)), dma((14,)), dma((14,)),
-        ] + pairs(4),
-        compiler_params=params(20, collective_id=0, has_side_effects=True),
-        name="gather",
+            dma((8,)), dma((n_node,)), dma(()), dma((14,)), dma((14,)),
+        ] + pairs(8),
+        compiler_params=params(24, collective_id=0, has_side_effects=True),
+        name="forward",
     )(
         keep(features), keep(tile_values.reshape(n_node * slots, TILE, TILE)), keep(cotangent),
         keep(tile_count), keep(tile_rows), keep(tile_cols),
@@ -492,40 +526,14 @@
     )
 
     acc = VMEM((row_tiles, rows, TILE), F32)
+    by_tiles = VMEM((row_tiles, 2 * rows, TILE), BF16)
     scalars = [pltpu.SMEM((8, n_node * slots), jnp.int32), dma(())]
-    z = pl.pallas_call(
-        forward_kernel,
-        out_shape=shape(block, BF16),
-        in_specs=[in_vmem] * 4,
-        out_specs=in_vmem,
-        scratch_shapes=[acc] + scalars,
-        compiler_params=params(16),
-        name="forward",
-    )(listed, x_all, tiles, made)
-
-    h, ost, gst = pl.pallas_call(
-        functools.partial(dense_kernel, 1.0 / float(nodes * n_node) ** 0.5),
-        out_shape=(
-            shape(block, BF16),
-            shape((n_feat, channels, span), BF16),
-            shape((n_feat,) + pair, BF16),
-        ),
-        in_specs=[in_vmem] * 3,
-        out_specs=(in_vmem,) * 3,
-        scratch_shapes=[
-            VMEM((n_feat, rows, span), BF16),
-            VMEM((n_feat, rows, span), BF16),
-        ] + pairs(4) + [dma(())],
-        compiler_params=params(16, collective_id=1, has_side_effects=True),
-        name="dense",
-    )(z, cin, win)
-
     part = pl.pallas_call(
         backward_kernel,
         out_shape=shape((n_node,) + block, BF16),
         in_specs=[in_vmem] * 3,
         out_specs=in_vmem,
-        scratch_shapes=[VMEM((n_node * row_tiles, rows, TILE), F32)] + scalars,
+        scratch_shapes=[VMEM((n_node * row_tiles, rows, TILE), F32)] + [by_tiles] * 2 + scalars,
         compiler_params=params(16),
         name="backward",
     )(listed, h, tiles)
@@ -546,10 +554,10 @@
         out_specs=(in_vmem,) * 7,
         scratch_shapes=[whole] * 3 + [half] * 4 + [whole] + [half] * 2 + [
             VMEM((n_feat,) + pair, BF16), VMEM((n_node,) + pair, F32),
-            VMEM((row_tiles, rows, TILE), BF16),
+            by_tiles, by_tiles,
             dma((14,)), dma((14,)), dma((n_node,)), dma((n_node,)),
         ] + pairs(4) + [dma(())],
-        compiler_params=params(16, collective_id=2, has_side_effects=True),
+        compiler_params=params(16, collective_id=1, has_side_effects=True),
         name="reduce",
     )(listed, part, h, tiles, gst, ost)
 

time: 60.9 us -> 55.3 us (0.908)
  Pallas kernels: 60.1 us -> 54.4 us
    pallas_call x3 -> x1, Pallas kernels: 37.4 us -> 33.1 us  [local(): pl.pallas_call(functools.partial(forward_kernel, 1.0 / float(nodes * n_no...]
    pallas_call x1, Pallas kernels: 19.4 us -> 18 us  [local(): pl.pallas_call(reduce_kernel, out_shape=(shape(block, BF16), shape(block,...]
where the time goes in v6:
time: 55.3 us; the launch traced here: 55.1 us
  Pallas kernels  54.4 us (98%)
  between operations  0.66 us (1%)
    pallas_call x1, Pallas kernels, local(): pl.pallas_call(functools.partial(forward_kernel, 1.0 / float(nodes * n_no...  33.1 us
    pallas_call x1, Pallas kernels, local(): pl.pallas_call(reduce_kernel, out_shape=(shape(block, BF16), shape(block,...  18 us
    pallas_call x1, Pallas kernels, local(): pl.pallas_call(backward_kernel, out_shape=shape((n_node,) + block, BF16),...  1.82 us
    pallas_call x1, Pallas kernels, local(): pl.pallas_call(final_kernel, out_shape=(shape(block, BF16), shape((channe...  1.55 us

profile of v6, /device:TPU:0, one launch (start us, length us, event | category | flops | bytes accessed | tf_op | source)
XLA Modules:
  0.0 55.1 jit_solution(158237601545266266)
XLA Ops:
  0.6 33.1 %forward.1 = (bf16[384,128,128]{2,1,0:T(8,128)(2,1)S(1)}, s32[8,384]{1,0:T(8,128)S(1)}, bf16[8,8192]{1,0:T(8,128)(2,1)S(1)}, bf16[16,16,512]{2,1,0:T(8,128)(2,1)S(1)}, bf16[16,2,16,128]{3,2,1,0:T(8,128)(2,1)S(1)}) custom-call(bf16[8,8192]{1,0:T(8,128)(2,1)} %x_ref.1, bf16[384,128,128]{2,1,0:T(8,128)(2,1)} %bitcast.5, bf16[16,8192]{1,0:T(8,128)(2,1)} %cot_ref.1, ...), custom_call_target="tpu_custom_call" | custom-call | tf_op jit(solution)/shard_map/forward/pallas_call | solution.py:498
  33.8 1.8 %backward.1.part_ref = bf16[8,8,8192]{2,1,0:T(8,128)(2,1)S(1)} custom-call(s32[8,384]{1,0:T(8,128)S(1)} %get-tuple-element.20.list_ref.listed, bf16[8,8192]{1,0:T(8,128)(2,1)S(1)} %get-tuple-element.21.h_ref, bf16[384,128,128]{2,1,0:T(8,128)(2,1)S(1)} %get-tuple-element.22.tiles), custom_call_target="tpu_custom_call" | custom-call | tf_op jit(solution)/shard_map/backward/pallas_call | solution.py:531
  35.6 18.0 %reduce.1 = (bf16[8,8192]{1,0:T(8,128)(2,1)S(1)}, bf16[8,8192]{1,0:T(8,128)(2,1)S(1)}, bf16[8,8192]{1,0:T(8,128)(2,1)S(1)}, f32[48,8,128]{2,1,0:T(8,128)S(1)}, f...) custom-call(s32[8,384]{1,0:T(8,128)S(1)} %get-tuple-element.20.list_ref.listed, ...), custom_call_target="tpu_custom_call" | custom-call | tf_op jit(solution)/shard_map/reduce/pallas_call | solution.py:542
  53.6 1.5 %final.1 = (bf16[8,8192]{1,0:T(8,128)(2,1)}, f32[16,128]{1,0:T(8,128)}, f32[1,16]{1,0:T(1,128)}, bf16[16,8192]{1,0:T(8,128)(2,1)}) custom-call(s32[8,384]{1,0:T(8,128)S(1)} %get-tuple-element.20.list_ref.listed, bf16[8,8192]{1,0:T(8,128)(2,1)S(1)} %get-tuple-element.21.h_ref, bf16[8,8192]{1,0:T(8,128)(2,1)S(1)} %get-tuple-element.25.fl, ...), custom_call_target="tpu_custom_call" | custom-call | tf_op jit(solution)/shard_map/final/pallas_call | solution.py:564

commit v7 on v6

v7 whole, which is shorter than its diff:
```python
import functools

import jax
import jax.numpy as jnp
from jax import lax
from jax.experimental import pallas as pl
from jax.experimental.pallas import tpu as pltpu
from jax.sharding import PartitionSpec as P

MESH = pl.DeviceIdType.MESH
VMEM = pltpu.VMEM
BF16 = jnp.bfloat16
F32 = jnp.float32
TILE = 128
GROUP = 48


def around():
    n, f = lax.axis_index("node"), lax.axis_index("feat")
    nx = lax.axis_size("node") // 2
    x, y = lax.rem(n, nx), n // nx

    def at(dx, dy):
        return (lax.rem(y + dy, 2)) * nx + lax.rem(x + dx + nx, nx)

    return n, f, at


def remote(src, dst, send, recv, node, feat):
    return pltpu.make_async_remote_copy(
        src_ref=src, dst_ref=dst, send_sem=send, recv_sem=recv, device_id=(node, feat), device_id_type=MESH
    )


def greet(places):
    barrier = pltpu.get_barrier_semaphore()
    for place in places:
        pl.semaphore_signal(barrier, inc=1, device_id=place, device_id_type=MESH)


def met(places):
    pl.semaphore_wait(pltpu.get_barrier_semaphore(), len(places))


def lanes(t, width):
    return pl.ds(pl.multiple_of(t * width, width), width)


class Sender:
    def __init__(self):
        self.sent = []

    def push(self, src, dst, send, recv, node, feat):
        self.sent.append(remote(src, dst, send, recv, node, feat))
        self.sent[-1].start()

    def arrived(self, dst, send, recv):
        remote(dst, dst, send, recv, lax.axis_index("node"), lax.axis_index("feat")).wait_recv()

    def finish(self):
        for copy in self.sent:
            copy.wait_send()


def ring(f, n_feat):
    if n_feat != 16:
        return [(d, lax.rem(f + d, n_feat), lax.rem(f - d + n_feat, n_feat)) for d in range(1, n_feat)]
    z, y, core = f // 4, lax.rem(f // 2, 2), lax.rem(f, 2)

    def by(dz, dy, dc):
        return lax.rem(z + dz + 4, 4) * 4 + lax.rem(y + dy, 2) * 2 + lax.rem(core + dc, 2)

    offsets = [(dz, dy, dc) for dz in (2, 1, 3, 0) for dy in (1, 0) for dc in (1, 0)][:-1]
    offsets.sort(key=lambda d: -(min(d[0], 4 - d[0]) + 2 * d[1] + d[2]))
    return [(dz * 4 + dy * 2 + dc, by(dz, dy, dc), by(-dz, dy, dc)) for dz, dy, dc in offsets]


def split(x):
    high = x.astype(BF16).astype(F32)
    mid = (x - high).astype(BF16).astype(F32)
    lane = lax.broadcasted_iota(jnp.int32, x.shape, 1)
    rest = jnp.where(lane == 1, mid, jnp.where(lane == 2, x - high - mid, 0.0))
    return jnp.where(lane == 0, high, rest).astype(BF16)


def by_tile(x_ref, upper, lower):
    rows = x_ref.shape[0]
    none = jnp.zeros((rows, TILE), F32)
    for t in range(upper.shape[0]):
        x = x_ref[:, t * TILE:(t + 1) * TILE].astype(F32)
        upper[t] = jnp.concatenate([x, none], axis=0).astype(BF16)
        lower[t] = jnp.concatenate([none, x], axis=0).astype(BF16)


def two(x, y, a, b, across):
    pair = jnp.concatenate([x, y], axis=1)
    both = jnp.concatenate([a, b], axis=across)
    return lax.dot_general(pair, both, (((1,), (across,)), ((), ())), preferred_element_type=F32)


def products(upper, lower, index, j, tiles, out_ref, across):
    rows = upper.shape[1] // 2
    slots = out_ref.shape[0] // rows

    @pl.loop(0, slots // GROUP)
    def _(c):
        for u in range(0, GROUP, 2):
            k = c * GROUP + u
            out_ref[pl.ds(pl.multiple_of(k * rows, rows), 2 * rows)] = two(
                upper[index[0, j, k]], lower[index[0, j, k + 1]],
                tiles[j * slots + k], tiles[j * slots + k + 1], across,
            )


def sum_tiles(count, index, j, made, out_ref, add):
    slots = index.shape[2]
    rows = made.shape[0] // slots
    row_tiles = out_ref.shape[0] // rows
    t = lax.broadcasted_iota(jnp.int32, (row_tiles, slots), 0)
    k = lax.broadcasted_iota(jnp.int32, (row_tiles, slots), 1)
    hit = jnp.where((t == index[0, pl.ds(j, 1)]) & (k < count[0, j]), 1.0, 0.0).astype(BF16)
    for c in range(rows):
        part = made[pl.ds(c, slots, stride=rows), :]
        high = part.astype(BF16)
        low = (part - high.astype(F32)).astype(BF16)
        where = pl.ds(c, row_tiles, stride=rows)
        total = jnp.dot(hit, high, preferred_element_type=F32) + jnp.dot(hit, low, preferred_element_type=F32)
        out_ref[where, :] = out_ref[where, :] + total if add else total


def layer_kernel(
    norm, x_ref, tiles_ref, cot_ref, count_ref, rows_ref, cols_ref, wt_ref, bias_ref,
    own_sum, fl_in, fr_in, fy_in, gw_out, gb_out, out_ref,
    tiles, x_all, x_own, upper, lower, made, tile_sum, z_ref, zin, hst, cin, win, h_ref, ost, gst,
    part_ref, far_in, dl_in, dr_in, hl_in, hr_in, hl_out, hr_out, y_out, r_out, l_out, gin, gall,
    count, rows_at, cols_at, rows_in, cols_in, wt_in, bias_in, wst,
    local_sem, tile_sem, own_sem, send, recv, back_send, back_recv, s_send, s_recv,
    c_send, c_recv, w_send, w_recv, z_send, z_recv, h_send, h_recv, g_send, g_recv, o_send, o_recv,
):
    n, f, at = around()
    n_feat, channels, span = cin.shape
    rows = x_ref.shape[0]
    inputs = wt_ref.shape[1]
    hidden = n_feat * channels
    n_node = count_ref.shape[1]
    slots = tiles.shape[0] // n_node
    half = x_ref.shape[1] // 2
    right, left, other, far = at(1, 0), at(-1, 0), at(0, 1), at(2, 0)
    order = [n, left, right, other, far, at(-1, 1), at(1, 1), at(2, 1)]
    link = Sender()
    here = [
        pltpu.make_async_copy(src, dst, local_sem.at[i])
        for i, (src, dst) in enumerate([
            (wt_ref, wt_in), (bias_ref, bias_in), (count_ref, count), (rows_ref, rows_in), (cols_ref, cols_in),
            (rows_ref, rows_at), (cols_ref, cols_at), (x_ref, x_own), (cot_ref.at[:, lanes(f, span)], cin.at[f]),
        ])
    ]
    moved = [
        pltpu.make_async_copy(
            tiles_ref.at[pl.ds(j * slots, slots)], tiles.at[pl.ds(j * slots, slots)], tile_sem.at[s]
        )
        for s, j in enumerate(order)
    ]
    partners = ring(f, n_feat)
    places = [(lax.rem(n + d, n_node), f) for d in range(1, n_node)] + [(n, p) for _, p, _ in partners]
    greet(places)
    for copy in here:
        copy.start()
    met(places)

    low, high = pl.ds(0, half), pl.ds(half, half)

    def push(m, part, k, to, src=None):
        block = x_all.at[m, :, part]
        link.push(block if src is None else src.at[:, part], block, send.at[k], recv.at[k], to, f)

    def arrived(m, part, k):
        link.arrived(x_all.at[m, :, part], send.at[k], recv.at[k])

    def work(s):
        moved[s].wait()
        by_tile(x_own if s == 0 else x_all.at[order[s]], upper, lower)
        products(upper, lower, cols_at, order[s], tiles, made, 1)
        sum_tiles(count, rows_in, order[s], made, tile_sum, True)

    push(n, low, 0, right, x_ref)
    push(n, high, 1, left, x_ref)
    push(n, low, 2, other, x_ref)
    push(n, high, 3, right, x_ref)
    push(n, low, 4, left, x_ref)
    push(n, high, 5, other, x_ref)
    for d, p, _ in partners:
        link.push(cot_ref.at[:, lanes(p, span)], cin.at[f], c_send.at[d], c_recv.at[d], n, p)
    for copy in here[:2]:
        copy.wait()
    wst[0] = wt_in[...]
    wst[1] = split(jnp.broadcast_to(bias_in[...], (inputs, channels)).T)
    win[f] = wst[...]
    for d, p, _ in partners:
        link.push(wst, win.at[f], w_send.at[d], w_recv.at[d], n, p)
    for copy in moved:
        copy.start()
    for copy in here[2:]:
        copy.wait()
    for t in range(upper.shape[0]):
        tile_sum[t * rows:(t + 1) * rows] = x_own[:, t * TILE:(t + 1) * TILE].astype(F32)
    work(0)
    arrived(left, low, 0)
    push(left, low, 6, right)
    arrived(right, high, 1)
    push(right, high, 7, left)
    arrived(other, low, 2)
    push(other, low, 8, right)
    push(other, low, 9, left)
    arrived(other, high, 5)
    push(other, high, 10, right)
    push(other, high, 11, left)
    arrived(left, high, 3)
    work(1)
    arrived(far, low, 6)
    push(far, low, 12, other)
    arrived(far, high, 7)
    push(far, high, 13, other)
    arrived(right, low, 4)
    work(2)
    work(3)
    work(4)
    arrived(at(-1, 1), low, 8)
    arrived(at(-1, 1), high, 10)
    work(5)
    arrived(at(1, 1), low, 9)
    arrived(at(1, 1), high, 11)
    work(6)
    arrived(at(2, 1), low, 12)
    arrived(at(2, 1), high, 13)
    work(7)
    for t in range(upper.shape[0]):
        z_ref[:, t * TILE:(t + 1) * TILE] = tile_sum[t * rows:(t + 1) * rows].astype(BF16)
    for d, p, _ in partners:
        link.push(z_ref.at[:, lanes(p, span)], zin.at[f], z_send.at[d], z_recv.at[d], n, p)
    zin[f] = z_ref[:, lanes(f, span)]
    for d, _, p in partners:
        link.arrived(cin.at[p], c_send.at[d], c_recv.at[d])
        link.arrived(win.at[p], w_send.at[d], w_recv.at[d])
    wt = win[:, 0].reshape(hidden, inputs)
    bias = jnp.sum(win[:, 1].reshape(hidden, inputs).astype(F32), axis=1, keepdims=True)
    cot = cin[...].reshape(hidden, span)
    w = wt.astype(F32).T.astype(BF16)
    for d, _, p in partners:
        link.arrived(zin.at[p], z_send.at[d], z_recv.at[d])
    z = zin[...].astype(F32).reshape(n_feat * rows, span).astype(BF16)
    parts = []
    for t in range(span // TILE):
        part = slice(t * TILE, (t + 1) * TILE)
        pre = jnp.dot(wt, z[:, part], preferred_element_type=F32) + bias
        s = jax.nn.sigmoid(pre)
        g = (cot[:, part].astype(F32) * s * (1.0 + pre * (1.0 - s))).astype(BF16)
        h = jnp.dot(w, g, preferred_element_type=F32)
        hst[:, :, part] = h.reshape(n_feat, rows, TILE).astype(BF16)
        ost[:, :, part] = (pre * s).astype(BF16).reshape(n_feat, channels, TILE)
        parts.append(g)
    for d, p, _ in partners:
        link.push(hst.at[p], h_ref.at[:, lanes(f, span)], h_send.at[d], h_recv.at[d], n, p)
    own_h = pltpu.make_async_copy(hst.at[f], h_ref.at[:, lanes(f, span)], own_sem.at[0])
    own_h.start()
    g = jnp.concatenate(parts, axis=1)
    both = jnp.concatenate([z, jnp.ones_like(z)], axis=0)
    sums = lax.dot_general(g, both, (((1,), (1,)), ((), ())), preferred_element_type=F32) * norm
    gst[:, 0] = sums[:, :inputs].astype(BF16).reshape(n_feat, channels, inputs)
    gst[:, 1] = split(sums[:, inputs:]).reshape(n_feat, channels, inputs)
    for d, p, _ in partners:
        link.push(gst.at[p], gin.at[f], g_send.at[d], g_recv.at[d], n, p)
    gin[f] = gst[f]
    for d, p, _ in partners:
        link.push(ost.at[p], out_ref.at[:, lanes(f, span)], o_send.at[d], o_recv.at[d], n, p)
    own_out = pltpu.make_async_copy(ost.at[f], out_ref.at[:, lanes(f, span)], own_sem.at[1])
    own_out.start()
    for d, _, p in partners:
        link.arrived(h_ref.at[:, lanes(p, span)], h_send.at[d], h_recv.at[d])
    own_h.wait()

    def go(src, dst, k, to):
        link.push(src, dst, back_send.at[k], back_recv.at[k], to, f)

    def came(dst, k):
        link.arrived(dst, back_send.at[k], back_recv.at[k])

    def add(*terms):
        total = terms[0].astype(F32)
        for term in terms[1:]:
            total = total + term.astype(F32)
        return total.astype(BF16)

    def spread(j):
        products(upper, lower, rows_at, j, tiles, made, 0)
        sum_tiles(count, cols_in, j, made, tile_sum, False)
        for t in range(upper.shape[0]):
            part_ref[j, :, t * TILE:(t + 1) * TILE] = tile_sum[t * rows:(t + 1) * rows].astype(BF16)

    halves = (low, high)
    by_tile(h_ref, upper, lower)
    spread(at(2, 1))
    for i, part in enumerate(halves):
        go(part_ref.at[at(2, 1), :, part], far_in.at[:, part], i, other)
    spread(at(1, 1))
    for i, part in enumerate(halves):
        go(part_ref.at[at(1, 1), :, part], dl_in.at[:, part], 2 + i, right)
    spread(at(-1, 1))
    for i, part in enumerate(halves):
        go(part_ref.at[at(-1, 1), :, part], dr_in.at[:, part], 4 + i, left)
    spread(far)
    came(far_in.at[:, low], 0)
    hl_out[...] = add(part_ref[far, :, low], far_in[:, low])
    go(hl_out, hl_in, 6, right)
    came(far_in.at[:, high], 1)
    hr_out[...] = add(part_ref[far, :, high], far_in[:, high])
    go(hr_out, hr_in, 7, left)
    spread(other)
    came(dl_in.at[:, low], 2)
    came(dr_in.at[:, low], 4)
    y_out[:, low] = add(part_ref[other, :, low], dl_in[:, low], dr_in[:, low])
    go(y_out.at[:, low], fy_in.at[:, low], 10, other)
    spread(right)
    go(part_ref.at[right, :, high], fl_in.at[:, high], 8, right)
    came(dl_in.at[:, high], 3)
    came(dr_in.at[:, high], 5)
    y_out[:, high] = add(part_ref[other, :, high], dl_in[:, high], dr_in[:, high])
    go(y_out.at[:, high], fy_in.at[:, high], 11, other)
    spread(left)
    go(part_ref.at[left, :, low], fr_in.at[:, low], 9, left)
    for d, _, p in partners:
        link.arrived(gin.at[p], g_send.at[d], g_recv.at[d])
    gall[n] = jnp.sum(gin[...].astype(F32), axis=0)
    for d in range(1, n_node):
        link.push(gall.at[n], gall.at[n], s_send.at[d], s_recv.at[d], lax.rem(n + d, n_node), f)
    came(hl_in, 6)
    r_out[...] = add(part_ref[right, :, low], hl_in[...])
    go(r_out, fl_in.at[:, low], 12, right)
    came(hr_in, 7)
    l_out[...] = add(part_ref[left, :, high], hr_in[...])
    go(l_out, fr_in.at[:, high], 13, left)
    for t in range(upper.shape[0]):
        own_sum[t * rows:(t + 1) * rows] = h_ref[:, t * TILE:(t + 1) * TILE].astype(F32)
    products(upper, lower, rows_at, n, tiles, made, 0)
    sum_tiles(count, cols_in, n, made, own_sum, True)
    for d in range(1, n_node):
        link.arrived(gall.at[lax.rem(n - d + n_node, n_node)], s_send.at[d], s_recv.at[d])
    total = jnp.sum(gall[...], axis=0)
    gw_out[...] = total[0]
    gb_out[...] = jnp.sum(total[1].T, axis=0, keepdims=True)
    for d, _, p in partners:
        link.arrived(out_ref.at[:, lanes(p, span)], o_send.at[d], o_recv.at[d])
    own_out.wait()
    came(fl_in.at[:, high], 8)
    came(fr_in.at[:, low], 9)
    for i, part in enumerate(halves):
        came(fy_in.at[:, part], 10 + i)
    came(fl_in.at[:, low], 12)
    came(fr_in.at[:, high], 13)
    link.finish()


def final_kernel(
    own_sum, fl, fr, fy, gw_ref, gb_ref, made_out,
    gf_ref, gw_out, gb_out, out_ref, out_sem,
):
    moved = pltpu.make_async_copy(made_out, out_ref, out_sem)
    moved.start()
    rows = gf_ref.shape[0]
    for t in range(gf_ref.shape[1] // TILE):
        span = slice(t * TILE, (t + 1) * TILE)
        gf_ref[:, span] = (
            own_sum[t * rows:(t + 1) * rows] + fl[:, span].astype(F32)
            + fr[:, span].astype(F32) + fy[:, span].astype(F32)
        ).astype(BF16)
    gw_out[...] = gw_ref[...]
    gb_out[...] = gb_ref[...]
    moved.wait()


def local(features, weight, bias, tile_values, tile_rows, tile_cols, tile_count, cotangent):
    n_node, n_feat = lax.axis_size("node"), lax.axis_size("feat")
    rows, nodes = features.shape
    inputs, channels = weight.shape
    row_tiles = nodes // TILE
    span = row_tiles // n_feat * TILE
    slots = tile_rows.shape[2]
    dma = pltpu.SemaphoreType.DMA
    in_vmem = pl.BlockSpec(memory_space=VMEM)
    in_smem = pl.BlockSpec(memory_space=pltpu.SMEM)
    in_hbm = pl.BlockSpec(memory_space=pltpu.HBM)
    shape = jax.ShapeDtypeStruct
    block = (rows, nodes)
    pair = (2, channels, inputs)

    def params(mib, **more):
        return pltpu.CompilerParams(vmem_limit_bytes=mib << 20, **more)

    def keep(x):
        return pltpu.with_memory_space_constraint(x, pltpu.HBM)

    def pairs(k):
        return [dma((n_feat,))] * k

    by_tiles = VMEM((row_tiles, 2 * rows, TILE), BF16)
    whole, half = VMEM(block, BF16), VMEM((rows, nodes // 2), BF16)
    sums = (row_tiles * rows, TILE)
    own, fl, fr, fy, gwt, gb, out = pl.pallas_call(
        functools.partial(layer_kernel, 1.0 / float(nodes * n_node) ** 0.5),
        out_shape=(
            shape(sums, F32),
            shape(block, BF16),
            shape(block, BF16),
            shape(block, BF16),
            shape((channels, inputs), F32),
            shape((1, channels), F32),
            shape((channels, nodes), BF16),
        ),
        in_specs=[in_hbm] * 8,
        out_specs=(in_vmem,) * 7,
        scratch_shapes=[
            VMEM((n_node * slots, TILE, TILE), BF16), VMEM((n_node,) + block, BF16), whole,
            by_tiles, by_tiles, VMEM((slots * rows, TILE), F32), VMEM(sums, F32), whole,
            VMEM((n_feat, rows, span), BF16), VMEM((n_feat, rows, span), BF16),
            VMEM((n_feat, channels, span), BF16), VMEM((n_feat,) + pair, BF16), whole,
            VMEM((n_feat, channels, span), BF16), VMEM((n_feat,) + pair, BF16),
            VMEM((n_node,) + block, BF16), whole, whole, whole, half, half, half, half, whole, half, half,
            VMEM((n_feat,) + pair, BF16), VMEM((n_node,) + pair, F32),
            pltpu.SMEM(tile_count.shape, jnp.int32), pltpu.SMEM(tile_rows.shape, jnp.int32),
            pltpu.SMEM(tile_cols.shape, jnp.int32),
            VMEM(tile_rows.shape, jnp.int32), VMEM(tile_cols.shape, jnp.int32),
            VMEM((channels, inputs), BF16), VMEM((1, channels), F32), VMEM(pair, BF16),
            dma((9,)), dma((n_node,)), dma((2,)), dma((14,)), dma((14,)), dma((14,)), dma((14,)),
            dma((n_node,)), dma((n_node,)),
        ] + pairs(12),
        compiler_params=params(40, collective_id=0, has_side_effects=True),
        name="layer",
    )(
        keep(features), keep(tile_values.reshape(n_node * slots, TILE, TILE)), keep(cotangent),
        keep(tile_count), keep(tile_rows), keep(tile_cols),
        keep(weight.T), keep(bias.reshape(1, channels)),
    )

    gf, gwt, gb, out = pl.pallas_call(
        final_kernel,
        out_shape=(
            shape(block, BF16),
            shape((channels, inputs), F32),
            shape((1, channels), F32),
            shape((channels, nodes), BF16),
        ),
        in_specs=[in_vmem] * 7,
        out_specs=(in_vmem,) * 3 + (in_hbm,),
        scratch_shapes=[dma(())],
        compiler_params=params(16),
        name="final",
    )(own, fl, fr, fy, gwt, gb, out)
    return out, gf, gwt.T, gb.reshape(channels)


def solution(mesh):
    return jax.shard_map(
        local,
        mesh=mesh,
        in_specs=(
            P("feat", "node"),
            P(None, "feat"),
            P("feat"),
            P("node", None, None, None, None),
            P("node", None, None),
            P("node", None, None),
            P("node", None),
            P("feat", "node"),
        ),
        out_specs=(P("feat", "node"), P("feat", "node"), P(None, "feat"), P("feat")),
        check_vma=False,
    )
```

time: 55.3 us -> 49.4 us (0.89)
  Pallas kernels: 54.4 us -> 48.6 us
    pallas_call x3 -> x1, Pallas kernels: 52.9 us -> 47.3 us  [local(): pl.pallas_call(functools.partial(layer_kernel, 1.0 / float(nodes * n_node...]
where the time goes in v7:
time: 49.4 us; the launch traced here: 49.3 us
  Pallas kernels  48.6 us (98%)
  between operations  0.64 us (1%)
    pallas_call x1, Pallas kernels, local(): pl.pallas_call(functools.partial(layer_kernel, 1.0 / float(nodes * n_node...  47.3 us
    pallas_call x1, Pallas kernels, local(): pl.pallas_call(final_kernel, out_shape=(shape(block, BF16), shape((channe...  1.37 us

profile of v7, /device:TPU:0, one launch (start us, length us, event | category | flops | bytes accessed | tf_op | source)
XLA Modules:
  0.0 49.3 jit_solution(846306514887668651)
XLA Ops:
  0.6 47.3 %layer.1 = (f32[512,128]{1,0:T(8,128)S(1)}, bf16[8,8192]{1,0:T(8,128)(2,1)S(1)}, bf16[8,8192]{1,0:T(8,128)(2,1)S(1)}, bf16[8,8192]{1,0:T(8,128)(2,1)S(1)}, f32[1...) custom-call(bf16[8,8192]{1,0:T(8,128)(2,1)} %x_ref.1, bf16[384,128,128]{2,1,0:T(8,128)(2,1)} %bitcast.5, ...), custom_call_target="tpu_custom_call" | custom-call | tf_op jit(solution)/shard_map/layer/pallas_call | solution.py:408
  47.9 1.4 %final.1 = (bf16[8,8192]{1,0:T(8,128)(2,1)}, f32[16,128]{1,0:T(8,128)}, f32[1,16]{1,0:T(1,128)}, bf16[16,8192]{1,0:T(8,128)(2,1)}) custom-call(f32[512,128]{1,0:T(8,128)S(1)} %get-tuple-element.15.own_sum, bf16[8,8192]{1,0:T(8,128)(2,1)S(1)} %get-tuple-element.16.fl, bf16[8,8192]{1,0:T(8,128)(2,1)S(1)} %get-tuple-element.17.fr, ...), custom_call_target="tpu_custom_call" | custom-call | tf_op jit(solution)/shard_map/final/pallas_call | solution.py:444

commit v8 on v7

--- a/solution.py
+++ b/solution.py
@@ -124,7 +124,8 @@
         high = part.astype(BF16)
         low = (part - high.astype(F32)).astype(BF16)
         where = pl.ds(c, row_tiles, stride=rows)
-        total = jnp.dot(hit, high, preferred_element_type=F32) + jnp.dot(hit, low, preferred_element_type=F32)
+        total = jnp.dot(hit, jnp.concatenate([high, low], axis=1), preferred_element_type=F32)
+        total = total[:, :TILE] + total[:, TILE:]
         out_ref[where, :] = out_ref[where, :] + total if add else total
 
 

time: 49.4 us -> 49.4 us (level)
  no operation moved by 1% of the time
where the time goes in v8:
time: 49.4 us; the launch traced here: 49.3 us
  Pallas kernels  48.6 us (98%)
  between operations  0.64 us (1%)
    pallas_call x1, Pallas kernels, local(): pl.pallas_call(functools.partial(layer_kernel, 1.0 / float(nodes * n_node...  47.2 us
    pallas_call x1, Pallas kernels, local(): pl.pallas_call(final_kernel, out_shape=(shape(block, BF16), shape((channe...  1.37 us

profile of v8, /device:TPU:0, one launch (start us, length us, event | category | flops | bytes accessed | tf_op | source)
XLA Modules:
  0.0 49.3 jit_solution(9717436557647104121)
XLA Ops:
  0.6 47.2 %layer.1 = (f32[512,128]{1,0:T(8,128)S(1)}, bf16[8,8192]{1,0:T(8,128)(2,1)S(1)}, bf16[8,8192]{1,0:T(8,128)(2,1)S(1)}, bf16[8,8192]{1,0:T(8,128)(2,1)S(1)}, f32[1...) custom-call(bf16[8,8192]{1,0:T(8,128)(2,1)} %x_ref.1, bf16[384,128,128]{2,1,0:T(8,128)(2,1)} %bitcast.5, ...), custom_call_target="tpu_custom_call" | custom-call | tf_op jit(solution)/shard_map/layer/pallas_call | solution.py:409
  47.9 1.4 %final.1 = (bf16[8,8192]{1,0:T(8,128)(2,1)}, f32[16,128]{1,0:T(8,128)}, f32[1,16]{1,0:T(1,128)}, bf16[16,8192]{1,0:T(8,128)(2,1)}) custom-call(f32[512,128]{1,0:T(8,128)S(1)} %get-tuple-element.15.own_sum, bf16[8,8192]{1,0:T(8,128)(2,1)S(1)} %get-tuple-element.16.fl, bf16[8,8192]{1,0:T(8,128)(2,1)S(1)} %get-tuple-element.17.fr, ...), custom_call_target="tpu_custom_call" | custom-call | tf_op jit(solution)/shard_map/final/pallas_call | solution.py:445
